TPU v7x, 32 devices: a whole 2x2x4 slice. The times are simulated.
32 devices in a mesh: fsdp: 4 (over x, core), ctx: 8 (over z, y).
Axes of the slice: x: 2, y: 2, z: 4, core: 2. Of those that a mesh axis runs over, the one named last changes fastest.
Arguments:
- tokens: bfloat16 [4, 1024, 1600], P('fsdp', 'ctx'), may hold values from -6 to 6
- cotangent: bfloat16 [4, 1024, 1600], P('fsdp', 'ctx'), may hold values from -6 to 6
- segments: int32 [4, 1024], P('fsdp'), may hold values from 0 to 3, never falling along the last dimension, each value on 1 to 512 neighbouring positions
- w_qkv: bfloat16 [1600, 2240], P('fsdp'), may hold values from -0.15625 to 0.15625
- m_qkv: float32 [2, 1600, 2240], P(None, 'ctx', 'fsdp'), may hold values from -12.8 to 40.96, as said below
- w_attn_out: bfloat16 [1600, 1600], P('fsdp'), may hold values from -0.15625 to 0.15625
- m_attn_out: float32 [2, 1600, 1600], P(None, 'ctx', 'fsdp'), may hold values from -12.8 to 40.96, as said below
- w_mamba_in: bfloat16 [1600, 6400], P('fsdp'), may hold values from -0.15625 to 0.15625
- m_mamba_in: float32 [2, 1600, 6400], P(None, 'ctx', 'fsdp'), may hold values from -12.8 to 40.96, as said below
- w_ssm_proj: bfloat16 [3200, 232], P('fsdp'), may hold values from -0.6 to 0.6
- m_ssm_proj: float32 [2, 3200, 232], P(None, 'ctx', 'fsdp'), may hold values from -12.8 to 40.96, as said below
- w_mamba_out: bfloat16 [3200, 1600], P('fsdp'), may hold values from -0.109375 to 0.109375
- m_mamba_out: float32 [2, 3200, 1600], P(None, 'ctx', 'fsdp'), may hold values from -12.8 to 40.96, as said below
- w_gate_up: bfloat16 [1600, 11008], P('fsdp'), may hold values from -0.15625 to 0.15625
- m_gate_up: float32 [2, 1600, 11008], P(None, 'ctx', 'fsdp'), may hold values from -12.8 to 40.96, as said below
- w_ffn_down: bfloat16 [5504, 1600], P('fsdp'), may hold values from -0.078125 to 0.078125
- m_ffn_down: float32 [2, 5504, 1600], P(None, 'ctx', 'fsdp'), may hold values from -12.8 to 40.96, as said below
- ssm_vec: float32 [22, 3200], replicated, may hold values from -10 to 3
- m_ssm_vec: float32 [2, 22, 3200], replicated, may hold values from -12.8 to 40.96, as said below
- embed_small: float32 [132, 1600], replicated, may hold values from -6 to 6
- m_embed_small: float32 [2, 132, 1600], replicated, may hold values from -12.8 to 40.96, as said below
Outputs:
- output: bfloat16 [4, 1024, 1600], P('fsdp', 'ctx')
- tokens_grad: float32 [4, 1024, 1600], P('fsdp', 'ctx')
- grad_qkv: float32 [1600, 2240], P('ctx', 'fsdp')
- moments_qkv: float32 [1600, 2240], P('ctx', 'fsdp')
- update_qkv: float32 [1600, 2240], P('ctx', 'fsdp')
- grad_attn_out: float32 [1600, 1600], P('ctx', 'fsdp')
- moments_attn_out: float32 [1600, 1600], P('ctx', 'fsdp')
- update_attn_out: float32 [1600, 1600], P('ctx', 'fsdp')
- grad_mamba_in: float32 [1600, 6400], P('ctx', 'fsdp')
- moments_mamba_in: float32 [1600, 6400], P('ctx', 'fsdp')
- update_mamba_in: float32 [1600, 6400], P('ctx', 'fsdp')
- grad_ssm_proj: float32 [3200, 232], P('ctx', 'fsdp')
- moments_ssm_proj: float32 [3200, 232], P('ctx', 'fsdp')
- update_ssm_proj: float32 [3200, 232], P('ctx', 'fsdp')
- grad_mamba_out: float32 [3200, 1600], P('ctx', 'fsdp')
- moments_mamba_out: float32 [3200, 1600], P('ctx', 'fsdp')
- update_mamba_out: float32 [3200, 1600], P('ctx', 'fsdp')
- grad_gate_up: float32 [1600, 11008], P('ctx', 'fsdp')
- moments_gate_up: float32 [1600, 11008], P('ctx', 'fsdp')
- update_gate_up: float32 [1600, 11008], P('ctx', 'fsdp')
- grad_ffn_down: float32 [5504, 1600], P('ctx', 'fsdp')
- moments_ffn_down: float32 [5504, 1600], P('ctx', 'fsdp')
- update_ffn_down: float32 [5504, 1600], P('ctx', 'fsdp')
- grad_ssm_vec: float32 [22, 3200], replicated
- moments_ssm_vec: float32 [22, 3200], replicated
- update_ssm_vec: float32 [22, 3200], replicated
- grad_embed_small: float32 [132, 1600], replicated
- moments_embed_small: float32 [132, 1600], replicated
- update_embed_small: float32 [132, 1600], replicated
Inputs may be any that keep to these rules, and one draw needn't show every extreme that they name: `m_qkv`: row 0 holds first moments, row 1 positive second moments. `segments`: along a row the segment numbers never fall, and the longest segment has exactly 512 tokens. `m_attn_out`: row 0 holds first moments, row 1 positive second moments. `m_mamba_in`: row 0 holds first moments, row 1 positive second moments. `m_ssm_proj`: row 0 holds first moments, row 1 positive second moments. `m_mamba_out`: row 0 holds first moments, row 1 positive second moments. `m_gate_up`: row 0 holds first moments, row 1 positive second moments. `m_ffn_down`: row 0 holds first moments, row 1 positive second moments. `m_ssm_vec`: row 0 holds first moments, row 1 positive second moments. `m_embed_small`: row 0 holds first moments, row 1 positive second moments.
All inputs are finite; a program needn't handle non-finite values.
Results may differ from a plain program's by a relative error of at most 0.025.
Values may be sent and summed in bfloat16 or wider, within the bound.
A program may use at most 512 MiB of HBM per device.

v0:
```python
import jax
import jax.numpy as jnp
from jax import lax
from jax.sharding import PartitionSpec as P

NH = 25
KVH = 5
HD = 64
DI = 3200
DS = 16
DTR = 100
FF = 5504
META = 128
CONV = 4
WINDOW = 1024
HOPS = 8


norm_eps = 1e-05
beta_one = 0.9
beta_two = 0.95
learn_rate = 0.01
decay_rate = 0.1
adam_eps = 1e-08
adam_count = 10.0


def shifted(block, axis, distance):
    devices = range(lax.axis_size(axis))
    route = [(i - distance, i) for i in devices if i - distance in devices]
    return lax.ppermute(block, axis, route)


def carried_in(shard, axis, combine, identity):
    length, mine = (lax.axis_size(axis), lax.axis_index(axis))
    everything = jax.tree.map(lambda part: lax.all_gather(part, axis), shard)
    start = jax.tree.map(
        lambda part, zero: jnp.broadcast_to(jnp.asarray(zero, part.dtype), part.shape),
        shard,
        identity,
    )

    def hop(k, before):
        reached = k < mine
        new = combine(before, jax.tree.map(lambda part: part[k], everything))
        return jax.tree.map(lambda a, b: jnp.where(reached, a, b), new, before)

    return lax.fori_loop(0, length, hop, start)


def carried_in_2(shard, axis, combine, identity):
    length, mine = (lax.axis_size(axis), lax.axis_index(axis))
    everything = jax.tree.map(
        lambda part, kind: lax.all_gather(part.astype(kind), axis),
        shard,
        jax.tree.map(lambda a: jnp.bfloat16 if a.dtype == jnp.float32 else a.dtype, shard),
    )
    start = jax.tree.map(
        lambda part, zero: jnp.broadcast_to(jnp.asarray(zero, part.dtype), part.shape),
        shard,
        identity,
    )

    def hop(k, before):
        at = length - 1 - k
        reached = at > mine
        new = combine(
            before, jax.tree.map(lambda part, own: part[at].astype(own.dtype), everything, shard)
        )
        return jax.tree.map(lambda a, b: jnp.where(reached, a, b), new, before)

    return lax.fori_loop(0, length, hop, start)


def rms_norm(values, gain_row):
    return (
        values * lax.rsqrt(jnp.mean(values * values, axis=-1, keepdims=True) + norm_eps) * gain_row
    )


def dense(operand, partner):
    return jnp.dot(operand, partner, preferred_element_type=jnp.float32)


def dense_tn(operand, partner):
    return lax.dot_general(
        operand, partner, (((0,), (0,)), ((), ())), preferred_element_type=jnp.float32
    )


def dense_nt(operand, partner):
    return lax.dot_general(
        operand, partner, (((1,), (1,)), ((), ())), preferred_element_type=jnp.float32
    )


def conv_silu(extended, conv_taps, seg_ext):
    length_out = extended.shape[0] - conv_taps.shape[0] + 1
    own_seg = seg_ext[conv_taps.shape[0] - 1 :]
    summed = jnp.zeros((length_out, extended.shape[1]), jnp.float32)
    for offset in range(conv_taps.shape[0]):
        same_seg = (seg_ext[offset : offset + length_out] == own_seg)[:, None]
        summed = summed + jnp.where(
            same_seg, extended[offset : offset + length_out] * conv_taps[offset], 0.0
        )
    return jax.nn.silu(summed)


def ssm_scan(inner_x, pre_delta, proj_b, proj_c, gate_z, ssm_small, starts, start_state):
    step_size = jax.nn.softplus(pre_delta + ssm_small[0])
    decay_rates = -jnp.exp(ssm_small[2:])

    def advance(running, element):
        step_delta, step_inner, step_b, step_c, step_start = element
        retain = jnp.where(step_start, 0.0, jnp.exp(step_delta[None, :] * decay_rates))
        running = retain * running + (step_delta * step_inner)[None, :] * step_b[:, None]
        return (running, jnp.sum(running * step_c[:, None], axis=0))

    last_state, readout = lax.scan(
        advance, start_state, (step_size, inner_x, proj_b, proj_c, starts)
    )
    chain_decay = jnp.where(
        jnp.any(starts), 0.0, jnp.exp(decay_rates * jnp.sum(step_size, axis=0)[None, :])
    )
    mixture = (readout + ssm_small[1] * inner_x) * jax.nn.silu(gate_z)
    return (mixture, last_state, chain_decay)


def fetch_rows(weight):
    return lax.all_gather(weight, "fsdp", axis=0, tiled=True)


def combine_affine(earlier, later):
    return (earlier[0] * later[0], later[0] * earlier[1] + later[1])


def reduce_grad(operand, partner):
    partial_rows = lax.psum_scatter(
        dense_tn(operand, partner).astype(jnp.bfloat16), "ctx", scatter_dimension=0, tiled=True
    )
    return lax.psum_scatter(partial_rows, "fsdp", scatter_dimension=1, tiled=True).astype(
        jnp.float32
    )


def adam_step(gradient, moments_old, weight_now):
    first_moment = beta_one * moments_old[0] + (1.0 - beta_one) * gradient
    second_moment = beta_two * moments_old[1] + (1.0 - beta_two) * gradient * gradient
    corrected = (
        first_moment
        / (1.0 - beta_one**adam_count)
        / (jnp.sqrt(second_moment / (1.0 - beta_two**adam_count)) + adam_eps)
    )
    return (second_moment, -learn_rate * (corrected + decay_rate * weight_now))


def adam_block(gradient, moments_old, weight_full):
    rows_here = gradient.shape[0]
    cols_here = gradient.shape[1]
    weight_block = lax.dynamic_slice(
        weight_full,
        (lax.axis_index("ctx") * rows_here, lax.axis_index("fsdp") * cols_here),
        (rows_here, cols_here),
    ).astype(jnp.float32)
    return adam_step(gradient, moments_old, weight_block)


def shards(
    tokens,
    cotangent,
    segments,
    w_qkv,
    m_qkv,
    w_attn_out,
    m_attn_out,
    w_mamba_in,
    m_mamba_in,
    w_ssm_proj,
    m_ssm_proj,
    w_mamba_out,
    m_mamba_out,
    w_gate_up,
    m_gate_up,
    w_ffn_down,
    m_ffn_down,
    ssm_vec,
    m_ssm_vec,
    embed_small,
    m_embed_small,
):
    tok_rows = tokens.shape[1]
    ctx_index = lax.axis_index("ctx")
    source = tokens[0].astype(jnp.float32)
    seg_row = segments[0]
    meta_rows = embed_small[:META]
    gain_rows = embed_small[META:]
    heads_dim = NH * HD
    kv_dim = KVH * HD
    groups = NH // KVH
    scale_factor = HD ** (-0.5)
    xproj_dim = DTR + 2 * DS
    normed_f, norm_pull = jax.vjp(rms_norm, source, gain_rows[0])
    normed = normed_f.astype(jnp.bfloat16)
    meta_f, meta_pull = jax.vjp(rms_norm, meta_rows, gain_rows[0])
    meta_low = meta_f.astype(jnp.bfloat16)
    qkv_full = fetch_rows(w_qkv)
    qkv_out = dense(normed, qkv_full).astype(jnp.bfloat16)
    meta_kv = dense(meta_low, qkv_full[:, heads_dim:]).astype(jnp.bfloat16)
    queries = qkv_out[:, :heads_dim]
    keyval = qkv_out[:, heads_dim:]
    neighbours = []
    for distance in range(HOPS, 0, -1):
        neighbours.append(shifted(keyval, "ctx", distance))
    window_kv = jnp.concatenate(neighbours + [keyval], axis=0)
    key_rows = jnp.concatenate([meta_kv, window_kv], axis=0)
    key_span = (HOPS + 1) * tok_rows
    padded_seg = jnp.concatenate([jnp.full((HOPS * tok_rows,), -1, jnp.int32), seg_row])
    key_seg = lax.dynamic_slice_in_dim(padded_seg, ctx_index * tok_rows, key_span, 0)
    query_seg = lax.dynamic_slice_in_dim(seg_row, ctx_index * tok_rows, tok_rows, 0)
    query_pos = jnp.arange(tok_rows, dtype=jnp.int32) + HOPS * tok_rows
    key_pos = jnp.arange(key_span, dtype=jnp.int32)
    allowed = (
        (key_seg[None, :] == query_seg[:, None])
        & (key_pos[None, :] <= query_pos[:, None])
        & (query_pos[:, None] - key_pos[None, :] < WINDOW)
    )
    allowed = jnp.concatenate([jnp.ones((tok_rows, META), jnp.bool_), allowed], axis=1)

    def group_scores(group_index):
        group_q = queries[:, group_index * groups * HD : (group_index + 1) * groups * HD].reshape(
            tok_rows, groups, HD
        )
        group_k = key_rows[:, group_index * HD : (group_index + 1) * HD]
        group_v = key_rows[:, kv_dim + group_index * HD : kv_dim + (group_index + 1) * HD]
        raw_scores = (
            jnp.einsum("qhd,kd->hqk", group_q, group_k, preferred_element_type=jnp.float32)
            * scale_factor
        )
        return (group_q, group_k, group_v, jnp.where(allowed[None], raw_scores, -1e30))

    attended_parts = []
    log_totals = []
    for group_index in range(KVH):
        group_q, group_k, group_v, scores = group_scores(group_index)
        row_peak = jnp.max(scores, axis=-1, keepdims=True)
        exponent = jnp.exp(scores - row_peak)
        row_total = jnp.sum(exponent, axis=-1, keepdims=True)
        attention = (exponent / row_total).astype(jnp.bfloat16)
        log_totals.append(row_peak + jnp.log(row_total))
        attended_parts.append(
            jnp.einsum(
                "hqk,kd->qhd", attention, group_v, preferred_element_type=jnp.float32
            ).reshape(tok_rows, groups * HD)
        )
    attended = jnp.concatenate(attended_parts, axis=1).astype(jnp.bfloat16)
    attn_out_full = fetch_rows(w_attn_out)
    attn_proj = dense(attended, attn_out_full)
    attn_branch, attn_pull = jax.vjp(rms_norm, attn_proj, gain_rows[1])
    mamba_in_full = fetch_rows(w_mamba_in)
    mamba_in = dense(normed, mamba_in_full)
    inner_pre = mamba_in[:, :DI]
    gate_z = mamba_in[:, DI:]
    tail_rows = shifted(inner_pre[tok_rows - (CONV - 1) :], "ctx", 1)
    extended = jnp.concatenate([tail_rows, inner_pre], axis=0)
    conv_seg = jnp.concatenate([jnp.full((CONV - 1,), -1, jnp.int32), seg_row])
    seg_ext = lax.dynamic_slice_in_dim(conv_seg, ctx_index * tok_rows, tok_rows + CONV - 1, 0)
    inner_x, conv_pull = jax.vjp(
        lambda ext_rows, conv_taps: conv_silu(ext_rows, conv_taps, seg_ext),
        extended,
        ssm_vec[:CONV],
    )
    inner_low = inner_x.astype(jnp.bfloat16)
    ssm_proj_full = fetch_rows(w_ssm_proj)
    xproj_out = dense(inner_low, ssm_proj_full[:, :xproj_dim])
    delta_low = xproj_out[:, :DTR].astype(jnp.bfloat16)
    pre_delta = dense_nt(delta_low, ssm_proj_full[:, xproj_dim:])
    starts = seg_ext[CONV - 1 :] != seg_ext[CONV - 2 : -1]
    ssm_small = ssm_vec[CONV:]
    proj_b = xproj_out[:, DTR : DTR + DS]
    proj_c = xproj_out[:, DTR + DS :]
    zero_state = jnp.zeros((DS, DI), jnp.float32)
    ones_state = jnp.ones((DS, DI), jnp.float32)
    local_run = ssm_scan(inner_x, pre_delta, proj_b, proj_c, gate_z, ssm_small, starts, zero_state)
    entry_state = carried_in(
        (local_run[2], local_run[1]), "ctx", combine_affine, (ones_state, zero_state)
    )

    def scan_piece(inner_arg, delta_arg, b_arg, c_arg, z_arg, small_arg, state_arg):
        return ssm_scan(inner_arg, delta_arg, b_arg, c_arg, z_arg, small_arg, starts, state_arg)

    ssm_result, ssm_pull = jax.vjp(
        scan_piece, inner_x, pre_delta, proj_b, proj_c, gate_z, ssm_small, entry_state[1]
    )
    mixture_low = ssm_result[0].astype(jnp.bfloat16)
    mamba_out_full = fetch_rows(w_mamba_out)
    ssm_proj = dense(mixture_low, mamba_out_full)
    ssm_branch, ssm_norm_pull = jax.vjp(rms_norm, ssm_proj, gain_rows[2])
    residual = source + 0.5 * (attn_branch + ssm_branch)
    ffn_in_f, ffn_norm_pull = jax.vjp(rms_norm, residual, gain_rows[3])
    ffn_in = ffn_in_f.astype(jnp.bfloat16)
    gate_up_full = fetch_rows(w_gate_up)
    gate_up = dense(ffn_in, gate_up_full)
    hidden_f, glu_pull = jax.vjp(
        lambda values: jax.nn.silu(values[:, :FF]) * values[:, FF:], gate_up
    )
    hidden = hidden_f.astype(jnp.bfloat16)
    ffn_down_full = fetch_rows(w_ffn_down)
    output = residual + dense(hidden, ffn_down_full)
    out_grad = cotangent[0]
    hidden_grad = dense_nt(out_grad, ffn_down_full)
    gate_up_grad = glu_pull(hidden_grad)[0].astype(jnp.bfloat16)
    ffn_in_grad = dense_nt(gate_up_grad, gate_up_full)
    resid_part, gain_ffn_grad = ffn_norm_pull(ffn_in_grad)
    residual_grad = out_grad.astype(jnp.float32) + resid_part
    branch_grad = 0.5 * residual_grad
    attn_proj_grad, gain_attn_grad = attn_pull(branch_grad)
    attn_proj_low = attn_proj_grad.astype(jnp.bfloat16)
    attended_grad = dense_nt(attn_proj_low, attn_out_full).astype(jnp.bfloat16)
    ssm_proj_grad, gain_ssm_grad = ssm_norm_pull(branch_grad)
    ssm_proj_low = ssm_proj_grad.astype(jnp.bfloat16)
    mixture_grad = dense_nt(ssm_proj_low, mamba_out_full)
    query_grads = []
    key_grads = []
    value_grads = []
    for group_index in range(KVH):
        group_q, group_k, group_v, scores = group_scores(group_index)
        attention_f = jnp.exp(scores - log_totals[group_index])
        attention = attention_f.astype(jnp.bfloat16)
        out_slice = attended_grad[
            :, group_index * groups * HD : (group_index + 1) * groups * HD
        ].reshape(tok_rows, groups, HD)
        prob_grad = jnp.einsum(
            "qhd,kd->hqk", out_slice, group_v, preferred_element_type=jnp.float32
        )
        value_grads.append(
            jnp.einsum("hqk,qhd->kd", attention, out_slice, preferred_element_type=jnp.float32)
        )
        score_grad = (
            attention_f * (prob_grad - jnp.sum(attention_f * prob_grad, axis=-1, keepdims=True))
        ).astype(jnp.bfloat16)
        query_grads.append(
            (
                jnp.einsum("hqk,kd->qhd", score_grad, group_k, preferred_element_type=jnp.float32)
                * scale_factor
            ).reshape(tok_rows, groups * HD)
        )
        key_grads.append(
            jnp.einsum("hqk,qhd->kd", score_grad, group_q, preferred_element_type=jnp.float32)
            * scale_factor
        )
    kv_grad_all = jnp.concatenate(key_grads + value_grads, axis=1)
    own_kv_grad = kv_grad_all[META + HOPS * tok_rows :]
    for distance in range(1, HOPS + 1):
        first_row = META + (HOPS - distance) * tok_rows
        own_kv_grad = own_kv_grad + shifted(
            kv_grad_all[first_row : first_row + tok_rows].astype(jnp.bfloat16), "ctx", -distance
        ).astype(jnp.float32)
    meta_kv_grad = lax.psum(kv_grad_all[:META].astype(jnp.bfloat16), "ctx")
    qkv_grad = jnp.concatenate(
        [
            jnp.concatenate(query_grads, axis=1).astype(jnp.bfloat16),
            own_kv_grad.astype(jnp.bfloat16),
        ],
        axis=1,
    )
    first_pull = ssm_pull((mixture_grad, zero_state, zero_state))
    adjoint = carried_in_2(
        (local_run[2], first_pull[6]), "ctx", combine_affine, (ones_state, zero_state)
    )
    grads_ssm = ssm_pull((mixture_grad, adjoint[1], zero_state))
    inner_grad, pre_delta_grad, b_grad, c_grad, z_grad, small_grad, _ = grads_ssm
    pre_delta_low = pre_delta_grad.astype(jnp.bfloat16)
    delta_low_grad = dense(pre_delta_low, ssm_proj_full[:, xproj_dim:])
    xproj_grad = jnp.concatenate([delta_low_grad, b_grad, c_grad], axis=1).astype(jnp.bfloat16)
    inner_grad = inner_grad + dense_nt(xproj_grad, ssm_proj_full[:, :xproj_dim])
    ext_grad, taps_grad = conv_pull(inner_grad)
    returned = shifted(ext_grad[: CONV - 1].astype(jnp.bfloat16), "ctx", -1).astype(jnp.float32)
    inner_pre_grad = ext_grad[CONV - 1 :] + jnp.concatenate(
        [jnp.zeros((tok_rows - (CONV - 1), DI), jnp.float32), returned], axis=0
    )
    mamba_in_grad = jnp.concatenate([inner_pre_grad, z_grad], axis=1).astype(jnp.bfloat16)
    normed_grad = dense_nt(qkv_grad, qkv_full) + dense_nt(mamba_in_grad, mamba_in_full)
    source_part, gain_in_grad = norm_pull(normed_grad)
    source_grad = residual_grad + source_part
    first_ctx = (ctx_index == 0).astype(jnp.float32)
    meta_low_grad = dense_nt(meta_kv_grad, qkv_full[:, heads_dim:])
    meta_grad, gain_in_meta = meta_pull(meta_low_grad)
    embed_grad = jnp.concatenate(
        [
            meta_grad * first_ctx,
            jnp.stack(
                [
                    gain_in_grad + gain_in_meta * first_ctx,
                    gain_attn_grad,
                    gain_ssm_grad,
                    gain_ffn_grad,
                ]
            ),
        ],
        axis=0,
    )
    ssm_grad = jnp.concatenate([taps_grad, small_grad], axis=0)
    ssm_total, embed_total = lax.psum((ssm_grad, embed_grad), ("fsdp", "ctx"))
    meta_left = (meta_low.astype(jnp.float32) * first_ctx).astype(jnp.bfloat16)
    qkv_operand = jnp.concatenate([normed, meta_left], axis=0)
    qkv_partner = jnp.concatenate(
        [
            qkv_grad,
            jnp.concatenate([jnp.zeros((META, heads_dim), jnp.bfloat16), meta_kv_grad], axis=1),
        ],
        axis=0,
    )
    ssm_operand = jnp.concatenate([inner_low, pre_delta_low], axis=0)
    ssm_partner = jnp.concatenate(
        [
            jnp.concatenate([xproj_grad, jnp.zeros((tok_rows, DTR), jnp.bfloat16)], axis=1),
            jnp.concatenate([jnp.zeros((tok_rows, xproj_dim), jnp.bfloat16), delta_low], axis=1),
        ],
        axis=0,
    )
    qkv_gradient = reduce_grad(qkv_operand, qkv_partner)
    attn_gradient = reduce_grad(attended, attn_proj_low)
    mamba_in_gradient = reduce_grad(normed, mamba_in_grad)
    ssm_proj_gradient = reduce_grad(ssm_operand, ssm_partner)
    mamba_out_gradient = reduce_grad(mixture_low, ssm_proj_low)
    gate_up_gradient = reduce_grad(ffn_in, gate_up_grad)
    ffn_down_gradient = reduce_grad(hidden, out_grad)
    qkv_moments, qkv_update = adam_block(qkv_gradient, m_qkv, qkv_full)
    attn_moments, attn_update = adam_block(attn_gradient, m_attn_out, attn_out_full)
    mamba_in_moments, mamba_in_update = adam_block(mamba_in_gradient, m_mamba_in, mamba_in_full)
    ssm_proj_moments, ssm_proj_update = adam_block(ssm_proj_gradient, m_ssm_proj, ssm_proj_full)
    mamba_out_moments, mamba_out_update = adam_block(
        mamba_out_gradient, m_mamba_out, mamba_out_full
    )
    gate_up_moments, gate_up_update = adam_block(gate_up_gradient, m_gate_up, gate_up_full)
    ffn_down_moments, ffn_down_update = adam_block(ffn_down_gradient, m_ffn_down, ffn_down_full)
    ssm_vec_moments, ssm_vec_update = adam_step(ssm_total, m_ssm_vec, ssm_vec)
    embed_moments, embed_update = adam_step(embed_total, m_embed_small, embed_small)
    return (
        output.astype(jnp.bfloat16)[None],
        source_grad[None],
        qkv_gradient,
        qkv_moments,
        qkv_update,
        attn_gradient,
        attn_moments,
        attn_update,
        mamba_in_gradient,
        mamba_in_moments,
        mamba_in_update,
        ssm_proj_gradient,
        ssm_proj_moments,
        ssm_proj_update,
        mamba_out_gradient,
        mamba_out_moments,
        mamba_out_update,
        gate_up_gradient,
        gate_up_moments,
        gate_up_update,
        ffn_down_gradient,
        ffn_down_moments,
        ffn_down_update,
        ssm_total,
        ssm_vec_moments,
        ssm_vec_update,
        embed_total,
        embed_moments,
        embed_update,
    )


def solution(mesh):
    in_specs = (
        P("fsdp", "ctx", None),
        P("fsdp", "ctx", None),
        P("fsdp", None),
        P("fsdp", None),
        P(None, "ctx", "fsdp"),
        P("fsdp", None),
        P(None, "ctx", "fsdp"),
        P("fsdp", None),
        P(None, "ctx", "fsdp"),
        P("fsdp", None),
        P(None, "ctx", "fsdp"),
        P("fsdp", None),
        P(None, "ctx", "fsdp"),
        P("fsdp", None),
        P(None, "ctx", "fsdp"),
        P("fsdp", None),
        P(None, "ctx", "fsdp"),
        P(),
        P(),
        P(),
        P(),
    )
    out_specs = (
        P("fsdp", "ctx", None),
        P("fsdp", "ctx", None),
        P("ctx", "fsdp"),
        P("ctx", "fsdp"),
        P("ctx", "fsdp"),
        P("ctx", "fsdp"),
        P("ctx", "fsdp"),
        P("ctx", "fsdp"),
        P("ctx", "fsdp"),
        P("ctx", "fsdp"),
        P("ctx", "fsdp"),
        P("ctx", "fsdp"),
        P("ctx", "fsdp"),
        P("ctx", "fsdp"),
        P("ctx", "fsdp"),
        P("ctx", "fsdp"),
        P("ctx", "fsdp"),
        P("ctx", "fsdp"),
        P("ctx", "fsdp"),
        P("ctx", "fsdp"),
        P("ctx", "fsdp"),
        P("ctx", "fsdp"),
        P("ctx", "fsdp"),
        P(),
        P(),
        P(),
        P(),
        P(),
        P(),
    )
    return jax.shard_map(shards, mesh=mesh, in_specs=in_specs, out_specs=out_specs, check_vma=False)
```

profile of v0, /device:TPU:2, one launch (start us, length us, event | category | flops | bytes accessed | tf_op | source)
XLA Modules:
  0.0 7306.7 jit_solution(7652709138754648717)
XLA Ops:
  14.4 124.2 %all-gather.19.cloned.1.call-done = bf16[1600,6400]{1,0:T(8,128)(2,1)} async-done(((bf16[400,6400]{1,0:T(8,128)(2,1)}), bf16[1600,6400]{1,0:T(8,128)(2,1)}) %all-gather.19.cloned.1.call-update) | async-done | bytes 20480016 | tf_op jit(solution)/shard_map/all_gather | solution.py:130
  138.6 8.7 fusion.257
  168.9 470.8 %while.111 = (s32[]{:T(128)}, f32[16,3200]{1,0:T(8,128)S(1)}, pred[128]{0:T(512)(128)(4,1)}, f32[128,3200]{1,0:T(8,128)}, f32[16,3200]{1,0:T(8,128)S(1)}, /*inde...) while((s32[]{:T(128)}, f32[16,3200]{1,0:T(8,128)S(1)}, ...), condition=%wide.region_16.17_spmd.clone, body=%wide.region_15.16_spmd.clone.sunk | while | flops 310403 | bytes 691518 | solution.py:119
  652.4 7.0 collective-permute-start.1
  708.6 5.7 multiply_reduce_fusion.26
  714.9 23.7 copy.300
  741.3 52.2 all-gather.2
  793.5 15.8 while.112
  810.7 1409.0 %while.110 = (s32[]{:T(128)}, f32[16,3200]{1,0:T(8,128)}, f32[128,3200]{1,0:T(8,128)}, f32[128,1,3200]{2,1,0:T(1,128)}, f32[128,16,3200]{2,1,0:T(8,128)}, /*inde...) while((s32[]{:T(128)}, f32[16,3200]{1,0:T(8,128)}, ...), condition=%wide.region_21.22_spmd, body=%wide.region_19.21_spmd.sunk | while | flops 464002 | bytes 1858067 | solution.py:119
  2223.4 8.6 multiply_reduce_fusion.25
  2234.3 16.8 fusion.225
  2251.2 12.4 fusion.183
  2263.6 20.8 multiply_reduce_fusion.16
  2288.9 9.7 multiply_reduce_fusion.11
  2298.6 437.1 %while.113 = (s32[]{:T(128)}, f32[16,3200]{1,0:T(8,128)}, f32[128,16,3200]{2,1,0:T(8,128)}, f32[128,3200]{1,0:T(8,128)}, f32[128,16,1]{1,2,0:T(1,128)}, /*index=5*/s32[]{:T(128)}, s32[]{:T(128)}, s32[]{:T(128)}) while((s32[]{:T(128)}, f32[16,3200]{1,0:T(8,128)}, f32[128,16,3200]{2,1,0:T(8,128)}, f32[128,3200]{1,0:T(8,128)}, ...), condition=%wide.region_33.34_spmd.clone, body=%wide.region_32.33_spmd.clone.sunk | while | flops 204804 | bytes 653119 | solution.py:119
  2736.6 34.5 all-gather.3
  2771.2 14.0 while.114
  2789.1 1991.0 %while.115 = (s32[]{:T(128)}, f32[16,3200]{1,0:T(8,128)}, f32[16,3200]{1,0:T(8,128)}, f32[128,3200]{1,0:T(8,128)}, f32[128,3200]{1,0:T(8,128)}, /*index=5*/bf16[...) while((s32[]{:T(128)}, f32[16,3200]{1,0:T(8,128)}, ...), condition=%wide.region_41.42_spmd.clone, body=%wide.region_36.41_spmd.clone.sunk | while | flops 873572 | bytes 2522454 | solution.py:119
  4817.7 4.9 convolution_convert_fusion.5
  4824.6 7.5 multiply_reduce_fusion.14
  4849.6 5.6 fusion.135
  4859.3 6.2 convolution_add_fusion.3
  4865.5 14.3 all-reduce.29.cloned.1.call-done
  4885.8 5.1 convolution_convert_fusion.4
  4892.2 6.9 convolution_convert_fusion.3
  4900.1 12.6 convolution_convert_fusion.2
  4913.9 10.9 convolution_convert_fusion.1
  4925.9 18.1 convolution_convert_fusion
  4954.5 120.7 %reduce-scatter.54.cloned.1.call-done = bf16[200,1600]{1,0:T(8,128)(2,1)} async-done(((bf16[1600,1600]{1,0:T(8,128)(2,1)}), bf16[200,1600]{1,0:T(8,128)(2,1)}) %reduce-scatter.54.cloned.1.call-update) | async-done | bytes 640016
  5077.6 134.9 %reduce-scatter.34.cloned.1.call-done = bf16[200,2240]{1,0:T(8,128)(2,1)} async-done(((bf16[1600,2240]{1,0:T(8,128)(2,1)}), bf16[200,2240]{1,0:T(8,128)(2,1)}) %reduce-scatter.34.cloned.1.call-update) | async-done | bytes 896016 | tf_op jit(solution)/shard_map/reduce_scatter | solution.py:138
  5215.0 181.3 %reduce-scatter.38.cloned.1.call-done = bf16[400,1600]{1,0:T(8,128)(2,1)} async-done(((bf16[3200,1600]{1,0:T(8,128)(2,1)}), bf16[400,1600]{1,0:T(8,128)(2,1)}) %reduce-scatter.38.cloned.1.call-update) | async-done | bytes 1280016 | tf_op jit(solution)/shard_map/reduce_scatter | solution.py:138
  5399.8 354.0 %reduce-scatter.40.cloned.1.call-done = bf16[688,1600]{1,0:T(8,128)(2,1)} async-done(((bf16[5504,1600]{1,0:T(8,128)(2,1)}), bf16[688,1600]{1,0:T(8,128)(2,1)}) %reduce-scatter.40.cloned.1.call-update) | async-done | bytes 2201616 | tf_op jit(solution)/shard_map/reduce_scatter | solution.py:138
  5758.4 387.9 %reduce-scatter.56.cloned.1.call-done = bf16[200,6400]{1,0:T(8,128)(2,1)} async-done(((bf16[1600,6400]{1,0:T(8,128)(2,1)}), bf16[200,6400]{1,0:T(8,128)(2,1)}) %reduce-scatter.56.cloned.1.call-update) | async-done | bytes 2560016
  6146.3 4.6 copy.415
  6151.0 730.6 %reduce-scatter.58.cloned.1.call-done = bf16[200,11008]{1,0:T(8,128)(2,1)} async-done(((bf16[1600,11008]{1,0:T(8,128)(2,1)}), bf16[200,11008]{1,0:T(8,128)(2,1)}) %reduce-scatter.58.cloned.1.call-update) | async-done | bytes 4403216
  6881.6 7.6 copy.421
  6913.9 14.6 fusion.54
  6928.5 107.3 %all-reduce.33.cloned.1.call-done = (f32[22,3200]{1,0:T(8,128)}, f32[132,1600]{0,1:T(8,128)}) async-done(((f32[22,3200]{1,0:T(8,128)}, f32[132,1600]{0,1:T(8,128)}), (f32[22,3200]{1,0:T(8,128)}, f32[132,1600]{0,1:T(8,128)})) %all-reduce.33.cloned.1.call-update) | async-done | bytes 1126416 | tf_op jit(solution)/shard_map/psum | solution.py:403
  7038.6 5.4 fusion.88
  7049.4 18.5 all-reduce.31.cloned.1.call-done
  7072.6 21.9 reduce-scatter.44.cloned.1.call-done
  7098.0 25.3 reduce-scatter.42.cloned.1.call-done
  7127.4 27.7 reduce-scatter.48.cloned.1.call-done
  7159.5 32.0 reduce-scatter.52.cloned.1.call-done
  7202.7 30.1 reduce-scatter.46.cloned.1.call-done
  7234.2 5.1 fusion.113
  7239.3 50.2 reduce-scatter.50.cloned.1.call-done
  7291.3 7.7 fusion.60
  (4072 shorter events, 4597.5 us)
Async XLA Ops:
  7.2 131.4 %all-gather.19.cloned.1.call-start = ((), (), s32[]{:S(2)}) async-start(), calls=%async_computation.15 | async-start | bytes 25600000 | tf_op jit(solution)/shard_map/all_gather | solution.py:130
  7.9 152.3 %all-gather.21.cloned.1.call-start = ((), (), s32[]{:S(2)}) async-start(), calls=%async_computation.16 | async-start | bytes 2048000 | tf_op jit(solution)/shard_map/all_gather | solution.py:130
  8.7 637.2 %all-gather.15.cloned.1.call-start = ((), (), s32[]{:S(2)}) async-start(), calls=%async_computation.13 | async-start | bytes 9216000 | tf_op jit(solution)/shard_map/all_gather | solution.py:130
  9.4 699.1 %all-gather.17.cloned.1.call-start = ((), (), s32[]{:S(2)}) async-start(), calls=%async_computation.14 | async-start | bytes 6656000 | tf_op jit(solution)/shard_map/all_gather | solution.py:130
  10.0 704.9 %all-gather.31.cloned.1.call-start = ((), (), s32[]{:S(2)}) async-start(), calls=%async_computation.26 | async-start | bytes 22528000 | tf_op jit(solution)/shard_map/all_gather | solution.py:130
  10.6 782.9 %all-gather.27.cloned.1.call-start = ((), (), s32[]{:S(2)}) async-start(), calls=%async_computation.24 | async-start | bytes 1843200 | tf_op jit(solution)/shard_map/all_gather | solution.py:36
  11.9 653.5 %copy-start.102 = (f32[1600]{0:T(1024)}, f32[1600]{0:T(1024)S(1)}, u32[]{:S(2)}) copy-start(f32[1600]{0:T(1024)S(1)} %get-tuple-element.1332) | copy-start | bytes 19204
  13.4 139.9 %copy-start.132 = (pred[128]{0:T(512)(128)(4,1)}, pred[128]{0:T(512)(128)(4,1)S(1)}, u32[]{:S(2)}) copy-start(pred[128]{0:T(512)(128)(4,1)S(1)} %get-tuple-element.1572) | copy-start | bytes 388
  13.4 139.9 %copy-start.133 = (pred[128]{0:T(512)(128)(4,1)}, pred[128]{0:T(512)(128)(4,1)S(1)}, u32[]{:S(2)}) copy-start(pred[128]{0:T(512)(128)(4,1)S(1)} %get-tuple-element.1573) | copy-start | bytes 388
  13.4 139.9 %copy-start.134 = (pred[128]{0:T(512)(128)(4,1)}, pred[128]{0:T(512)(128)(4,1)S(1)}, u32[]{:S(2)}) copy-start(pred[128]{0:T(512)(128)(4,1)S(1)} %get-tuple-element.1574) | copy-start | bytes 388
  147.4 5.9 collective-permute-start.8
  167.3 571.2 %copy-start.98 = (f32[3200]{0:T(1024)}, f32[3200]{0:T(1024)S(1)}, u32[]{:S(2)}) copy-start(f32[3200]{0:T(1024)S(1)} %get-tuple-element.1547) | copy-start | bytes 38404
  168.8 624.7 %all-gather.29.cloned.1.call-start = ((), (), s32[]{:S(2)}) async-start(), calls=%async_computation.25 | async-start | bytes 1843200 | tf_op jit(solution)/shard_map/all_gather | solution.py:36
  640.4 1583.0 %all-gather.23.cloned.1.call-start = ((), (), s32[]{:S(2)}) async-start(), calls=%async_computation.17 | async-start | bytes 13312000 | tf_op jit(solution)/shard_map/all_gather | solution.py:130
  641.1 1593.2 %all-gather.25.cloned.1.call-start = ((), (), s32[]{:S(2)}) async-start(), calls=%async_computation.18 | async-start | bytes 44032000 | tf_op jit(solution)/shard_map/all_gather | solution.py:130
  641.9 4238.0 %all-reduce.29.cloned.1.call-start = ((), (), s32[]{:S(2)}) async-start(), calls=%async_computation.19 | async-start | bytes 327680 | tf_op jit(solution)/shard_map/psum | solution.py:358
  651.1 21.1 collective-permute-start
  652.4 22.0 collective-permute-start.1
  659.4 17.2 collective-permute-start.2
  661.4 19.0 collective-permute-start.3
  663.4 18.0 collective-permute-start.4
  672.1 10.2 collective-permute-start.5
  674.4 8.0 collective-permute-start.6
  676.6 7.2 collective-permute-start.7
  4809.7 144.1 %reduce-scatter.36.cloned.1.call-start = ((), (), s32[]{:S(2)}) async-start(), calls=%async_computation.21 | async-start | bytes 1843200 | tf_op jit(solution)/shard_map/reduce_scatter | solution.py:138
  4816.7 258.5 %reduce-scatter.54.cloned.1.call-start = ((), (), s32[]{:S(2)}) async-start(), calls=%async_computation.34 | async-start | bytes 5990400
  4822.7 389.9 %reduce-scatter.34.cloned.1.call-start = ((), (), s32[]{:S(2)}) async-start(), calls=%async_computation.20 | async-start | bytes 8294400 | tf_op jit(solution)/shard_map/reduce_scatter | solution.py:138
  4832.8 9.8 collective-permute-start.17
  4834.4 10.2 collective-permute-start.16
  4835.2 11.6 collective-permute-start.15
  4836.5 11.5 collective-permute-start.14
  4837.8 17.4 collective-permute-start.13
  4842.9 14.2 collective-permute-start.12
  4844.6 12.6 collective-permute-start.11
  4846.8 10.4 collective-permute-start.10
  4848.1 9.1 collective-permute-start.9
  4891.0 505.3 %reduce-scatter.38.cloned.1.call-start = ((), (), s32[]{:S(2)}) async-start(), calls=%async_computation.22 | async-start | bytes 11980800 | tf_op jit(solution)/shard_map/reduce_scatter | solution.py:138
  4899.1 854.7 %reduce-scatter.40.cloned.1.call-start = ((), (), s32[]{:S(2)}) async-start(), calls=%async_computation.23 | async-start | bytes 20606976 | tf_op jit(solution)/shard_map/reduce_scatter | solution.py:138
  4912.7 1233.6 %reduce-scatter.56.cloned.1.call-start = ((), (), s32[]{:S(2)}) async-start(), calls=%async_computation.35 | async-start | bytes 23040000
  4924.8 1956.8 %reduce-scatter.58.cloned.1.call-start = ((), (), s32[]{:S(2)}) async-start(), calls=%async_computation.36 | async-start | bytes 39628800
  4944.1 2091.8 %all-reduce.33.cloned.1.call-start = ((), (), s32[]{:S(2)}) async-start(), calls=%async_computation.37 | async-start | bytes 3891200 | tf_op jit(solution)/shard_map/psum | solution.py:403
  4953.7 2114.2 %all-reduce.31.cloned.1.call-start = ((), (), s32[]{:S(2)}) async-start(), calls=%async_computation.33 | async-start | bytes 409600
  4954.5 2140.0 %reduce-scatter.44.cloned.1.call-start = ((), (), s32[]{:S(2)}) async-start(), calls=%async_computation.28 | async-start | bytes 1024000
  5077.6 2045.8 %reduce-scatter.42.cloned.1.call-start = ((), (), s32[]{:S(2)}) async-start(), calls=%async_computation.27 | async-start | bytes 1433600
  5214.9 1940.2 %reduce-scatter.48.cloned.1.call-start = ((), (), s32[]{:S(2)}) async-start(), calls=%async_computation.30 | async-start | bytes 2048000
  5399.7 1791.8 %reduce-scatter.52.cloned.1.call-start = ((), (), s32[]{:S(2)}) async-start(), calls=%async_computation.32 | async-start | bytes 3072000
  5758.3 1474.4 %reduce-scatter.46.cloned.1.call-start = ((), (), s32[]{:S(2)}) async-start(), calls=%async_computation.29 | async-start | bytes 4096000
  6150.9 1138.6 %reduce-scatter.50.cloned.1.call-start = ((), (), s32[]{:S(2)}) async-start(), calls=%async_computation.31 | async-start | bytes 7045120
  (147 other events, 1325.0 us)
Sparse Core Ops, SparseCore 0:
  9.6 128.9 all-gather.18
  140.2 20.0 all-gather.20
  161.8 52.5 all-gather.14
  215.8 40.9 all-gather.16
  258.1 115.3 all-gather.30
  376.1 45.7 all-gather.26
  640.5 61.8 all-gather.28
  703.9 71.5 all-gather.22
  777.1 213.2 all-gather.24
  4809.8 69.9 all-reduce.28
  4884.3 65.1 reduce-scatter.35
  4952.8 122.4 reduce-scatter.53
  5079.4 133.1 reduce-scatter.33
  5215.9 180.3 reduce-scatter.37
  5399.7 354.1 reduce-scatter.39
  5757.7 388.5 reduce-scatter.55
  6148.6 732.9 reduce-scatter.57
  6888.9 146.8 all-reduce.32
  7038.3 29.5 all-reduce.30
  7070.9 23.5 reduce-scatter.43
  7097.8 25.5 reduce-scatter.41
  7126.5 28.5 reduce-scatter.47
  7157.8 33.6 reduce-scatter.51
  7194.0 38.7 reduce-scatter.45
  7235.5 53.9 reduce-scatter.49
where the time goes:
time: 7400 us; the launch traced here: 7310 us
  local copies, waits for them, and re-layouts  2430 us (33%)
  waiting for transfers between devices  2370 us (32%)
  other arithmetic  2140 us (29%)
  matrix products  220 us (3%)
  blocking collectives  86.8 us (1%)
    unnamed x35, waiting for transfers between devices  1450 us
    dynamic_update_slice x768, local copies, waits for them, and re-layouts, ssm_scan(): lax.scan(advance, start_state, (step_size, inner_x, proj_b, proj_c, starts))  1090 us
    dynamic_slice x768, local copies, waits for them, and re-layouts, ssm_scan(): lax.scan(advance, start_state, (step_size, inner_x, proj_b, proj_c, starts))  820 us
    reduce_scatter x4, waiting for transfers between devices, reduce_grad(): lax.psum_scatter(dense_tn(operand, partner).astype(jnp.bfloat16), 'ctx',...  670 us
    dynamic_update_slice x256, other arithmetic, ssm_scan(): lax.scan(advance, start_state, (step_size, inner_x, proj_b, proj_c, starts))  532 us
    reduce_sum x128, other arithmetic, advance(): (step_delta * step_inner)[None, :] * step_b[:, None]  444 us
    dynamic_slice x256, other arithmetic, ssm_scan(): lax.scan(advance, start_state, (step_size, inner_x, proj_b, proj_c, starts))  256 us
    mul x128, other arithmetic, advance(): retain * running + (step_delta * step_inner)[None, :] * step_b[:, None]  232 us

commit v1 on v0

v1 whole, which is shorter than its diff:
```python
import functools

import jax
import jax.numpy as jnp
from jax import lax
from jax.experimental import pallas as pl
from jax.experimental.pallas import tpu as pltpu
from jax.sharding import PartitionSpec as P

NH = 25
KVH = 5
HD = 64
DI = 3200
DS = 16
DTR = 100
FF = 5504
META = 128
CONV = 4
WINDOW = 1024

norm_eps = 1e-05
beta_one = 0.9
beta_two = 0.95
learn_rate = 0.01
decay_rate = 0.1
adam_eps = 1e-08
adam_count = 10.0

LOG2E = 1.4426950408889634
LN2 = 0.6931471805599453
FAR = 1e30
bf16 = jnp.bfloat16
f32 = jnp.float32
ANY = pl.BlockSpec(memory_space=pl.ANY)
MIB = 1024 * 1024


def ceil_to(value, unit):
    return (value + unit - 1) // unit * unit


def exchange_body(axis, n, reach, modes, *refs):
    count = len(modes)
    ins, outs = refs[:count], refs[count : 2 * count]
    send_sem, recv_sem, own_sem = refs[2 * count :]
    me = lax.axis_index(axis)
    barrier = pltpu.get_barrier_semaphore()
    for d in range(1, n):
        pl.semaphore_signal(
            barrier,
            inc=1,
            device_id={axis: lax.rem(me + d, n)},
            device_id_type=pl.DeviceIdType.MESH,
        )
    pl.semaphore_wait(barrier, n - 1)

    def copy(k, d, source, target, peer):
        return pltpu.make_async_remote_copy(
            src_ref=source,
            dst_ref=target,
            send_sem=send_sem.at[k, d],
            recv_sem=recv_sem.at[k, d],
            device_id={axis: peer},
            device_id_type=pl.DeviceIdType.MESH,
        )

    waits = []
    for k, mode in enumerate(modes):
        src, dst = ins[k], outs[k]
        if mode in ("all", "each"):
            own = pltpu.make_async_copy(
                src.at[me] if mode == "each" else src, dst.at[me], own_sem.at[k]
            )
            own.start()
            waits.append((own.wait, None))
            for d in range(1, n):
                peer = lax.rem(me + d, n)
                c = copy(k, d, src.at[peer] if mode == "each" else src, dst.at[me], peer)
                c.start()
                waits.append((c.wait_send, None))
                waits.append((c.wait_recv, None))
        else:
            for d in range(1, reach + 1):
                up = mode == "next"
                peer = me + d if up else me - d
                sends = peer < n if up else peer >= 0
                takes = me - d >= 0 if up else me + d < n
                source = src.at[d - 1] if mode == "back" else src
                c = copy(k, d, source, dst.at[d - 1], lax.rem(peer + n, n))
                pl.when(sends)(c.start)
                waits.append((c.wait_send, sends))
                waits.append((c.wait_recv, takes))
    for wait, condition in waits:
        if condition is None:
            wait()
        else:
            pl.when(condition)(wait)


def exchange(axis, cid, items, reach=0):
    n = lax.axis_size(axis)
    shapes, modes = [], []
    for value, mode in items:
        lead = {"all": (n,), "next": (reach,), "prev": (reach,)}.get(mode, ())
        shapes.append(jax.ShapeDtypeStruct(lead + value.shape, value.dtype))
        modes.append(mode)
    count = len(items)
    return pl.pallas_call(
        functools.partial(exchange_body, axis, n, reach, tuple(modes)),
        out_shape=tuple(shapes),
        in_specs=[ANY] * count,
        out_specs=(ANY,) * count,
        scratch_shapes=[
            pltpu.SemaphoreType.DMA((count, n)),
            pltpu.SemaphoreType.DMA((count, n)),
            pltpu.SemaphoreType.DMA((count,)),
        ],
        compiler_params=pltpu.CompilerParams(collective_id=cid, has_side_effects=True),
    )(*[value for value, _ in items])


def scan_tail_body(rows, length, step_ref, u_ref, b_ref, rate_ref, last_ref):
    rate = rate_ref[...]

    def advance(i, states):
        new = []
        for r in range(rows):
            keep = jnp.exp2(step_ref[r, pl.ds(i, 1), :] * rate)
            new.append(keep * states[r] + u_ref[r, pl.ds(i, 1), :] * b_ref[r, i])
        return tuple(new)

    start = tuple(jnp.zeros((DS, 128), f32) for _ in range(rows))
    end = lax.fori_loop(0, length, advance, start, unroll=4)
    for r in range(rows):
        last_ref[r] = end[r]


def scan_full_body(
    rows, length, step_ref, u_ref, b_ref, c_ref, rate_ref, entry_ref, read_ref, hist_ref
):
    rate = rate_ref[...]

    def advance(i, states):
        new = []
        for r in range(rows):
            hist_ref[r, i] = states[r]
            keep = jnp.exp2(step_ref[r, pl.ds(i, 1), :] * rate)
            h = keep * states[r] + u_ref[r, pl.ds(i, 1), :] * b_ref[r, i]
            read_ref[r, pl.ds(i, 1), :] = jnp.sum(h * c_ref[r, i], axis=0, keepdims=True)
            new.append(h)
        return tuple(new)

    lax.fori_loop(0, length, advance, tuple(entry_ref[r] for r in range(rows)), unroll=4)


def adjoint_head_body(rows, length, step_ref, dy_ref, c_ref, rate_ref, first_ref):
    rate = rate_ref[...]

    def advance(k, carried):
        i = length - 1 - k
        new = []
        for r in range(rows):
            keep = jnp.exp2(step_ref[r, pl.ds(i, 1), :] * rate)
            new.append(keep * (carried[r] + dy_ref[r, pl.ds(i, 1), :] * c_ref[r, i]))
        return tuple(new)

    start = tuple(jnp.zeros((DS, 128), f32) for _ in range(rows))
    end = lax.fori_loop(0, length, advance, start, unroll=4)
    for r in range(rows):
        first_ref[r] = end[r]


def adjoint_full_body(
    rows,
    length,
    step_ref,
    u_ref,
    dy_ref,
    b_ref,
    c_ref,
    rate_ref,
    hist_ref,
    later_ref,
    du_ref,
    dexp_ref,
    db_ref,
    dc_ref,
    drate_ref,
):
    rate = rate_ref[...]

    @pl.when(pl.program_id(1) == 0)
    def _():
        db_ref[...] = jnp.zeros_like(db_ref)
        dc_ref[...] = jnp.zeros_like(dc_ref)

    def advance(k, carried):
        i = length - 1 - k
        new = []
        drate = carried[rows]
        for r in range(rows):
            step = step_ref[r, pl.ds(i, 1), :]
            u = u_ref[r, pl.ds(i, 1), :]
            dy = dy_ref[r, pl.ds(i, 1), :]
            keep = jnp.exp2(step * rate)
            b = b_ref[r, i]
            kept = keep * hist_ref[r, i]
            g = carried[r] + dy * c_ref[r, i]
            w = g * kept
            dc_ref[r, i] += (kept + u * b) * dy
            db_ref[r, i] += g * u
            du_ref[r, pl.ds(i, 1), :] = jnp.sum(g * b, axis=0, keepdims=True)
            dexp_ref[r, pl.ds(i, 1), :] = jnp.sum(w * rate, axis=0, keepdims=True)
            drate = drate + w * step
            new.append(keep * g)
        return tuple(new) + (drate,)

    start = tuple(later_ref[r] for r in range(rows)) + (jnp.zeros((DS, 128), f32),)
    end = lax.fori_loop(0, length, advance, start, unroll=2)
    drate_ref[0] = end[rows]


def scan_call(body, args, kinds, outs, rows_all, length, width):
    rows = 4 if rows_all % 4 == 0 else rows_all
    single = pl.Buffered(buffer_count=1)

    def spec(kind, one=False):
        extra = {"pipeline_mode": single} if one else {}
        if kind == "seq":
            return pl.BlockSpec((rows, length, 128), lambda r, g: (r, 0, g), **extra)
        if kind == "spread":
            return pl.BlockSpec((rows, length, DS, 128), lambda r, g: (r, 0, 0, 0), **extra)
        if kind == "hist":
            return pl.BlockSpec((rows, length, DS, 128), lambda r, g: (r, 0, 0, g), **extra)
        if kind == "state":
            return pl.BlockSpec((rows, DS, 128), lambda r, g: (r, 0, g), **extra)
        if kind == "rate":
            return pl.BlockSpec((DS, 128), lambda r, g: (0, g), **extra)
        return pl.BlockSpec((1, DS, 128), lambda r, g: (r, 0, g), **extra)

    shape_of = {
        "seq": (rows_all, length, width),
        "spread": (rows_all, length, DS, 128),
        "hist": (rows_all, length, DS, width),
        "state": (rows_all, DS, width),
        "drate": (rows_all // rows, DS, width),
    }
    return pl.pallas_call(
        functools.partial(body, rows, length),
        grid=(rows_all // rows, width // 128),
        in_specs=[spec(k, k == "spread") for k in kinds],
        out_specs=tuple(spec(k, k == "spread") for k in outs),
        out_shape=tuple(jax.ShapeDtypeStruct(shape_of[k], f32) for k in outs),
        compiler_params=pltpu.CompilerParams(vmem_limit_bytes=56 * MIB),
    )(*args)


def rms_norm(values, gain_row):
    return (
        values * lax.rsqrt(jnp.mean(values * values, axis=-1, keepdims=True) + norm_eps) * gain_row
    )


def dense(operand, partner):
    return jnp.dot(operand, partner, preferred_element_type=f32)


def dense_tn(operand, partner):
    return lax.dot_general(
        operand, partner, (((0,), (0,)), ((), ())), preferred_element_type=f32
    )


def dense_nt(operand, partner):
    return lax.dot_general(
        operand, partner, (((1,), (1,)), ((), ())), preferred_element_type=f32
    )


def conv_silu(extended, conv_taps, same_seg):
    length_out = extended.shape[1] - CONV + 1
    summed = jnp.zeros((extended.shape[0], length_out, extended.shape[2]), f32)
    for offset in range(CONV):
        summed = summed + jnp.where(
            same_seg[offset][:, :, None],
            extended[:, offset : offset + length_out] * conv_taps[offset],
            0.0,
        )
    return jax.nn.silu(summed)


def adam_step(gradient, moments_old, weight_now):
    first_moment = beta_one * moments_old[0] + (1.0 - beta_one) * gradient
    second_moment = beta_two * moments_old[1] + (1.0 - beta_two) * gradient * gradient
    corrected = (
        first_moment
        / (1.0 - beta_one**adam_count)
        / (jnp.sqrt(second_moment / (1.0 - beta_two**adam_count)) + adam_eps)
    )
    return (second_moment, -learn_rate * (corrected + decay_rate * weight_now))


def pad_last(values, width):
    return jnp.pad(values, [(0, 0)] * (values.ndim - 1) + [(0, width - values.shape[-1])])


def column_parts(weight, parts, shards_of, width):
    own = weight.shape[1] // parts // shards_of
    return jnp.stack(
        [
            jnp.concatenate(
                [
                    pad_last(weight[:, (p * shards_of + j) * own : (p * shards_of + j + 1) * own], width)
                    for p in range(parts)
                ],
                axis=1,
            )
            for j in range(shards_of)
        ]
    )


def shards(
    tokens,
    cotangent,
    segments,
    w_qkv,
    m_qkv,
    w_attn_out,
    m_attn_out,
    w_mamba_in,
    m_mamba_in,
    w_ssm_proj,
    m_ssm_proj,
    w_mamba_out,
    m_mamba_out,
    w_gate_up,
    m_gate_up,
    w_ffn_down,
    m_ffn_down,
    ssm_vec,
    m_ssm_vec,
    embed_small,
    m_embed_small,
):
    fs, cs = lax.axis_size("fsdp"), lax.axis_size("ctx")
    fi, ci = lax.axis_index("fsdp"), lax.axis_index("ctx")
    tok = tokens.shape[1]
    dim = tokens.shape[2]
    row_len = segments.shape[1]
    halves = cs // fs
    reach = min(row_len // 2, WINDOW) // tok
    metas = META // cs
    chan = DI // fs
    chan_p = ceil_to(chan, 128)
    ffw = FF // fs
    ffw_p = ceil_to(ffw, 128)
    heads_dim = NH * HD
    kv_dim = KVH * HD
    groups = NH // KVH
    scale_factor = HD ** (-0.5)
    xdim = DTR + 2 * DS
    both = ("fsdp", "ctx")

    cross = [
        (f * cs + c, (c // halves) * cs + halves * f + c % halves)
        for f in range(fs)
        for c in range(cs)
    ]

    def crossed(value):
        return lax.ppermute(value, both, cross)

    def weight_block(weight):
        rows, cols = weight.shape[0] // halves, weight.shape[1] // fs
        piece = lax.dynamic_slice(
            weight, ((ci % halves) * rows, (ci // halves) * cols), (rows, cols)
        )
        return crossed(piece)

    gu_send = column_parts(w_gate_up, 2, fs, ffw_p)
    mi_send = column_parts(w_mamba_in, 2, fs, chan_p)
    qkv_send = column_parts(w_qkv, 1, fs, w_qkv.shape[1] // fs)
    gain_rows = embed_small[META:]
    meta_rows = lax.dynamic_slice_in_dim(embed_small, ci * metas, metas, 0)
    source = tokens[0].astype(f32)
    normed_f, norm_pull = jax.vjp(rms_norm, source, gain_rows[0])
    normed = normed_f.astype(bf16)
    meta_f, meta_pull = jax.vjp(rms_norm, meta_rows, gain_rows[0])
    meta_low = meta_f.astype(bf16)

    normed_all, cot_all, seg_all, mi_w, qkv_w = exchange(
        "fsdp",
        0,
        [
            (normed, "all"),
            (cotangent[0], "all"),
            (segments, "all"),
            (mi_send, "each"),
            (qkv_send, "each"),
        ],
    )
    gu_w = lax.all_to_all(gu_send, "fsdp", 0, 0).reshape(dim, 2 * ffw_p)
    mi_w = mi_w.reshape(dim, 2 * chan_p)
    qkv_w = qkv_w.reshape(dim, -1)
    seg_all = seg_all.reshape(fs, row_len)
    seg_row = segments[0]
    normed_all = normed_all.reshape(fs * tok, dim)
    cot_all = cot_all.reshape(fs * tok, dim)
    xp_w = jnp.pad(w_ssm_proj[:, :xdim], ((0, chan_p - chan), (0, 0)))
    dt_w = jnp.pad(w_ssm_proj[:, xdim:], ((0, chan_p - chan), (0, 0)))
    mo_w = jnp.pad(w_mamba_out, ((0, chan_p - chan), (0, 0)))
    vec = pad_last(lax.dynamic_slice_in_dim(ssm_vec, fi * chan, chan, 1), chan_p)

    qkv_tp = dense(jnp.concatenate([normed_all, meta_low], axis=0), qkv_w).astype(bf16)
    qkv_parts = jnp.concatenate(
        [
            qkv_tp[: fs * tok].reshape(fs, tok, -1),
            jnp.broadcast_to(qkv_tp[fs * tok :][None], (fs, metas, qkv_tp.shape[1])),
        ],
        axis=1,
    )
    (qkv_got,) = exchange("fsdp", 1, [(qkv_parts, "each")])
    qkv_own = jnp.concatenate([qkv_got[j] for j in range(fs)], axis=1)
    queries = qkv_own[:tok, :heads_dim]
    keyval = qkv_own[:tok, heads_dim:]
    kv_before, meta_kv = exchange(
        "ctx", 2, [(keyval, "next"), (qkv_own[tok:, heads_dim:], "all")], reach
    )
    kv_before = jnp.where(
        (ci - 1 - jnp.arange(reach) >= 0)[:, None, None], kv_before, jnp.zeros_like(kv_before)
    )
    key_rows = jnp.concatenate(
        [meta_kv.reshape(META, 2 * kv_dim)]
        + [kv_before[d - 1] for d in range(reach, 0, -1)]
        + [keyval],
        axis=0,
    )

    mamba_in = dense(normed_all, mi_w).reshape(fs, tok, 2 * chan_p)
    inner_pre = mamba_in[:, :, :chan_p]
    gate_z = mamba_in[:, :, chan_p:]
    up_ring = [(c, c + 1) for c in range(cs - 1)]
    down_ring = [(c + 1, c) for c in range(cs - 1)]
    tail_rows = lax.ppermute(inner_pre[:, tok - (CONV - 1) :], "ctx", up_ring)
    extended = jnp.concatenate([tail_rows, inner_pre], axis=1)
    seg_ext = lax.dynamic_slice_in_dim(
        jnp.concatenate([jnp.full((fs, CONV - 1), -1, jnp.int32), seg_all], axis=1),
        ci * tok,
        tok + CONV - 1,
        1,
    )
    own_seg = seg_ext[:, CONV - 1 :]
    same_seg = [seg_ext[:, o : o + tok] == own_seg for o in range(CONV)]
    starts = own_seg != seg_ext[:, CONV - 2 : -1]
    inner_x, conv_pull = jax.vjp(
        lambda ext_rows, taps: conv_silu(ext_rows, taps, same_seg), extended, vec[:CONV]
    )
    inner_low = inner_x.astype(bf16).reshape(fs * tok, chan_p)
    xproj_part = pad_last(dense(inner_low, xp_w), ceil_to(xdim, 128))
    (xproj_got,) = exchange("fsdp", 3, [(xproj_part, "all")])
    xproj = jnp.sum(xproj_got, axis=0)
    delta_low = xproj[:, :DTR].astype(bf16)
    pre_delta = dense_nt(delta_low, dt_w).reshape(fs, tok, chan_p) + vec[CONV]
    step = jax.nn.softplus(pre_delta)
    step_far = jnp.where(starts[:, :, None], FAR, step)
    drive = step * inner_x

    def spread(columns):
        return jnp.broadcast_to(columns.reshape(fs, tok, DS, 1), (fs, tok, DS, 128))

    b_wide = spread(xproj[:, DTR : DTR + DS])
    c_wide = spread(xproj[:, DTR + DS : xdim])
    rate = -jnp.exp(vec[CONV + 2 :])
    rate2 = rate * LOG2E
    sizes = (fs, tok, chan_p)
    (last_state,) = scan_call(
        scan_tail_body,
        (step_far, drive, b_wide, rate2),
        ("seq", "seq", "spread", "rate"),
        ("state",),
        *sizes,
    )
    step_sum = jnp.sum(step_far, axis=1)
    state_before, sums = exchange(
        "ctx", 4, [(last_state.astype(bf16), "next"), (step_sum, "all")], reach
    )

    def decay_of(block):
        total = lax.dynamic_index_in_dim(sums, jnp.clip(block, 0, cs - 1), 0, keepdims=False)
        return jnp.exp2(total[:, None, :] * rate2)

    entry = jnp.zeros((fs, DS, chan_p), f32)
    for d in range(reach, 0, -1):
        there = jnp.where(ci >= d, state_before[d - 1].astype(f32), 0.0)
        entry = decay_of(ci - d) * entry + there
    readout, hist = scan_call(
        scan_full_body,
        (step_far, drive, b_wide, c_wide, rate2, entry),
        ("seq", "seq", "spread", "spread", "rate", "state"),
        ("seq", "hist"),
        *sizes,
    )
    skip = vec[CONV + 1]
    pre_mix = readout + skip * inner_x
    gate_s = jax.nn.sigmoid(gate_z)
    gate_silu = gate_z * gate_s
    mixture_low = (pre_mix * gate_silu).astype(bf16).reshape(fs * tok, chan_p)
    ssm_part = dense(mixture_low, mo_w).astype(bf16).reshape(fs, tok, dim)

    key_span = (reach + 1) * tok
    padded_seg = jnp.concatenate([jnp.full((reach * tok,), -1, jnp.int32), seg_row])
    key_seg = lax.dynamic_slice_in_dim(padded_seg, ci * tok, key_span, 0)
    query_seg = lax.dynamic_slice_in_dim(seg_row, ci * tok, tok, 0)
    query_pos = jnp.arange(tok, dtype=jnp.int32) + reach * tok
    key_pos = jnp.arange(key_span, dtype=jnp.int32)
    allowed = (
        (key_seg[None, :] == query_seg[:, None])
        & (key_pos[None, :] <= query_pos[:, None])
        & (query_pos[:, None] - key_pos[None, :] < WINDOW)
    )
    allowed = jnp.concatenate([jnp.ones((tok, META), jnp.bool_), allowed], axis=1)

    def group_scores(group_index):
        group_q = queries[:, group_index * groups * HD : (group_index + 1) * groups * HD].reshape(
            tok, groups, HD
        )
        group_k = key_rows[:, group_index * HD : (group_index + 1) * HD]
        group_v = key_rows[:, kv_dim + group_index * HD : kv_dim + (group_index + 1) * HD]
        raw_scores = (
            jnp.einsum("qhd,kd->hqk", group_q, group_k, preferred_element_type=f32) * scale_factor
        )
        return (group_q, group_k, group_v, jnp.where(allowed[None], raw_scores, -1e30))

    attended_parts = []
    log_totals = []
    for group_index in range(KVH):
        group_q, group_k, group_v, scores = group_scores(group_index)
        row_peak = jnp.max(scores, axis=-1, keepdims=True)
        exponent = jnp.exp(scores - row_peak)
        row_total = jnp.sum(exponent, axis=-1, keepdims=True)
        attention = (exponent / row_total).astype(bf16)
        log_totals.append(row_peak + jnp.log(row_total))
        attended_parts.append(
            jnp.einsum("hqk,kd->qhd", attention, group_v, preferred_element_type=f32).reshape(
                tok, groups * HD
            )
        )
    attended = jnp.concatenate(attended_parts, axis=1).astype(bf16)
    wide = heads_dim // fs
    (att_got,) = exchange(
        "fsdp",
        5,
        [(jnp.stack([attended[:, j * wide : (j + 1) * wide] for j in range(fs)]), "each")],
    )
    att_tp = att_got.reshape(fs * tok, wide)
    attn_part = dense(att_tp, w_attn_out).astype(bf16).reshape(fs, tok, dim)
    attn_got, ssm_got = exchange("fsdp", 6, [(attn_part, "each"), (ssm_part, "each")])
    attn_proj = jnp.sum(attn_got.astype(f32), axis=0)
    ssm_proj = jnp.sum(ssm_got.astype(f32), axis=0)
    attn_branch, attn_pull = jax.vjp(rms_norm, attn_proj, gain_rows[1])
    ssm_branch, ssm_norm_pull = jax.vjp(rms_norm, ssm_proj, gain_rows[2])
    residual = source + 0.5 * (attn_branch + ssm_branch)
    ffn_in_f, ffn_norm_pull = jax.vjp(rms_norm, residual, gain_rows[3])
    (ffn_in,) = exchange("fsdp", 7, [(ffn_in_f.astype(bf16), "all")])
    ffn_in = ffn_in.reshape(fs * tok, dim)

    gate_up = dense(ffn_in, gu_w)
    hidden_f, glu_pull = jax.vjp(
        lambda values: jax.nn.silu(values[:, :ffw_p]) * values[:, ffw_p:], gate_up
    )
    hidden = hidden_f.astype(bf16)[:, :ffw]
    down_part = dense(hidden, w_ffn_down).astype(bf16).reshape(fs, tok, dim)
    hidden_grad = pad_last(dense_nt(cot_all, w_ffn_down), ffw_p)
    gate_up_grad = glu_pull(hidden_grad)[0].astype(bf16)
    ffn_back = dense_nt(gate_up_grad, gu_w).astype(bf16).reshape(fs, tok, dim)
    back_got, down_got = exchange("fsdp", 8, [(ffn_back, "each"), (down_part, "each")])
    output = residual + jnp.sum(down_got.astype(f32), axis=0)
    resid_part, gain_ffn_grad = ffn_norm_pull(jnp.sum(back_got.astype(f32), axis=0))
    residual_grad = cotangent[0].astype(f32) + resid_part
    branch_grad = 0.5 * residual_grad
    attn_proj_grad, gain_attn_grad = attn_pull(branch_grad)
    ssm_proj_grad, gain_ssm_grad = ssm_norm_pull(branch_grad)
    attn_proj_low, ssm_proj_low = exchange(
        "fsdp", 9, [(attn_proj_grad.astype(bf16), "all"), (ssm_proj_grad.astype(bf16), "all")]
    )
    attn_proj_low = attn_proj_low.reshape(fs * tok, dim)
    ssm_proj_low = ssm_proj_low.reshape(fs * tok, dim)
    att_grad_tp = dense_nt(attn_proj_low, w_attn_out).astype(bf16).reshape(fs, tok, wide)
    (att_grad_got,) = exchange("fsdp", 10, [(att_grad_tp, "each")])
    attended_grad = jnp.concatenate([att_grad_got[j] for j in range(fs)], axis=1)

    mixture_grad = dense_nt(ssm_proj_low, mo_w).reshape(fs, tok, chan_p)
    read_grad = mixture_grad * gate_silu
    gate_grad = mixture_grad * pre_mix * (gate_s * (1.0 + gate_z * (1.0 - gate_s)))
    (first_adj,) = scan_call(
        adjoint_head_body,
        (step_far, read_grad, c_wide, rate2),
        ("seq", "seq", "spread", "rate"),
        ("state",),
        *sizes,
    )
    (adj_after,) = exchange("ctx", 11, [(first_adj.astype(bf16), "prev")], reach)
    later = jnp.zeros((fs, DS, chan_p), f32)
    for d in range(reach, 0, -1):
        there = jnp.where(ci + d < cs, adj_after[d - 1].astype(f32), 0.0)
        later = decay_of(ci + d) * later + there
    drive_grad, exp_grad, b_acc, c_acc, rate_grad = scan_call(
        adjoint_full_body,
        (step_far, drive, read_grad, b_wide, c_wide, rate2, hist, later),
        ("seq", "seq", "seq", "spread", "spread", "rate", "hist", "state"),
        ("seq", "seq", "spread", "spread", "drate"),
        *sizes,
    )
    step_grad = drive_grad * inner_x + exp_grad * LN2
    pre_delta_grad = step_grad * jax.nn.sigmoid(pre_delta)
    inner_grad = drive_grad * step + skip * read_grad
    small_grad = jnp.concatenate(
        [
            jnp.sum(pre_delta_grad, axis=(0, 1))[None],
            jnp.sum(inner_x * read_grad, axis=(0, 1))[None],
            jnp.sum(rate_grad, axis=0) * rate,
        ],
        axis=0,
    )
    pre_delta_low = pre_delta_grad.astype(bf16).reshape(fs * tok, chan_p)
    xgrad_part = pad_last(
        jnp.concatenate(
            [
                dense(pre_delta_low, dt_w),
                jnp.sum(b_acc, axis=-1).reshape(fs * tok, DS),
                jnp.sum(c_acc, axis=-1).reshape(fs * tok, DS),
            ],
            axis=1,
        ),
        ceil_to(xdim, 128),
    )
    (xgrad_got,) = exchange("fsdp", 12, [(xgrad_part, "all")])
    xproj_grad = jnp.sum(xgrad_got, axis=0)[:, :xdim].astype(bf16)
    inner_grad = inner_grad + dense_nt(xproj_grad, xp_w).reshape(fs, tok, chan_p)
    ext_grad, taps_grad = conv_pull(inner_grad)
    returned = lax.ppermute(ext_grad[:, : CONV - 1].astype(bf16), "ctx", down_ring).astype(f32)
    inner_pre_grad = ext_grad[:, CONV - 1 :] + jnp.pad(
        returned, ((0, 0), (tok - (CONV - 1), 0), (0, 0))
    )
    mamba_in_grad = (
        jnp.concatenate([inner_pre_grad, gate_grad], axis=2)
        .astype(bf16)
        .reshape(fs * tok, 2 * chan_p)
    )

    query_grads = []
    key_grads = []
    value_grads = []
    for group_index in range(KVH):
        group_q, group_k, group_v, scores = group_scores(group_index)
        attention_f = jnp.exp(scores - log_totals[group_index])
        attention = attention_f.astype(bf16)
        out_slice = attended_grad[
            :, group_index * groups * HD : (group_index + 1) * groups * HD
        ].reshape(tok, groups, HD)
        prob_grad = jnp.einsum("qhd,kd->hqk", out_slice, group_v, preferred_element_type=f32)
        value_grads.append(
            jnp.einsum("hqk,qhd->kd", attention, out_slice, preferred_element_type=f32)
        )
        score_grad = (
            attention_f * (prob_grad - jnp.sum(attention_f * prob_grad, axis=-1, keepdims=True))
        ).astype(bf16)
        query_grads.append(
            (
                jnp.einsum("hqk,kd->qhd", score_grad, group_k, preferred_element_type=f32)
                * scale_factor
            ).reshape(tok, groups * HD)
        )
        key_grads.append(
            jnp.einsum("hqk,qhd->kd", score_grad, group_q, preferred_element_type=f32)
            * scale_factor
        )
    kv_grad_all = jnp.concatenate(key_grads + value_grads, axis=1)
    kv_send = jnp.stack(
        [
            kv_grad_all[META + (reach - d) * tok : META + (reach - d + 1) * tok]
            for d in range(1, reach + 1)
        ]
    ).astype(bf16)
    meta_send = kv_grad_all[:META].astype(bf16).reshape(cs, metas, 2 * kv_dim)
    kv_back, meta_back = exchange("ctx", 13, [(kv_send, "back"), (meta_send, "each")], reach)
    own_kv_grad = kv_grad_all[META + reach * tok :]
    for d in range(1, reach + 1):
        own_kv_grad = own_kv_grad + jnp.where(ci + d < cs, kv_back[d - 1].astype(f32), 0.0)
    meta_kv_grad = jnp.sum(meta_back.astype(f32), axis=0).astype(bf16)
    qkv_grad = jnp.concatenate(
        [
            jnp.concatenate(
                [
                    jnp.concatenate(query_grads, axis=1).astype(bf16),
                    jnp.zeros((metas, heads_dim), bf16),
                ],
                axis=0,
            ),
            jnp.concatenate([own_kv_grad.astype(bf16), meta_kv_grad], axis=0),
        ],
        axis=1,
    )
    (qkv_grad_got,) = exchange(
        "fsdp", 14, [(column_parts(qkv_grad, 1, fs, qkv_grad.shape[1] // fs), "each")]
    )
    qkv_grad_tp = qkv_grad_got.reshape(fs * (tok + metas), -1)
    normed_back = dense_nt(qkv_grad_tp, qkv_w).reshape(fs, tok + metas, dim)
    normed_back = normed_back + jnp.pad(
        dense_nt(mamba_in_grad, mi_w).reshape(fs, tok, dim), ((0, 0), (0, metas), (0, 0))
    )
    (normed_got,) = exchange("fsdp", 15, [(normed_back.astype(bf16), "each")])
    normed_grad = jnp.sum(normed_got.astype(f32), axis=0)
    source_part, gain_in_grad = norm_pull(normed_grad[:tok])
    source_grad = residual_grad + source_part
    meta_grad, gain_in_meta = meta_pull(normed_grad[tok:])

    embed_grad = jnp.concatenate(
        [
            lax.dynamic_update_slice(jnp.zeros((META, dim), f32), meta_grad, (ci * metas, 0)),
            jnp.stack([gain_in_grad + gain_in_meta, gain_attn_grad, gain_ssm_grad, gain_ffn_grad]),
        ],
        axis=0,
    )
    vec_grad = jnp.concatenate([taps_grad, small_grad], axis=0)[:, :chan]
    vec_grad = lax.dynamic_update_slice(
        jnp.zeros((vec_grad.shape[0], DI), f32), vec_grad, (0, fi * chan)
    )
    ssm_total, embed_total = lax.psum((vec_grad, embed_grad), ("fsdp", "ctx"))

    def summed(value):
        return lax.psum_scatter(value, "ctx", scatter_dimension=0, tiled=True)

    def by_columns(operand, partner):
        rows = operand.shape[1] // halves
        cols = partner.shape[1] // fs
        pieces = jnp.stack([partner[:, j * cols : (j + 1) * cols] for j in range(fs)])
        grad = jnp.einsum("tr,jtn->jrn", operand, pieces, preferred_element_type=f32)
        return crossed(summed(grad.astype(bf16).reshape(cs * rows, cols))).astype(f32)

    even = fi % 2 == 0
    low_side = fi < fs // 2
    route_a = [(j, j // 2 if j % 2 == 0 else (fs + j) // 2) for j in range(fs)]
    route_b = [(j, (fs + j) // 2 if j % 2 == 0 else j // 2) for j in range(fs)]

    def paired(operand, partner, width):
        grad = summed(dense_tn(operand, partner).astype(bf16))
        padded = grad.shape[1] // 2
        first, second = grad[:, :padded], grad[:, padded:]
        got_a = lax.ppermute(jnp.where(even, first, second), "fsdp", route_a)
        got_b = lax.ppermute(jnp.where(even, second, first), "fsdp", route_b)
        left = jnp.where(low_side, got_a, got_b)[:, :width]
        right = jnp.where(low_side, got_b, got_a)[:, :width]
        return jnp.concatenate([left, right], axis=1).astype(f32)

    ffn_down_gradient = by_columns(hidden, cot_all)
    gate_up_gradient = paired(ffn_in, gate_up_grad, ffw)
    attn_gradient = by_columns(att_tp, attn_proj_low)
    mamba_out_gradient = by_columns(mixture_low[:, :chan], ssm_proj_low)
    mamba_in_gradient = paired(normed_all, mamba_in_grad, chan)
    ssm_proj_gradient = by_columns(
        jnp.concatenate([inner_low[:, :chan], pre_delta_low[:, :chan]], axis=0),
        jnp.concatenate(
            [
                jnp.pad(xproj_grad, ((0, 0), (0, DTR))),
                jnp.pad(delta_low, ((0, 0), (xdim, 0))),
            ],
            axis=0,
        ),
    )
    qkv_operand = jnp.concatenate(
        [
            normed_all.reshape(fs, tok, dim),
            jnp.broadcast_to(meta_low[None], (fs, metas, dim)),
        ],
        axis=1,
    ).reshape(fs * (tok + metas), dim)
    qkv_gradient = summed(dense_tn(qkv_operand, qkv_grad_tp).astype(bf16)).astype(f32)

    def adam_block(gradient, moments_old, weight):
        return adam_step(gradient, moments_old, weight_block(weight).astype(f32))

    qkv_moments, qkv_update = adam_block(qkv_gradient, m_qkv, w_qkv)
    attn_moments, attn_update = adam_block(attn_gradient, m_attn_out, w_attn_out)
    mamba_in_moments, mamba_in_update = adam_block(mamba_in_gradient, m_mamba_in, w_mamba_in)
    ssm_proj_moments, ssm_proj_update = adam_block(ssm_proj_gradient, m_ssm_proj, w_ssm_proj)
    mamba_out_moments, mamba_out_update = adam_block(mamba_out_gradient, m_mamba_out, w_mamba_out)
    gate_up_moments, gate_up_update = adam_block(gate_up_gradient, m_gate_up, w_gate_up)
    ffn_down_moments, ffn_down_update = adam_block(ffn_down_gradient, m_ffn_down, w_ffn_down)
    ssm_vec_moments, ssm_vec_update = adam_step(ssm_total, m_ssm_vec, ssm_vec)
    embed_moments, embed_update = adam_step(embed_total, m_embed_small, embed_small)
    return (
        output.astype(jnp.bfloat16)[None],
        source_grad[None],
        qkv_gradient,
        qkv_moments,
        qkv_update,
        attn_gradient,
        attn_moments,
        attn_update,
        mamba_in_gradient,
        mamba_in_moments,
        mamba_in_update,
        ssm_proj_gradient,
        ssm_proj_moments,
        ssm_proj_update,
        mamba_out_gradient,
        mamba_out_moments,
        mamba_out_update,
        gate_up_gradient,
        gate_up_moments,
        gate_up_update,
        ffn_down_gradient,
        ffn_down_moments,
        ffn_down_update,
        ssm_total,
        ssm_vec_moments,
        ssm_vec_update,
        embed_total,
        embed_moments,
        embed_update,
    )


def solution(mesh):
    in_specs = (
        P("fsdp", "ctx", None),
        P("fsdp", "ctx", None),
        P("fsdp", None),
        P("fsdp", None),
        P(None, "ctx", "fsdp"),
        P("fsdp", None),
        P(None, "ctx", "fsdp"),
        P("fsdp", None),
        P(None, "ctx", "fsdp"),
        P("fsdp", None),
        P(None, "ctx", "fsdp"),
        P("fsdp", None),
        P(None, "ctx", "fsdp"),
        P("fsdp", None),
        P(None, "ctx", "fsdp"),
        P("fsdp", None),
        P(None, "ctx", "fsdp"),
        P(),
        P(),
        P(),
        P(),
    )
    out_specs = (
        P("fsdp", "ctx", None),
        P("fsdp", "ctx", None),
        P("ctx", "fsdp"),
        P("ctx", "fsdp"),
        P("ctx", "fsdp"),
        P("ctx", "fsdp"),
        P("ctx", "fsdp"),
        P("ctx", "fsdp"),
        P("ctx", "fsdp"),
        P("ctx", "fsdp"),
        P("ctx", "fsdp"),
        P("ctx", "fsdp"),
        P("ctx", "fsdp"),
        P("ctx", "fsdp"),
        P("ctx", "fsdp"),
        P("ctx", "fsdp"),
        P("ctx", "fsdp"),
        P("ctx", "fsdp"),
        P("ctx", "fsdp"),
        P("ctx", "fsdp"),
        P("ctx", "fsdp"),
        P("ctx", "fsdp"),
        P("ctx", "fsdp"),
        P(),
        P(),
        P(),
        P(),
        P(),
        P(),
    )
    return jax.shard_map(shards, mesh=mesh, in_specs=in_specs, out_specs=out_specs, check_vma=False)
```

time: 7400 us -> 1830 us (0.25); the launches traced: 7310 us -> 1810 us
  local copies, waits for them, and re-layouts: 2430 us -> 196 us
  other arithmetic: 2140 us -> 134 us
  waiting for transfers between devices: 2370 us -> 588 us
  Pallas kernels: 0 us -> 638 us
  blocking collectives: 86.8 us -> 0 us
    unnamed x35 -> x12, waiting for transfers between devices: 1450 us -> 185 us
    dynamic_update_slice x768 -> x1, local copies, waits for them, and re-layouts: 1090 us -> 1.8 us  [shards(): lax.dynamic_update_slice(jnp.zeros((vec_grad.shape[0], DI), f32), vec_gra...]
    dynamic_slice x770 -> x9, local copies, waits for them, and re-layouts: 820 us -> 15.1 us  [the longest x7 14.1 us: weight_block(): lax.dynamic_slice(weight, (ci % halves * rows, ci // halves * cols), (row...]
    pallas_call x0 -> x20, Pallas kernels: none -> 638 us  [the longest x16 560 us: exchange(): pl.pallas_call(functools.partial(exchange_body, axis, n, reach, tuple(mod...]
    reduce_sum x257 -> x13, other arithmetic: 580 us -> 33 us  [the longest x1 7 us: conv_silu(): extended[:, offset:offset + length_out] * conv_taps[offset]]
    dynamic_update_slice x256 -> x1, other arithmetic: 532 us -> 1.72 us  [shards(): lax.dynamic_update_slice(jnp.zeros((META, dim), f32), meta_grad, (ci * me...]
    reduce_scatter x4 -> x3, waiting for transfers between devices: 670 us -> 268 us  [summed(): return lax.psum_scatter(value, 'ctx', scatter_dimension=0, tiled=True)]
    mul x259 -> x4, other arithmetic: 360 us -> 4.55 us  [the longest x1 3.22 us: shards(): jax.nn.silu(values[:, :ffw_p]) * values[:, ffw_p:]]
where the time goes in v1:
time: 1830 us; the launch traced here: 1810 us
  Pallas kernels  638 us (35%)
  waiting for transfers between devices  588 us (32%)
  local copies, waits for them, and re-layouts  196 us (11%)
  matrix products  174 us (10%)
  other arithmetic  134 us (7%)
  starting transfers between devices  62.7 us (3%)
  between operations  18.7 us (1%)
    pallas_call x16, Pallas kernels, exchange(): pl.pallas_call(functools.partial(exchange_body, axis, n, reach, tuple(mod...  560 us
    reduce_scatter x3, waiting for transfers between devices, summed(): return lax.psum_scatter(value, 'ctx', scatter_dimension=0, tiled=True)  268 us
    unnamed x12, waiting for transfers between devices  185 us
    unnamed x354, local copies, waits for them, and re-layouts  83.5 us
    ppermute x11, waiting for transfers between devices, crossed(): return lax.ppermute(value, both, cross)  78.9 us
    pallas_call x4, Pallas kernels, scan_call(): pl.pallas_call(functools.partial(body, rows, length), grid=(rows_all // r...  77.8 us
    ppermute x11, starting transfers between devices, crossed(): return lax.ppermute(value, both, cross)  44.3 us
    dot_general x8, matrix products, dense_nt(): lax.dot_general(operand, partner, (((1,), (1,)), ((), ())), preferred_ele...  42.5 us
  transfers between devices with their start and end apart: 26, of which 12 were waited for; matrix products, arithmetic and copies ran while one was open for 15% of the time, Pallas kernels for 15%

profile of v1, /device:TPU:2, one launch (start us, length us, event | category | flops | bytes accessed | tf_op | source)
XLA Modules:
  0.0 1811.3 jit_solution(15506519318501494039)
XLA Ops:
  8.0 7.3 fusion.302
  32.3 121.7 %shard_map.428 = (bf16[4,128,1600]{2,1,0:T(8,128)(2,1)}, bf16[4,128,1600]{2,1,0:T(8,128)(2,1)}, s32[4,1,1024]{2,1,0:T(1,128)}, bf16[4,400,1792]{2,1,0:T(8,128)(2,1)}, bf16[4,400,560]{2,1,0:T(8,128)(2,1)}) custom-call(bf16[128,1600]{1,0:T(8,128)(2,1)} %fusion.160.refs_0_, bf16[128,1600]{1,0:T(8,128)(2,1)} %bitcast.699, s32[1,1024]{1,0:T(1,128)} %refs_2_.1, ...), custom_call_target="tpu_custom_call" | custom-call | tf_op jit(solution)/shard_map/pallas_call | solution.py:108
  154.0 6.8 fusion.319
  174.8 7.3 all-to-all-start
  189.4 98.1 %shard_map.429 = bf16[4,144,560]{2,1,0:T(8,128)(2,1)} custom-call(bf16[4,144,560]{2,1,0:T(8,128)(2,1)} %pad_maximum_fusion.7.refs_0_), custom_call_target="tpu_custom_call" | custom-call | tf_op jit(solution)/shard_map/pallas_call | solution.py:108
  290.3 17.6 shard_map.430
  336.7 7.0 shard_map.431
  348.2 7.1 fusion.321
  366.5 5.9 fusion.286
  374.7 25.3 %shard_map.432 = f32[4,512,256]{2,1,0:T(8,128)} custom-call(f32[512,256]{1,0:T(8,128)} %pad.140.refs_0_), custom_call_target="tpu_custom_call" | custom-call | tf_op jit(solution)/shard_map/pallas_call | solution.py:108
  410.8 9.9 shard_map.433
  422.3 25.9 %shard_map.434 = (bf16[4,4,16,896]{3,2,1,0:T(8,128)(2,1)}, f32[8,4,896]{2,1,0:T(4,128)}) custom-call(bf16[4,16,896]{2,1,0:T(8,128)(2,1)} %convert_element_type.324.refs_0_, f32[4,896]{1,0:T(4,128)} %get-tuple-element.251.refs_1_), custom_call_target="tpu_custom_call" | custom-call | tf_op jit(solution)/shard_map/pallas_call | solution.py:108
  454.3 19.7 %shard_map.435 = (f32[4,128,896]{2,1,0:T(8,128)}, f32[4,128,16,896]{3,2,1,0:T(8,128)}) custom-call(f32[4,128,896]{2,1,0:T(8,128)} %get-tuple-element.252.step_ref, f32[4,128,896]{2,1,0:T(8,128)} %get-tuple-element.278.u_ref, f32[4,128,16,128]{3,2,1,0:T(8,128)} %broadcast_in_dim.262.b_ref, f32[4,128,16,128]{3,2,1,0:T(8,128)} %broadcast_in_dim.264.c_ref, ...), custom_call_target="tpu_custom_call" | custom-call | tf_op jit(solution)/shard_map/pallas_call | solution.py:248
  484.8 39.9 %shard_map.436 = (bf16[4,128,1600]{2,1,0:T(8,128)(2,1)}, bf16[4,128,1600]{2,1,0:T(8,128)(2,1)}) custom-call(bf16[4,128,1600]{2,1,0:T(8,128)(2,1)} %bitcast.693, bf16[4,128,1600]{2,1,0:T(8,128)(2,1)} %bitcast.695), custom_call_target="tpu_custom_call" | custom-call | tf_op jit(solution)/shard_map/pallas_call | solution.py:108
  530.1 21.1 %shard_map.437 = bf16[4,128,1600]{2,1,0:T(8,128)(2,1)} custom-call(bf16[128,1600]{1,0:T(8,128)(2,1)} %multiply_convert_fusion.2.refs_0_), custom_call_target="tpu_custom_call" | custom-call | tf_op jit(solution)/shard_map/pallas_call | solution.py:108
  553.4 9.1 fusion.320
  567.2 6.1 convolution_convert_fusion.2
  576.9 11.4 convolution_convert_fusion.5
  592.2 39.5 %shard_map.438 = (bf16[4,128,1600]{2,1,0:T(8,128)(2,1)}, bf16[4,128,1600]{2,1,0:T(8,128)(2,1)}) custom-call(bf16[4,128,1600]{2,1,0:T(8,128)(2,1)} %bitcast.696, bf16[4,128,1600]{2,1,0:T(8,128)(2,1)} %bitcast.694), custom_call_target="tpu_custom_call" | custom-call | tf_op jit(solution)/shard_map/pallas_call | solution.py:108
  637.3 39.4 %shard_map.439 = (bf16[4,128,1600]{2,1,0:T(8,128)(2,1)}, bf16[4,128,1600]{2,1,0:T(8,128)(2,1)}) custom-call(bf16[128,1600]{1,0:T(8,128)(2,1)} %get-tuple-element.311.refs_0_, bf16[128,1600]{1,0:T(8,128)(2,1)} %get-tuple-element.310.refs_1_), custom_call_target="tpu_custom_call" | custom-call | tf_op jit(solution)/shard_map/pallas_call | solution.py:108
  682.2 8.5 shard_map.440
  763.5 38.7 %shard_map.441 = (bf16[4,128,640]{2,1,0:T(8,128)(2,1)}, bf16[8,16,640]{2,1,0:T(8,128)(2,1)}) custom-call(bf16[4,128,640]{2,1,0:T(8,128)(2,1)} %pad_maximum_fusion.9.refs_0_, bf16[8,16,640]{2,1,0:T(8,128)(2,1)} %bitcast.739), custom_call_target="tpu_custom_call" | custom-call | tf_op jit(solution)/shard_map/pallas_call | solution.py:108
  803.2 8.0 multiply_reduce_fusion
  811.1 10.8 shard_map.443
  823.6 19.3 %shard_map.444 = bf16[4,4,16,896]{3,2,1,0:T(8,128)(2,1)} custom-call(bf16[4,16,896]{2,1,0:T(8,128)(2,1)} %convert_element_type.360.refs_0_), custom_call_target="tpu_custom_call" | custom-call | tf_op jit(solution)/shard_map/pallas_call | solution.py:108
  847.0 37.3 %shard_map.445 = (f32[4,128,896]{2,1,0:T(8,128)}, f32[4,128,896]{2,1,0:T(8,128)}, f32[4,128,16,128]{3,2,1,0:T(8,128)}, f32[4,128,16,128]{3,2,1,0:T(8,128)}, f32[1,16,896]{2,1,0:T(8,128)}) custom-call(f32[4,128,896]{2,1,0:T(8,128)} %get-tuple-element.252.step_ref, f32[4,128,896]{2,1,0:T(8,128)} %get-tuple-element.278.u_ref, ...), custom_call_target="tpu_custom_call" | custom-call | tf_op jit(solution)/shard_map/pallas_call | solution.py:248
  899.1 24.2 %shard_map.446 = f32[4,512,256]{2,1,0:T(8,128)} custom-call(f32[512,256]{1,0:T(8,128)} %select_maximum_fusion.refs_0_), custom_call_target="tpu_custom_call" | custom-call | tf_op jit(solution)/shard_map/pallas_call | solution.py:108
  928.7 7.0 multiply_reduce_fusion.3
  941.0 10.7 shard_map.442
  955.6 6.4 fusion.128
  965.1 23.4 %shard_map.447 = bf16[4,144,1600]{2,1,0:T(8,128)(2,1)} custom-call(bf16[4,144,1600]{2,1,0:T(8,128)(2,1)} %add_convert_fusion.1.refs_0_), custom_call_target="tpu_custom_call" | custom-call | tf_op jit(solution)/shard_map/pallas_call | solution.py:108
  1054.7 6.6 fusion.7
  1061.3 8.1 copy.658
  1070.6 7.4 bitcast_convert_fusion
  1078.2 11.7 convolution_convert_fusion
  1140.1 38.8 %all-reduce.42.cloned.1.call-done = (f32[22,3200]{1,0:T(8,128)}, f32[132,1600]{1,0:T(8,128)}) async-done(((f32[22,3200]{1,0:T(8,128)}, f32[132,1600]{1,0:T(8,128)}), (f32[22,3200]{1,0:T(8,128)}, f32[132,1600]{1,0:T(8,128)})) %all-reduce.42.cloned.1.call-update) | async-done | bytes 1126416 | tf_op jit(solution)/shard_map/psum | solution.py:730
  1182.8 8.2 collective-permute-start.8
  1194.3 45.7 %collective-permute-done.9 = bf16[400,58]{0,1:T(8,128)(2,1)} collective-permute-done((bf16[400,58]{0,1:T(8,128)(2,1)}, bf16[400,58]{0,1:T(8,128)(2,1)}, u32[]{:S(2)}, u32[]{:S(2)}) %collective-permute-start.9) | collective-permute-done | bytes 46432 | tf_op jit(solution)/shard_map/ppermute | solution.py:372
  1242.0 5.7 collective-permute-start.3
  1249.4 18.0 reduce-scatter.24.cloned.1.call-done
  1277.5 33.1 %collective-permute-done.2 = bf16[200,560]{1,0:T(8,128)(2,1)S(1)} collective-permute-done((bf16[200,560]{1,0:T(8,128)(2,1)S(1)}, bf16[200,560]{1,0:T(8,128)(2,1)S(1)}, u32[]{:S(2)}, u32[]{:S(2)}) %collective-permute-start.2) | collective-permute-done | bytes 224032 | tf_op jit(solution)/shard_map/ppermute | solution.py:372
  1312.5 58.0 %reduce-scatter.28.cloned.1.call-done = bf16[200,560]{1,0:T(8,128)(2,1)} async-done(((bf16[1600,560]{1,0:T(8,128)(2,1)}), bf16[200,560]{1,0:T(8,128)(2,1)}) %reduce-scatter.28.cloned.1.call-update) | async-done | bytes 224016
  1373.0 108.9 %reduce-scatter.26.cloned.1.call-done = bf16[688,400]{1,0:T(8,128)(2,1)} async-done(((bf16[5504,400]{1,0:T(8,128)(2,1)}), bf16[688,400]{1,0:T(8,128)(2,1)}) %reduce-scatter.26.cloned.1.call-update) | async-done | bytes 550416
  1496.2 121.4 %reduce-scatter.18.cloned.1.call-done = bf16[200,1792]{1,0:T(8,128)(2,1)} async-done(((bf16[1600,1792]{1,0:T(8,128)(2,1)}), bf16[200,1792]{1,0:T(8,128)(2,1)}) %reduce-scatter.18.cloned.1.call-update) | async-done | bytes 716816 | tf_op jit(solution)/shard_map/reduce_scatter | solution.py:733
  1624.1 6.6 collective-permute-done.5
  1631.3 146.6 %reduce-scatter.20.cloned.1.call-done = bf16[200,2816]{1,0:T(8,128)(2,1)} async-done(((bf16[1600,2816]{1,0:T(8,128)(2,1)}), bf16[200,2816]{1,0:T(8,128)(2,1)}) %reduce-scatter.20.cloned.1.call-update) | async-done | bytes 1126416 | tf_op jit(solution)/shard_map/reduce_scatter | solution.py:733
  1786.0 9.6 collective-permute-done.12
  1796.3 5.5 fusion.35
  (642 shorter events, 432.2 us)
Async XLA Ops:
  19.7 164.5 %copy-start.92 = (f32[1600]{0:T(1024)}, f32[1600]{0:T(1024)S(1)}, u32[]{:S(2)}) copy-start(f32[1600]{0:T(1024)S(1)} %get-tuple-element.210) | copy-start | bytes 19204
  19.7 507.4 %copy-start.99 = (f32[1600]{0:T(1024)}, f32[1600]{0:T(1024)S(1)}, u32[]{:S(2)}) copy-start(f32[1600]{0:T(1024)S(1)} %get-tuple-element.208) | copy-start | bytes 19204
  19.7 507.4 %copy-start.101 = (f32[1600]{0:T(1024)}, f32[1600]{0:T(1024)S(1)}, u32[]{:S(2)}) copy-start(f32[1600]{0:T(1024)S(1)} %get-tuple-element.209) | copy-start | bytes 19204
  161.5 204.9 %collective-permute-start = (f32[4,3,896]{2,1,0:T(4,128)}, f32[4,3,896]{2,1,0:T(4,128)}, u32[]{:S(2)}, u32[]{:S(2)}) collective-permute-start(f32[4,3,896]{2,1,0:T(4,128)} %slice.731), channel_id=1, source_target_pairs={{0,1},{1,2},{2,3},{3,4},{4,5},{5,6},{6,7},{8,9},{9,10},{10,11},{11... | collective-permute-start | bytes 129032 | tf_op jit(solution)/shard_map/ppermute | solution.py:445
  174.8 378.6 %all-to-all-start = ((bf16[4,400,2816]{2,1,0:T(8,128)(2,1)}), bf16[4,400,2816]{2,1,0:T(8,128)(2,1)}, u32[]{:S(2)}, u32[]{:S(2)}) async-start(bf16[4,400,2816]{2,1,0:T(8,128)(2,1)} %pad_maximum_fusion), calls=%async_computation | async-start | bytes 18022400 | tf_op jit(solution)/shard_map/all_to_all | solution.py:403
  182.1 996.8 %all-reduce.42.cloned.1.call-start = ((), (), s32[]{:S(2)}) async-start(), calls=%async_computation.15 | async-start | bytes 2424832 | tf_op jit(solution)/shard_map/psum | solution.py:730
  290.3 23.2 %copy-start.60 = (bf16[128,640]{1,0:T(8,128)(2,1)S(1)}, bf16[128,640]{1,0:T(8,128)(2,1)}, u32[]{:S(2)}) copy-start(bf16[128,640]{1,0:T(8,128)(2,1)} %pad_maximum_fusion.14.refs_0_) | copy-start | bytes 491524
  336.7 29.1 %copy-start.62 = (f32[22,800]{1,0:T(8,128)}, f32[22,800]{1,0:T(8,128)S(1)}, u32[]{:S(2)}) copy-start(f32[22,800]{1,0:T(8,128)S(1)} %constant_dynamic-slice_fusion) | copy-start | bytes 211204
  366.4 37.8 %copy-start.106 = (f32[896]{0:T(1024)}, f32[896]{0:T(1024)S(1)}, u32[]{:S(2)}) copy-start(f32[896]{0:T(1024)S(1)} %get-tuple-element.217) | copy-start | bytes 10756
  410.8 39.0 %copy-start.49 = (f32[16,896]{1,0:T(8,128)S(1)}, f32[16,896]{1,0:T(8,128)}, u32[]{:S(2)}) copy-start(f32[16,896]{1,0:T(8,128)} %fusion.252.rate_ref) | copy-start | bytes 172036
  527.1 108.8 %copy-start.128 = (f32[128]{0:T(128)}, f32[128]{0:T(128)S(1)}, u32[]{:S(2)}) copy-start(f32[128]{0:T(128)S(1)} %fusion.264) | copy-start | bytes 1540
  527.9 108.1 %copy-start.130 = (f32[128]{0:T(128)}, f32[128]{0:T(128)S(1)}, u32[]{:S(2)}) copy-start(f32[128]{0:T(128)S(1)} %fusion.265) | copy-start | bytes 1540
  757.6 45.5 %copy-start.13 = (f32[4,128,896]{2,1,0:T(8,128)S(1)}, f32[4,128,896]{2,1,0:T(8,128)}, u32[]{:S(2)}) copy-start(f32[4,128,896]{2,1,0:T(8,128)} %get-tuple-element.254) | copy-start | bytes 5505028
  847.0 37.4 %copy-start.18 = (f32[512,896]{1,0:T(8,128)S(1)}, f32[512,896]{1,0:T(8,128)}, u32[]{:S(2)}) copy-start(f32[512,896]{1,0:T(8,128)} %copy-done.17) | copy-start | bytes 5505028
  847.0 37.4 %copy-start.107 = (f32[896]{0:T(1024)S(1)}, f32[896]{0:T(1024)}, u32[]{:S(2)}) copy-start(f32[896]{0:T(1024)} %copy-done.106) | copy-start | bytes 10756
  937.7 16.7 collective-permute-start.1
  998.6 182.6 %reduce-scatter.22.cloned.1.call-start = ((), (), s32[]{:S(2)}) async-start(), calls=%async_computation.11 | async-start | bytes 921600
  1005.3 236.7 %reduce-scatter.16.cloned.1.call-start = ((), (), s32[]{:S(2)}) async-start(), calls=%async_computation.8 | async-start | bytes 1843200 | tf_op jit(solution)/shard_map/reduce_scatter | solution.py:733
  1019.1 248.3 %reduce-scatter.24.cloned.1.call-start = ((), (), s32[]{:S(2)}) async-start(), calls=%async_computation.12 | async-start | bytes 3686400
  1038.8 331.7 %reduce-scatter.28.cloned.1.call-start = ((), (), s32[]{:S(2)}) async-start(), calls=%async_computation.14 | async-start | bytes 2304000
  1044.8 437.1 %reduce-scatter.26.cloned.1.call-start = ((), (), s32[]{:S(2)}) async-start(), calls=%async_computation.13 | async-start | bytes 6340608
  1069.4 548.2 %reduce-scatter.18.cloned.1.call-start = ((), (), s32[]{:S(2)}) async-start(), calls=%async_computation.9 | async-start | bytes 6451200 | tf_op jit(solution)/shard_map/reduce_scatter | solution.py:733
  1078.0 700.0 %reduce-scatter.20.cloned.1.call-start = ((), (), s32[]{:S(2)}) async-start(), calls=%async_computation.10 | async-start | bytes 10137600 | tf_op jit(solution)/shard_map/reduce_scatter | solution.py:733
  1092.2 528.4 %collective-permute-start.16 = (bf16[688,400]{0,1:T(8,128)(2,1)}, bf16[688,400]{0,1:T(8,128)(2,1)}, u32[]{:S(2)}, u32[]{:S(2)}) collective-permute-start(bf16[688,400]{0,1:T(8,128)(2,1)} %dynamic_slice.80), channel_id=1, source_target_pairs={{0,0},{1,1},{2,8},{3,9},{4,16},{5,17},{6,24},{7,25},{8,2},{9,3},{1... | collective-permute-start | bytes 1651208 | tf_op jit(solution)/shard_map/ppermute | solution.py:372
  1097.7 698.6 %collective-permute-start.14 = (bf16[200,2752]{1,0:T(8,128)(2,1)}, bf16[200,2752]{1,0:T(8,128)(2,1)}, u32[]{:S(2)}, u32[]{:S(2)}) collective-permute-start(bf16[200,2752]{1,0:T(8,128)(2,1)} %dynamic_slice.79), channel_id=1, source_target_pairs={{0,0},{1,1},{2,8},{3,9},{4,16},{5,17},{6,24},{7,25},{8,2},{9,3},{1... | collective-permute-start | bytes 3302408 | tf_op jit(solution)/shard_map/ppermute | solution.py:372
  1104.8 379.3 %collective-permute-start.11 = (bf16[400,400]{0,1:T(8,128)(2,1)}, bf16[400,400]{0,1:T(8,128)(2,1)}, u32[]{:S(2)}, u32[]{:S(2)}) collective-permute-start(bf16[400,400]{0,1:T(8,128)(2,1)} %dynamic_slice.78), channel_id=1, source_target_pairs={{0,0},{1,1},{2,8},{3,9},{4,16},{5,17},{6,24},{7,25},{8,2},{9,3},{1... | collective-permute-start | bytes 960008 | tf_op jit(solution)/shard_map/ppermute | solution.py:372
  1109.2 130.9 %collective-permute-start.9 = (bf16[400,58]{0,1:T(8,128)(2,1)}, bf16[400,58]{0,1:T(8,128)(2,1)}, u32[]{:S(2)}, u32[]{:S(2)}) collective-permute-start(bf16[400,58]{0,1:T(8,128)(2,1)} %copy.671), channel_id=1, source_target_pairs={{0,0},{1,1},{2,8},{3,9},{4,16},{5,17},{6,24},{7,25},{8,2},{9,3},{1... | collective-permute-start | bytes 139208 | tf_op jit(solution)/shard_map/ppermute | solution.py:372
  1137.6 53.5 %copy-start.37 = (f32[1,132,1600]{2,0,1:T(1,128)S(1)}, f32[1,132,1600]{2,0,1:T(1,128)}, u32[]{:S(2)}) copy-start(f32[1,132,1600]{2,0,1:T(1,128)} %get-tuple-element.283) | copy-start | bytes 2534404
  1137.6 53.5 %copy-start.38 = (f32[1,132,1600]{2,0,1:T(1,128)S(1)}, f32[1,132,1600]{2,0,1:T(1,128)}, u32[]{:S(2)}) copy-start(f32[1,132,1600]{2,0,1:T(1,128)} %get-tuple-element.284) | copy-start | bytes 2534404
  1182.8 59.2 %collective-permute-start.8 = (bf16[400,58]{0,1:T(8,128)(2,1)}, bf16[400,58]{0,1:T(8,128)(2,1)S(1)}, u32[]{:S(2)}, u32[]{:S(2)}) collective-permute-start(bf16[400,58]{0,1:T(8,128)(2,1)} %copy.651), channel_id=1, source_target_pairs={{0,0},{1,1},{2,8},{3,9},{4,16},{5,17},{6,24},{7,25},{8,2},{9,3},{1... | collective-permute-start | bytes 139208 | tf_op jit(solution)/shard_map/ppermute | solution.py:372
  1191.1 49.0 %copy-start.98 = (bf16[200,400]{1,0:T(8,128)(2,1)S(1)}, bf16[200,400]{1,0:T(8,128)(2,1)}, u32[]{:S(2)}) copy-start(bf16[200,400]{1,0:T(8,128)(2,1)} %dynamic_slice.75) | copy-start | bytes 480004
  1191.1 56.7 %copy-start.90 = (f32[1,400,58]{1,0,2:T(1,128)S(1)}, f32[1,400,58]{1,0,2:T(1,128)}, u32[]{:S(2)}) copy-start(f32[1,400,58]{1,0,2:T(1,128)} %get-tuple-element.334) | copy-start | bytes 278404
  1191.1 56.7 %copy-start.91 = (f32[1,400,58]{1,0,2:T(1,128)S(1)}, f32[1,400,58]{1,0,2:T(1,128)}, u32[]{:S(2)}) copy-start(f32[1,400,58]{1,0,2:T(1,128)} %get-tuple-element.335) | copy-start | bytes 278404
  1191.1 77.5 %copy-start.94 = (bf16[200,560]{1,0:T(8,128)(2,1)S(1)}, bf16[200,560]{1,0:T(8,128)(2,1)}, u32[]{:S(2)}) copy-start(bf16[200,560]{1,0:T(8,128)(2,1)} %dynamic_slice.74) | copy-start | bytes 672004
  1194.3 82.0 %copy-start.68 = (f32[2,200,400]{2,1,0:T(8,128)S(1)}, f32[2,200,400]{2,1,0:T(8,128)}, u32[]{:S(2)}) copy-start(f32[2,200,400]{2,1,0:T(8,128)} %param.27) | copy-start | bytes 1920004
  1240.1 28.6 %collective-permute-start.4 = (bf16[200,400]{1,0:T(8,128)(2,1)S(1)}, bf16[200,400]{1,0:T(8,128)(2,1)S(1)}, u32[]{:S(2)}, u32[]{:S(2)}) collective-permute-start(bf16[200,400]{1,0:T(8,128)(2,1)S(1)} %copy-done.98), channel_id=1, source_target_pairs={{0,0},{1,1},{2,8},{3,9},{4,16},{5,17},{6,24},{7,25},{8,2},{9,3},{1... | collective-permute-start | bytes 480008 | tf_op jit(solution)/shard_map/ppermute | solution.py:372
  1242.0 31.5 %collective-permute-start.3 = (bf16[200,400]{1,0:T(8,128)(2,1)}, bf16[200,400]{1,0:T(8,128)(2,1)S(1)}, u32[]{:S(2)}, u32[]{:S(2)}) collective-permute-start(bf16[200,400]{1,0:T(8,128)(2,1)} %reduce-scatter.16.cloned.1.call-done), channel_id=1, source_target_pairs={{0,0},{1,1},{2,8},{3,9},{4,16},{5,17},{6,24},{7,25},{8,2},{9,3},{1... | collective-permute-start | bytes 480008 | tf_op jit(solution)/shard_map/ppermute | solution.py:372
  1268.7 42.0 %collective-permute-start.2 = (bf16[200,560]{1,0:T(8,128)(2,1)S(1)}, bf16[200,560]{1,0:T(8,128)(2,1)S(1)}, u32[]{:S(2)}, u32[]{:S(2)}) collective-permute-start(bf16[200,560]{1,0:T(8,128)(2,1)S(1)} %copy-done.94), channel_id=1, source_target_pairs={{0,0},{1,1},{2,8},{3,9},{4,16},{5,17},{6,24},{7,25},{8,2},{9,3},{1... | collective-permute-start | bytes 672008 | tf_op jit(solution)/shard_map/ppermute | solution.py:372
  1273.6 214.1 %collective-permute-start.10 = (bf16[400,400]{0,1:T(8,128)(2,1)S(1)}, bf16[400,400]{0,1:T(8,128)(2,1)}, u32[]{:S(2)}, u32[]{:S(2)}) collective-permute-start(bf16[400,400]{0,1:T(8,128)(2,1)S(1)} %copy.653), channel_id=1, source_target_pairs={{0,0},{1,1},{2,8},{3,9},{4,16},{5,17},{6,24},{7,25},{8,2},{9,3},{1... | collective-permute-start | bytes 960008 | tf_op jit(solution)/shard_map/ppermute | solution.py:372
  1277.5 210.3 %copy-start.39 = (f32[1,400,400]{1,2,0:T(8,128)S(1)}, f32[1,400,400]{1,2,0:T(8,128)}, u32[]{:S(2)}) copy-start(f32[1,400,400]{1,2,0:T(8,128)} %copy.677) | copy-start | bytes 1920004
  1277.5 210.3 %copy-start.40 = (f32[1,400,400]{1,2,0:T(8,128)S(1)}, f32[1,400,400]{1,2,0:T(8,128)}, u32[]{:S(2)}) copy-start(f32[1,400,400]{1,2,0:T(8,128)} %copy.678) | copy-start | bytes 1920004
  1310.6 470.6 %collective-permute-start.7 = (bf16[200,1600]{1,0:T(8,128)(2,1)}, bf16[200,1600]{1,0:T(8,128)(2,1)}, u32[]{:S(2)}, u32[]{:S(2)}) collective-permute-start(bf16[200,1600]{1,0:T(8,128)(2,1)} %dynamic_slice.76), channel_id=1, source_target_pairs={{0,0},{1,1},{2,8},{3,9},{4,16},{5,17},{6,24},{7,25},{8,2},{9,3},{1... | collective-permute-start | bytes 1920008 | tf_op jit(solution)/shard_map/ppermute | solution.py:372
  1484.0 136.6 %collective-permute-start.15 = (bf16[688,400]{0,1:T(8,128)(2,1)}, bf16[688,400]{0,1:T(8,128)(2,1)}, u32[]{:S(2)}, u32[]{:S(2)}) collective-permute-start(bf16[688,400]{0,1:T(8,128)(2,1)} %copy.655), channel_id=1, source_target_pairs={{0,0},{1,1},{2,8},{3,9},{4,16},{5,17},{6,24},{7,25},{8,2},{9,3},{1... | collective-permute-start | bytes 1651208 | tf_op jit(solution)/shard_map/ppermute | solution.py:372
  1494.0 126.7 %copy-start.52 = (f32[2,688,400]{1,2,0:T(8,128)S(1)}, f32[2,688,400]{1,2,0:T(8,128)}, u32[]{:S(2)}) copy-start(f32[2,688,400]{1,2,0:T(8,128)} %param.37) | copy-start | bytes 6604804
  1618.7 12.0 collective-permute-start.5
  1620.7 10.6 collective-permute-start.6
  1779.2 16.4 collective-permute-start.12
  1781.2 15.0 collective-permute-start.13
  (135 other events, 684.7 us)
Sparse Core Ops, SparseCore 0:
  998.7 180.1 all-reduce.41
Sparse Core Ops, SparseCore 1:
  1005.4 58.2 reduce-scatter.21
  1067.9 78.2 reduce-scatter.15
  1149.6 117.8 reduce-scatter.23
  1272.0 98.5 reduce-scatter.27
  1374.6 107.2 reduce-scatter.25
  1485.8 131.8 reduce-scatter.17
  1621.3 156.5 reduce-scatter.19

commit v2 on v1

v2 whole, which is shorter than its diff:
```python
import functools

import jax
import jax.numpy as jnp
from jax import lax
from jax.experimental import pallas as pl
from jax.experimental.pallas import tpu as pltpu
from jax.sharding import PartitionSpec as P

NH = 25
KVH = 5
HD = 64
DI = 3200
DS = 16
DTR = 100
FF = 5504
META = 128
CONV = 4
WINDOW = 1024

norm_eps = 1e-05
beta_one = 0.9
beta_two = 0.95
learn_rate = 0.01
decay_rate = 0.1
adam_eps = 1e-08
adam_count = 10.0

FSDP = "fsdp"
CTX = "ctx"
EACH = "each"
ALL = "all"
GATHER = "gather"
REDUCE = "reduce"
HALF = "half"
WEIGHTS = "weights"
BOTH = "both"
CROSS = "cross"
PAIR = "pair"
NEXT = "next"
PREV = "prev"
BACK = "back"
LINE = "line"
SEQ = "seq"
SPREAD = "spread"
HIST = "hist"
STATE = "state"
RATE = "rate"
DRATE = "drate"
RING = "ring"
LOG2E = 1.4426950408889634
LN2 = 0.6931471805599453
FAR = 1e30
bf16 = jnp.bfloat16
f32 = jnp.float32
ANY = pl.BlockSpec(memory_space=pltpu.HBM)
MIB = 1024 * 1024


def together(*values):
    return lax.optimization_barrier(values)


def ceil_to(value, unit):
    return (value + unit - 1) // unit * unit


def span_of(axis):
    return lax.axis_size(axis), lax.axis_index(axis)


def ring_spot(ci, cs):
    odd = lax.rem(ci, 2)
    return (ci // 2) * (1 - odd) + (cs - 1 - ci // 2) * odd


def ring_block(spot, cs):
    spot = lax.rem(spot + 2 * cs, cs)
    far = spot // (cs // 2)
    return 2 * spot * (1 - far) + (2 * (cs - 1 - spot) + 1) * far


def when(condition, action):
    if condition is None:
        action()
    else:
        pl.when(condition)(action)


class Ring:
    def __init__(self, chunks, uses):
        self.chunks, self.uses = chunks, uses
        self.got, self.hop = [], 0

    def finish(self):
        block = lax.axis_index(CTX)
        sums = []
        for (k, part, _), got in zip(self.uses, self.got):
            own = lax.dynamic_index_in_dim(self.chunks[k], block, 0, keepdims=False)[part]
            sums.append(got.astype(f32) + own.astype(f32))
        return sums


class Traffic:
    def __init__(self, items, ring=None, hops=0, reach=0):
        self.items, self.ring, self.reach = items, ring, reach
        fs, cs = lax.axis_size(FSDP), lax.axis_size(CTX)
        self.hops = min(hops, cs - 1 - ring.hop) if ring is not None else 0
        self.ins = [value for value, _, _ in items]
        self.outs = []
        dma = pltpu.SemaphoreType.DMA
        most = 2 * max(fs, cs)
        count = max(len(items), 1)
        self.scratch = [dma((count, most)), dma((count, most)), dma((count, 2))]
        self.places = {}

        def own_scratch(k, shapes):
            self.places[k] = len(self.scratch)
            self.scratch += shapes

        for k, (value, mode, axis) in enumerate(items):
            shape = value.shape
            if mode in (ALL, GATHER, LINE):
                shape = (lax.axis_size(axis),) + shape
            elif mode in (NEXT, PREV):
                shape = (reach,) + shape
            elif mode == REDUCE:
                shape = (fs // 2,) + shape[1:]
                own_scratch(k, [pltpu.VMEM(shape, value.dtype)] * 2 + [dma((fs // 2,))])
            elif mode[0] == HALF:
                pieces = mode[2] - mode[1]
                shape = shape[:2] + (pieces,) + shape[3:]
                own_scratch(k, [dma((pieces, 2 * fs)), dma((pieces, 2 * fs))])
            self.outs.append(jax.ShapeDtypeStruct(shape, value.dtype))
        if self.hops:
            self.ins += list(ring.chunks) + list(ring.got)
            uses = len(ring.uses)
            shapes = [dma((uses, self.hops)), dma((uses, self.hops)), dma((uses, self.hops, 2))]
            for k, _, _ in ring.uses:
                shape = ring.chunks[k].shape[2:]
                self.outs += [jax.ShapeDtypeStruct(shape, bf16)] * self.hops
                shapes.append(pltpu.VMEM((self.hops, 2) + shape, bf16))
            own_scratch(RING, shapes)

    def vmem(self):
        total = 4 * MIB
        for held in self.scratch:
            if held.memory_space == pltpu.VMEM:
                size = 2
                for extent in held.shape[:-2]:
                    size *= extent
                total += size * ceil_to(held.shape[-2], 16) * ceil_to(held.shape[-1], 128)
        return total

    def bind(self, ins, outs, scratch):
        self.in_refs, self.out_refs, self.sems = ins, outs, scratch

    def remote(self, source, target, send, take, peer):
        return pltpu.make_async_remote_copy(
            src_ref=source,
            dst_ref=target,
            send_sem=send,
            recv_sem=take,
            device_id=peer,
            device_id_type=pl.DeviceIdType.MESH,
        )

    def greet(self):
        barrier = pltpu.get_barrier_semaphore()
        fs, fi = span_of(FSDP)
        cs, ci = span_of(CTX)

        def signal(peer):
            pl.semaphore_signal(
                barrier, inc=1, device_id=peer, device_id_type=pl.DeviceIdType.MESH
            )

        axes = {axis for _, _, axis in self.items}
        if WEIGHTS in axes:
            axes.add(FSDP)
        total = 0
        for axis in (FSDP, CTX):
            if axis in axes:
                n, me = span_of(axis)
                for d in range(1, n):
                    signal({axis: lax.rem(me + d, n)})
                total += n - 1
        if self.hops and CTX not in axes:
            spot = ring_spot(ci, cs)
            signal({CTX: ring_block(spot + 1, cs)})
            signal({CTX: ring_block(spot - 1, cs)})
            total += 2
        if WEIGHTS in axes and CTX not in axes:
            signal({CTX: ci + 1 - 2 * lax.rem(ci, 2)})
            total += 1
        if BOTH in axes:
            halves = cs // fs
            away = ci // halves != fi

            def meet():
                signal({FSDP: ci // halves, CTX: halves * fi + lax.rem(ci, halves)})

            pl.when(away)(meet)
            if total:
                pl.semaphore_wait(barrier, total + jnp.where(away, 1, 0))
            else:
                pl.when(away)(lambda: pl.semaphore_wait(barrier, 1))
        else:
            pl.semaphore_wait(barrier, total)

    def copies(self):
        starts, relays, waits = [], [], []
        fs, fi = span_of(FSDP)
        cs, ci = span_of(CTX)
        send_sem, take_sem, own_sem = self.sems[:3]
        for k, (_, mode, axis) in enumerate(self.items):
            src, dst = self.in_refs[k], self.out_refs[k]

            def add(copy, sends=None, takes=None):
                starts.append((copy.start, sends))
                waits.append((copy.wait_send, sends))
                waits.append((copy.wait_recv, takes))

            def keep(copy, condition=None):
                starts.append((copy.start, condition))
                waits.append((copy.wait, condition))

            core, chip, chips = lax.rem(fi, 2), fi // 2, fs // 2
            mate = {FSDP: fi + 1 - 2 * core}

            def relay(first, second):
                starts.append((first.start, None))
                relays.append((first.wait_recv, None))
                relays.append((second.start, None))
                waits.append((first.wait_send, None))
                waits.append((second.wait_send, None))
                waits.append((second.wait_recv, None))

            if mode == GATHER:
                for d in range(1, chips):
                    to = 2 * lax.rem(chip + d, chips) + core
                    came = 2 * lax.rem(chip + chips - d, chips) + core
                    relay(
                        self.remote(
                            src, dst.at[fi], send_sem.at[k, d], take_sem.at[k, d], {FSDP: to}
                        ),
                        self.remote(
                            dst.at[came],
                            dst.at[came],
                            send_sem.at[k, chips + d],
                            take_sem.at[k, chips + d],
                            mate,
                        ),
                    )
                add(self.remote(src, dst.at[fi], send_sem.at[k, 0], take_sem.at[k, 0], mate))
                keep(pltpu.make_async_copy(src, dst.at[fi], own_sem.at[k, 0]))
            elif mode == LINE:
                across = {CTX: ci + 1 - 2 * lax.rem(ci, 2)}
                for d in range(1, cs // 2):
                    came = lax.rem(ci + cs - 2 * d, cs)
                    relay(
                        self.remote(
                            src,
                            dst.at[ci],
                            send_sem.at[k, d],
                            take_sem.at[k, d],
                            {CTX: lax.rem(ci + 2 * d, cs)},
                        ),
                        self.remote(
                            dst.at[came],
                            dst.at[came],
                            send_sem.at[k, cs // 2 + d],
                            take_sem.at[k, cs // 2 + d],
                            across,
                        ),
                    )
                add(self.remote(src, dst.at[ci], send_sem.at[k, 0], take_sem.at[k, 0], across))
                keep(pltpu.make_async_copy(src, dst.at[ci], own_sem.at[k, 0]))
            elif mode == REDUCE:
                mine, other, load_sem = self.sems[self.places[k] : self.places[k] + 3]
                for d in list(range(1, chips)) + [0]:
                    to = lax.rem(chip + d, chips)
                    first = self.remote(
                        src.at[2 * to + 1 - core],
                        other.at[to],
                        send_sem.at[k, d],
                        take_sem.at[k, d],
                        mate,
                    )
                    load = pltpu.make_async_copy(
                        src.at[2 * to + core], mine.at[to], load_sem.at[d]
                    )
                    starts.append((first.start, None))
                    starts.append((load.start, None))
                    relays.append((load.wait, None))
                    relays.append((first.wait_recv, None))
                    waits.append((first.wait_send, None))

                    def total(mine=mine, other=other, to=to):
                        mine[to] = mine[to] + other[to]

                    relays.append((total, None))
                    if d:
                        second = self.remote(
                            mine.at[to],
                            dst.at[chip],
                            send_sem.at[k, chips + d],
                            take_sem.at[k, chips + d],
                            {FSDP: 2 * to + core},
                        )
                        waits.append((second.wait_send, None))
                        waits.append((second.wait_recv, None))
                    else:
                        second = pltpu.make_async_copy(mine.at[to], dst.at[to], own_sem.at[k, 0])
                        waits.append((second.wait, None))
                    relays.append((second.start, None))
            elif mode[0] == HALF:
                piece_send, piece_take = self.sems[self.places[k] : self.places[k] + 2]
                side = lax.rem(ci, 2)
                across = {CTX: ci + 1 - 2 * side}
                for q in range(mode[2] - mode[1]):
                    for d in range(1, chips):
                        for b in range(2):
                            to = 2 * lax.rem(chip + d, chips) + lax.rem(core + b, 2)
                            came = 2 * lax.rem(chip + chips - d, chips) + lax.rem(core + b, 2)
                            e = 2 * d + b
                            relay(
                                self.remote(
                                    src.at[to, side, mode[1] + q],
                                    dst.at[fi, side, q],
                                    piece_send.at[q, e],
                                    piece_take.at[q, e],
                                    {FSDP: to},
                                ),
                                self.remote(
                                    dst.at[came, side, q],
                                    dst.at[came, side, q],
                                    piece_send.at[q, fs + e],
                                    piece_take.at[q, fs + e],
                                    across,
                                ),
                            )
                for b in range(2):
                    to = mate[FSDP]
                    add(
                        self.remote(
                            src.at[to, b, mode[1] : mode[2]],
                            dst.at[fi, b],
                            send_sem.at[k, b],
                            take_sem.at[k, b],
                            mate,
                        )
                    )
                    keep(
                        pltpu.make_async_copy(
                            src.at[fi, b, mode[1] : mode[2]], dst.at[fi, b], own_sem.at[k, b]
                        )
                    )
            elif mode in (ALL, EACH):
                n, me = span_of(axis)
                for d in range(1, n):
                    peer = lax.rem(me + d, n)
                    source = src.at[peer] if mode == EACH else src
                    add(
                        self.remote(
                            source, dst.at[me], send_sem.at[k, d], take_sem.at[k, d], {axis: peer}
                        )
                    )
                source = src.at[me] if mode == EACH else src
                keep(pltpu.make_async_copy(source, dst.at[me], own_sem.at[k, 0]))
            elif mode == PAIR:
                for p in range(2):
                    peer = (p * fs + fi) // 2
                    slot = lax.rem(fi, 2)
                    away = peer != fi
                    q = 2 * fi + p
                    comes = lax.rem(q, fs) != fi
                    copy = self.remote(
                        src.at[p],
                        dst.at[slot],
                        send_sem.at[k, p],
                        take_sem.at[k, slot],
                        {FSDP: peer},
                    )
                    starts.append((copy.start, away))
                    waits.append((copy.wait_send, away))
                    taken = self.remote(
                        src.at[p], dst.at[p], send_sem.at[k, p], take_sem.at[k, p], {FSDP: peer}
                    )
                    waits.append((taken.wait_recv, comes))
                    keep(
                        pltpu.make_async_copy(src.at[p], dst.at[slot], own_sem.at[k, p]),
                        peer == fi,
                    )
            elif mode == CROSS:
                halves = cs // fs
                away = ci // halves != fi
                peer = {FSDP: ci // halves, CTX: halves * fi + lax.rem(ci, halves)}
                add(self.remote(src, dst, send_sem.at[k, 0], take_sem.at[k, 0], peer), away, away)
                keep(pltpu.make_async_copy(src, dst, own_sem.at[k, 0]), ci // halves == fi)
            else:
                for d in range(1, self.reach + 1):
                    up = mode == NEXT
                    peer = ci + d if up else ci - d
                    source = src.at[d - 1] if mode == BACK else src
                    add(
                        self.remote(
                            source,
                            dst.at[d - 1],
                            send_sem.at[k, d],
                            take_sem.at[k, d],
                            {CTX: lax.rem(peer + cs, cs)},
                        ),
                        peer < cs if up else peer >= 0,
                        ci - d >= 0 if up else ci + d < cs,
                    )
        return starts, relays, waits

    def ring_refs(self, u):
        base = self.places[RING]
        outs = self.out_refs[len(self.items) + u * self.hops :]
        return self.sems[base], self.sems[base + 1], self.sems[base + 2], self.sems[base + 3 + u], outs

    def hop_copy(self, u, t):
        cs, ci = span_of(CTX)
        spot = ring_spot(ci, cs)
        k, part, way = self.ring.uses[u]
        send, take, _, buffer, outs = self.ring_refs(u)
        if self.ring.hop + t == 0:
            source = self.in_refs[len(self.items) + k].at[ring_block(spot - way, cs), part]
        else:
            source = buffer.at[t, 1]
        return self.remote(
            source, outs[t], send.at[u, t], take.at[u, t], {CTX: ring_block(spot + way, cs)}
        )

    def load_own(self, u, t):
        cs, ci = span_of(CTX)
        k, part, way = self.ring.uses[u]
        _, _, load, buffer, _ = self.ring_refs(u)
        block = ring_block(ring_spot(ci, cs) - way * (self.ring.hop + t + 1), cs)
        return pltpu.make_async_copy(
            self.in_refs[len(self.items) + k].at[block, part], buffer.at[t, 1], load.at[u, t, 1]
        )

    def load_got(self, u, t):
        _, _, load, buffer, outs = self.ring_refs(u)
        if t == 0:
            source = self.in_refs[len(self.items) + len(self.ring.chunks) + u]
        else:
            source = outs[t - 1]
        return pltpu.make_async_copy(source, buffer.at[t, 0], load.at[u, t, 0])

    def hop_step(self, t):
        uses = range(len(self.ring.uses))
        if self.ring.hop + t > 0:
            for u in uses:
                self.load_own(u, t).start()
                if t > 0:
                    self.hop_copy(u, t - 1).wait_recv()
                self.load_got(u, t).start()
        for u in uses:
            if self.ring.hop + t > 0:
                self.load_own(u, t).wait()
                self.load_got(u, t).wait()
                buffer = self.ring_refs(u)[3]
                buffer[t, 1] = buffer[t, 0] + buffer[t, 1]
            self.hop_copy(u, t).start()

    def begin(self):
        self.greet()
        for start, condition in self.copies()[0]:
            when(condition, start)
        if self.hops:
            self.hop_step(0)

    def end(self, hopped=1):
        _, relays, waits = self.copies()
        for step, condition in relays:
            when(condition, step)
        for t in range(hopped, self.hops):
            self.hop_step(t)
        for wait, condition in waits:
            when(condition, wait)
        for u in range(len(self.ring.uses) if self.hops else 0):
            for t in range(self.hops):
                self.hop_copy(u, t).wait_send()
            self.hop_copy(u, self.hops - 1).wait_recv()

    def take(self, results):
        count = len(self.items)
        if self.hops:
            last = count + self.hops - 1
            self.ring.got = [results[last + u * self.hops] for u in range(len(self.ring.uses))]
            self.ring.hop += self.hops
        return tuple(results[:count])


def exchange(cid, items, ring=None, hops=0, reach=0):
    plan = Traffic(items, ring, hops, reach)
    ins, outs = len(plan.ins), len(plan.outs)

    def body(*refs):
        plan.bind(refs[:ins], refs[ins : ins + outs], refs[ins + outs :])
        plan.begin()
        plan.end()

    results = pl.pallas_call(
        body,
        out_shape=tuple(plan.outs),
        in_specs=[ANY] * ins,
        out_specs=(ANY,) * outs,
        scratch_shapes=plan.scratch,
        compiler_params=pltpu.CompilerParams(
            collective_id=cid, has_side_effects=True, vmem_limit_bytes=plan.vmem() + 4 * MIB
        ),
    )(*plan.ins)
    return plan.take(results)


def scan_tail_body(rows, length, step_ref, u_ref, b_ref, rate_ref, last_ref):
    rate = rate_ref[...]

    def advance(i, states):
        new = []
        for r in range(rows):
            keep = jnp.exp2(step_ref[r, pl.ds(i, 1), :] * rate)
            new.append(keep * states[r] + u_ref[r, pl.ds(i, 1), :] * b_ref[r, i])
        return tuple(new)

    start = tuple(jnp.zeros((DS, 128), f32) for _ in range(rows))
    end = lax.fori_loop(0, length, advance, start, unroll=4)
    for r in range(rows):
        last_ref[r] = end[r]


def scan_full_body(
    rows, length, step_ref, u_ref, b_ref, c_ref, rate_ref, entry_ref, read_ref, hist_ref
):
    rate = rate_ref[...]

    def advance(i, states):
        new = []
        for r in range(rows):
            hist_ref[r, i] = states[r]
            keep = jnp.exp2(step_ref[r, pl.ds(i, 1), :] * rate)
            h = keep * states[r] + u_ref[r, pl.ds(i, 1), :] * b_ref[r, i]
            read_ref[r, pl.ds(i, 1), :] = jnp.sum(h * c_ref[r, i], axis=0, keepdims=True)
            new.append(h)
        return tuple(new)

    lax.fori_loop(0, length, advance, tuple(entry_ref[r] for r in range(rows)), unroll=4)


def adjoint_head_body(rows, length, step_ref, dy_ref, c_ref, rate_ref, first_ref):
    rate = rate_ref[...]

    def advance(k, carried):
        i = length - 1 - k
        new = []
        for r in range(rows):
            keep = jnp.exp2(step_ref[r, pl.ds(i, 1), :] * rate)
            new.append(keep * (carried[r] + dy_ref[r, pl.ds(i, 1), :] * c_ref[r, i]))
        return tuple(new)

    start = tuple(jnp.zeros((DS, 128), f32) for _ in range(rows))
    end = lax.fori_loop(0, length, advance, start, unroll=4)
    for r in range(rows):
        first_ref[r] = end[r]


def adjoint_full_body(
    rows,
    length,
    step_ref,
    u_ref,
    dy_ref,
    b_ref,
    c_ref,
    rate_ref,
    hist_ref,
    later_ref,
    du_ref,
    dexp_ref,
    db_ref,
    dc_ref,
    drate_ref,
):
    rate = rate_ref[...]

    @pl.when(pl.program_id(1) == 0)
    def _():
        db_ref[...] = jnp.zeros_like(db_ref)
        dc_ref[...] = jnp.zeros_like(dc_ref)

    def advance(k, carried):
        i = length - 1 - k
        new = []
        drate = carried[rows]
        for r in range(rows):
            step = step_ref[r, pl.ds(i, 1), :]
            u = u_ref[r, pl.ds(i, 1), :]
            dy = dy_ref[r, pl.ds(i, 1), :]
            keep = jnp.exp2(step * rate)
            b = b_ref[r, i]
            kept = keep * hist_ref[r, i]
            g = carried[r] + dy * c_ref[r, i]
            w = g * kept
            dc_ref[r, i] += (kept + u * b) * dy
            db_ref[r, i] += g * u
            du_ref[r, pl.ds(i, 1), :] = jnp.sum(g * b, axis=0, keepdims=True)
            dexp_ref[r, pl.ds(i, 1), :] = jnp.sum(w * rate, axis=0, keepdims=True)
            drate = drate + w * step
            new.append(keep * g)
        return tuple(new) + (drate,)

    start = tuple(later_ref[r] for r in range(rows)) + (jnp.zeros((DS, 128), f32),)
    end = lax.fori_loop(0, length, advance, start, unroll=2)
    drate_ref[0] = end[rows]


def hosted_call(body, grid, in_specs, out_specs, out_shape, args, cid, plan, own_vmem, later=()):
    steps = 1
    for size in grid:
        steps *= size
    n_in, n_out, x_in, x_out = len(args), len(out_shape), len(plan.ins), len(plan.outs)

    def hosted(*refs):
        mine_in, refs = refs[:n_in], refs[n_in:]
        plan_in, refs = refs[:x_in], refs[x_in:]
        mine_out, refs = refs[:n_out], refs[n_out:]
        plan.bind(plan_in, refs[:x_out], refs[x_out:])
        at = pl.program_id(0)
        for k in range(1, len(grid)):
            at = at * grid[k] + pl.program_id(k)
        pl.when(at == 0)(plan.begin)
        for t in range(1, min(plan.hops, len(later) + 1)):
            pl.when(at == later[t - 1])(functools.partial(plan.hop_step, t))
        body(*mine_in, *mine_out)
        pl.when(at == steps - 1)(functools.partial(plan.end, 1 + len(later)))

    results = pl.pallas_call(
        hosted,
        grid=grid,
        in_specs=in_specs + [ANY] * x_in,
        out_specs=tuple(out_specs) + (ANY,) * x_out,
        out_shape=tuple(out_shape) + tuple(plan.outs),
        scratch_shapes=plan.scratch,
        compiler_params=pltpu.CompilerParams(
            vmem_limit_bytes=plan.vmem() + own_vmem, collective_id=cid, has_side_effects=True
        ),
    )(*args, *plan.ins)
    return tuple(results[:n_out]) + plan.take(results[n_out:])


def scan_call(body, args, kinds, outs, rows_all, length, width, cid, plan, later=()):
    rows = 4 if rows_all % 4 == 0 else rows_all
    single = pl.Buffered(buffer_count=1)
    grid = (rows_all // rows, width // 128)

    def spec(kind):
        extra = {"pipeline_mode": single} if kind == SPREAD else {}
        if kind == SEQ:
            return pl.BlockSpec((rows, length, 128), lambda r, g: (r, 0, g), **extra)
        if kind == SPREAD:
            return pl.BlockSpec((rows, length, DS, 128), lambda r, g: (r, 0, 0, 0), **extra)
        if kind == HIST:
            return pl.BlockSpec((rows, length, DS, 128), lambda r, g: (r, 0, 0, g), **extra)
        if kind == STATE:
            return pl.BlockSpec((rows, DS, 128), lambda r, g: (r, 0, g), **extra)
        if kind == RATE:
            return pl.BlockSpec((DS, 128), lambda r, g: (0, g), **extra)
        return pl.BlockSpec((1, DS, 128), lambda r, g: (r, 0, g), **extra)

    def block_bytes(kind):
        wide = rows * length * 128 * 4
        return {SEQ: 2 * wide, SPREAD: DS * wide, HIST: 2 * DS * wide}.get(kind, MIB // 2)

    shape_of = {
        SEQ: (rows_all, length, width),
        SPREAD: (rows_all, length, DS, 128),
        HIST: (rows_all, length, DS, width),
        STATE: (rows_all, DS, width),
        DRATE: (rows_all // rows, DS, width),
    }
    return hosted_call(
        functools.partial(body, rows, length),
        grid,
        [spec(k) for k in kinds],
        [spec(k) for k in outs],
        [jax.ShapeDtypeStruct(shape_of[k], f32) for k in outs],
        args,
        cid,
        plan,
        8 * MIB + sum(block_bytes(k) for k in tuple(kinds) + tuple(outs)),
        later,
    )


def attend_body(heads, q_ref, k_ref, v_ref, bias_ref, out_ref, total_ref):
    keys = k_ref[...].T
    for h in range(heads):
        rows = slice(h * HD, (h + 1) * HD)
        scores = jnp.dot(keys, q_ref[rows], preferred_element_type=f32)
        scores = scores * HD**-0.5 + bias_ref[...]
        peak = jnp.max(scores, axis=0, keepdims=True)
        grown = jnp.exp(scores - peak)
        total = jnp.sum(grown, axis=0, keepdims=True)
        probs = (grown * (1.0 / total)).astype(bf16)
        out_ref[rows] = jnp.dot(v_ref[...], probs, preferred_element_type=f32).astype(bf16)
        total_ref[0, h : h + 1] = peak + jnp.log(total)


def attend_back_body(
    heads, q_ref, k_ref, v_ref, bias_ref, total_ref, grad_ref, dq_ref, dk_ref, dv_ref
):
    keys = k_ref[...].T
    values = v_ref[...].T
    for h in range(heads):
        rows = slice(h * HD, (h + 1) * HD)
        scores = jnp.dot(keys, q_ref[rows], preferred_element_type=f32)
        probs = jnp.exp(scores * HD**-0.5 + bias_ref[...] - total_ref[0, h : h + 1])
        grad = jnp.dot(values, grad_ref[rows], preferred_element_type=f32)
        mean = jnp.sum(probs * grad, axis=0, keepdims=True)
        low = (probs * (grad - mean)).astype(bf16)
        dq = jnp.dot(k_ref[...], low, preferred_element_type=f32)
        dq_ref[rows] = (dq * HD**-0.5).astype(bf16)
        dk = dense_nt(q_ref[rows], low) * HD**-0.5
        dv = dense_nt(grad_ref[rows], probs.astype(bf16))
        if h == 0:
            dk_ref[...] = dk
            dv_ref[...] = dv
        else:
            dk_ref[...] += dk
            dv_ref[...] += dv


def rms_norm(values, gain_row):
    return (
        values * lax.rsqrt(jnp.mean(values * values, axis=-1, keepdims=True) + norm_eps) * gain_row
    )


def dense(operand, partner):
    return jnp.dot(operand, partner, preferred_element_type=f32)


def dense_tn(operand, partner):
    return lax.dot_general(
        operand, partner, (((0,), (0,)), ((), ())), preferred_element_type=f32
    )


def dense_nt(operand, partner):
    return lax.dot_general(
        operand, partner, (((1,), (1,)), ((), ())), preferred_element_type=f32
    )


def conv_silu(extended, conv_taps, same_seg):
    length_out = extended.shape[1] - CONV + 1
    summed = jnp.zeros((extended.shape[0], length_out, extended.shape[2]), f32)
    for offset in range(CONV):
        summed = summed + jnp.where(
            same_seg[offset][:, :, None],
            extended[:, offset : offset + length_out] * conv_taps[offset],
            0.0,
        )
    return jax.nn.silu(summed)


def adam_step(gradient, moments_old, weight_now):
    first_moment = beta_one * moments_old[0] + (1.0 - beta_one) * gradient
    second_moment = beta_two * moments_old[1] + (1.0 - beta_two) * gradient * gradient
    corrected = (
        first_moment
        / (1.0 - beta_one**adam_count)
        / (jnp.sqrt(second_moment / (1.0 - beta_two**adam_count)) + adam_eps)
    )
    return (second_moment, -learn_rate * (corrected + decay_rate * weight_now))


def pad_last(values, width):
    return jnp.pad(values, [(0, 0)] * (values.ndim - 1) + [(0, width - values.shape[-1])])


def column_parts(weight, parts, shards_of, width):
    own = weight.shape[1] // parts // shards_of
    return jnp.stack(
        [
            jnp.concatenate(
                [
                    pad_last(weight[:, (p * shards_of + j) * own : (p * shards_of + j + 1) * own], width)
                    for p in range(parts)
                ],
                axis=1,
            )
            for j in range(shards_of)
        ]
    )


def shards(
    tokens,
    cotangent,
    segments,
    w_qkv,
    m_qkv,
    w_attn_out,
    m_attn_out,
    w_mamba_in,
    m_mamba_in,
    w_ssm_proj,
    m_ssm_proj,
    w_mamba_out,
    m_mamba_out,
    w_gate_up,
    m_gate_up,
    w_ffn_down,
    m_ffn_down,
    ssm_vec,
    m_ssm_vec,
    embed_small,
    m_embed_small,
):
    fs, cs = lax.axis_size(FSDP), lax.axis_size(CTX)
    fi, ci = lax.axis_index(FSDP), lax.axis_index(CTX)
    tok = tokens.shape[1]
    dim = tokens.shape[2]
    row_len = segments.shape[1]
    halves = cs // fs
    reach = min(row_len // 2, WINDOW) // tok
    metas = META // cs
    chan = DI // fs
    chan_p = ceil_to(chan, 128)
    ffw = FF // fs
    ffw_p = ceil_to(ffw, 128)
    heads_dim = NH * HD
    kv_dim = KVH * HD
    groups = NH // KVH
    scale_factor = HD ** (-0.5)
    xdim = DTR + 2 * DS
    both = (FSDP, CTX)

    def row_block(weight):
        rows, cols = weight.shape[0] // halves, weight.shape[1] // fs
        return lax.dynamic_slice(
            weight, ((ci % halves) * rows, (ci // halves) * cols), (rows, cols)
        )

    def unpaired(value, width):
        return jnp.concatenate([value[0][:, :width], value[1][:, :width]], axis=1).astype(f32)

    def spread_hops(weights):
        total, done, out = sum(weights), 0, []
        for k in range(len(weights)):
            upto = (cs - 1) * sum(weights[: k + 1]) // total
            out.append(upto - done)
            done = upto
        return out

    def row_chunks(operand, partner):
        grad = dense_tn(operand, partner).astype(bf16)
        return grad.reshape(cs, 1, grad.shape[0] // cs, grad.shape[1])

    def column_chunks(operand, partner, parts=1):
        cols = partner.shape[1] // fs
        pieces = jnp.stack([partner[:, j * cols : (j + 1) * cols] for j in range(fs)])
        grad = jnp.einsum("tr,jtn->jrn", operand, pieces, preferred_element_type=f32)
        return grad.astype(bf16).reshape(cs, parts, operand.shape[1] // halves // parts, cols)

    def in_blocks(value):
        return value.reshape(fs, 2, 5, value.shape[1] // 10, value.shape[2])

    mi_send = column_parts(w_mamba_in, 2, fs, chan_p)
    qkv_send = column_parts(w_qkv, 1, fs, w_qkv.shape[1] // fs)
    gain_rows = embed_small[META:]
    meta_rows = lax.dynamic_slice_in_dim(embed_small, ci * metas, metas, 0)
    source = tokens[0].astype(f32)
    normed_f, norm_pull = jax.vjp(rms_norm, source, gain_rows[0])
    normed = normed_f.astype(bf16)
    meta_f, meta_pull = jax.vjp(rms_norm, meta_rows, gain_rows[0])
    meta_low = meta_f.astype(bf16)

    blocks = 5
    normed_all, seg_all, mi_w, qkv_w = exchange(
        0,
        [
            (normed, GATHER, FSDP),
            (segments, ALL, FSDP),
            (in_blocks(mi_send), (HALF, 0, blocks), WEIGHTS),
            (in_blocks(qkv_send), (HALF, 0, blocks), WEIGHTS),
        ],
    )
    gu_send = in_blocks(column_parts(w_gate_up, 2, fs, ffw_p))
    mi_w = mi_w.reshape(dim, 2 * chan_p)
    qkv_w = qkv_w.reshape(dim, -1)
    seg_all = seg_all.reshape(fs, row_len)
    seg_row = segments[0]
    normed_all = normed_all.reshape(fs * tok, dim)
    xp_w = jnp.pad(w_ssm_proj[:, :xdim], ((0, chan_p - chan), (0, 0)))
    dt_w = jnp.pad(w_ssm_proj[:, xdim:], ((0, chan_p - chan), (0, 0)))
    mo_w = jnp.pad(w_mamba_out, ((0, chan_p - chan), (0, 0)))
    vec = pad_last(lax.dynamic_slice_in_dim(ssm_vec, fi * chan, chan, 1), chan_p)

    normed_rows = normed_all.reshape(fs, tok, dim)
    qkv_parts = jnp.einsum("ftd,dc->fct", normed_rows, qkv_w, preferred_element_type=f32)
    meta_part = jnp.broadcast_to(
        dense(meta_low, qkv_w).astype(bf16)[None], (fs, metas, qkv_w.shape[1])
    )
    qkv_got, meta_got = exchange(
        1, [(qkv_parts.astype(bf16), EACH, FSDP), (meta_part, EACH, FSDP)]
    )
    qkv_own = qkv_got.reshape(heads_dim + 2 * kv_dim, tok)
    queries = qkv_own[:heads_dim]
    keyval = qkv_own[heads_dim:]
    meta_own = jnp.concatenate([meta_got[j] for j in range(fs)], axis=1)[:, heads_dim:]
    kv_before, meta_kv, gu_0 = exchange(
        2,
        [
            (keyval, NEXT, CTX),
            (meta_own, ALL, CTX),
            (gu_send, (HALF, 0, 1), WEIGHTS),
        ],
        reach=reach,
    )
    kv_before = jnp.where(
        (ci - 1 - jnp.arange(reach) >= 0)[:, None, None], kv_before, jnp.zeros_like(kv_before)
    )
    key_rows = jnp.concatenate(
        [meta_kv.reshape(META, 2 * kv_dim).T]
        + [kv_before[d - 1] for d in range(reach, 0, -1)]
        + [keyval],
        axis=1,
    )

    mamba_in = dense(normed_all, mi_w).reshape(fs, tok, 2 * chan_p)
    inner_pre = mamba_in[:, :, :chan_p]
    gate_z = mamba_in[:, :, chan_p:]
    up_ring = [(c, c + 1) for c in range(cs - 1)]
    down_ring = [(c + 1, c) for c in range(cs - 1)]
    tail_rows = lax.ppermute(inner_pre[:, tok - (CONV - 1) :], CTX, up_ring)
    extended = jnp.concatenate([tail_rows, inner_pre], axis=1)
    seg_ext = lax.dynamic_slice_in_dim(
        jnp.concatenate([jnp.full((fs, CONV - 1), -1, jnp.int32), seg_all], axis=1),
        ci * tok,
        tok + CONV - 1,
        1,
    )
    own_seg = seg_ext[:, CONV - 1 :]
    same_seg = [seg_ext[:, o : o + tok] == own_seg for o in range(CONV)]
    starts = own_seg != seg_ext[:, CONV - 2 : -1]
    inner_x, conv_pull = jax.vjp(
        lambda ext_rows, taps: conv_silu(ext_rows, taps, same_seg), extended, vec[:CONV]
    )
    inner_low = inner_x.astype(bf16).reshape(fs * tok, chan_p)
    xproj_part = lax.dot_general(
        xp_w, inner_low, (((0,), (1,)), ((), ())), preferred_element_type=f32
    )
    xproj_got, attn_old, ssm_proj_old = exchange(
        3,
        [
            (xproj_part, GATHER, FSDP),
            (row_block(w_attn_out), CROSS, BOTH),
            (row_block(w_ssm_proj), CROSS, BOTH),
        ],
    )
    xproj = jnp.sum(xproj_got, axis=0).T
    delta_low = xproj[:, :DTR].astype(bf16)
    pre_delta = dense_nt(delta_low, dt_w).reshape(fs, tok, chan_p) + vec[CONV]
    step = jax.nn.softplus(pre_delta)
    step_far = jnp.where(starts[:, :, None], FAR, step)
    drive = step * inner_x

    def spread(columns):
        return jnp.broadcast_to(columns.reshape(fs, tok, DS, 1), (fs, tok, DS, 128))

    b_wide = spread(xproj[:, DTR : DTR + DS])
    c_wide = spread(xproj[:, DTR + DS : xdim])
    rate = -jnp.exp(vec[CONV + 2 :])
    rate2 = rate * LOG2E
    sizes = (fs, tok, chan_p)
    last_state, mamba_out_old = scan_call(
        scan_tail_body,
        (step_far, drive, b_wide, rate2),
        (SEQ, SEQ, SPREAD, RATE),
        (STATE,),
        *sizes,
        cid=19,
        plan=Traffic([(row_block(w_mamba_out), CROSS, BOTH)]),
    )
    step_sum = jnp.sum(step_far, axis=1)
    state_before, sums, gu_2 = exchange(
        4,
        [
            (last_state.astype(bf16), NEXT, CTX),
            (step_sum, ALL, CTX),
            (gu_send, (HALF, 2, 4), WEIGHTS),
        ],
        reach=reach,
    )

    def decay_of(block):
        total = lax.dynamic_index_in_dim(sums, jnp.clip(block, 0, cs - 1), 0, keepdims=False)
        return jnp.exp2(total[:, None, :] * rate2)

    entry = jnp.zeros((fs, DS, chan_p), f32)
    for d in range(reach, 0, -1):
        there = jnp.where(ci >= d, state_before[d - 1].astype(f32), 0.0)
        entry = decay_of(ci - d) * entry + there
    readout, hist, ffn_down_old = scan_call(
        scan_full_body,
        (step_far, drive, b_wide, c_wide, rate2, entry),
        (SEQ, SEQ, SPREAD, SPREAD, RATE, STATE),
        (SEQ, HIST),
        *sizes,
        cid=20,
        plan=Traffic([(row_block(w_ffn_down), CROSS, BOTH)]),
    )
    skip = vec[CONV + 1]
    pre_mix = readout + skip * inner_x
    gate_s = jax.nn.sigmoid(gate_z)
    gate_silu = gate_z * gate_s
    mixture_low = (pre_mix * gate_silu).astype(bf16).reshape(fs * tok, chan_p)
    ssm_part = dense(mixture_low, mo_w).astype(bf16).reshape(fs, tok, dim)

    key_span = (reach + 1) * tok
    padded_seg = jnp.concatenate([jnp.full((reach * tok,), -1, jnp.int32), seg_row])
    key_seg = lax.dynamic_slice_in_dim(padded_seg, ci * tok, key_span, 0)
    query_seg = lax.dynamic_slice_in_dim(seg_row, ci * tok, tok, 0)
    query_pos = jnp.arange(tok, dtype=jnp.int32) + reach * tok
    key_pos = jnp.arange(key_span, dtype=jnp.int32)
    allowed = (
        (key_seg[:, None] == query_seg[None, :])
        & (key_pos[:, None] <= query_pos[None, :])
        & (query_pos[None, :] - key_pos[:, None] < WINDOW)
    )
    allowed = jnp.concatenate([jnp.ones((META, tok), jnp.bool_), allowed], axis=0)
    bias = jnp.where(allowed, 0.0, -1e30)
    seen = META + key_span
    q_spec = pl.BlockSpec((groups * HD, tok), lambda g: (g, 0))
    k_spec = pl.BlockSpec((HD, seen), lambda g: (g, 0))
    v_spec = pl.BlockSpec((HD, seen), lambda g: (g + KVH, 0))
    bias_spec = pl.BlockSpec((seen, tok), lambda g: (0, 0))
    total_spec = pl.BlockSpec((1, groups, tok), lambda g: (g, 0, 0))
    attended, log_totals, gu_1 = hosted_call(
        functools.partial(attend_body, groups),
        (KVH,),
        [q_spec, k_spec, v_spec, bias_spec],
        [q_spec, total_spec],
        [
            jax.ShapeDtypeStruct((heads_dim, tok), bf16),
            jax.ShapeDtypeStruct((KVH, groups, tok), f32),
        ],
        (queries, key_rows, key_rows, bias),
        16,
        Traffic([(gu_send, (HALF, 1, 2), WEIGHTS)]),
        12 * MIB,
    )
    wide = heads_dim // fs
    att_got, gu_3 = exchange(
        5,
        [
            (attended.reshape(fs, wide, tok), EACH, FSDP),
            (gu_send, (HALF, 4, 5), WEIGHTS),
        ],
    )
    gu_w = jnp.concatenate([gu_0, gu_1, gu_2, gu_3], axis=2).reshape(dim, 2 * ffw_p)
    att_tp = jnp.swapaxes(att_got, 1, 2).reshape(fs * tok, wide)
    attn_part = dense(att_tp, w_attn_out).astype(bf16).reshape(fs, tok, dim)
    attn_got, ssm_got = exchange(
        6, [(attn_part, REDUCE, FSDP), (ssm_part, REDUCE, FSDP)]
    )
    attn_proj = jnp.sum(attn_got.astype(f32), axis=0)
    ssm_proj = jnp.sum(ssm_got.astype(f32), axis=0)
    attn_branch, attn_pull = jax.vjp(rms_norm, attn_proj, gain_rows[1])
    ssm_branch, ssm_norm_pull = jax.vjp(rms_norm, ssm_proj, gain_rows[2])
    residual = source + 0.5 * (attn_branch + ssm_branch)
    ffn_in_f, ffn_norm_pull = jax.vjp(rms_norm, residual, gain_rows[3])
    ffn_in, cot_all = exchange(
        7, [(ffn_in_f.astype(bf16), GATHER, FSDP), (cotangent[0], GATHER, FSDP)]
    )
    cot_all = cot_all.reshape(fs * tok, dim)
    ffn_in = ffn_in.reshape(fs * tok, dim)

    gate_up = dense(ffn_in, gu_w)
    hidden_f, glu_pull = jax.vjp(
        lambda values: jax.nn.silu(values[:, :ffw_p]) * values[:, ffw_p:], gate_up
    )
    hidden = hidden_f.astype(bf16)[:, :ffw]
    down_part = dense(hidden, w_ffn_down).astype(bf16).reshape(fs, tok, dim)
    hidden_grad = pad_last(dense_nt(cot_all, w_ffn_down), ffw_p)
    gate_up_grad = glu_pull(hidden_grad)[0].astype(bf16)
    ring_one = Ring(
        [
            row_chunks(ffn_in, gate_up_grad[:, :ffw_p]),
            row_chunks(ffn_in, gate_up_grad[:, ffw_p:]),
            column_chunks(hidden, cot_all, 2),
        ],
        [(0, 0, 1), (1, 0, -1), (2, 0, 1), (2, 1, -1)],
    )
    hops = spread_hops([1, 1, 1, 1, 2, 1])
    ffn_back = dense_nt(gate_up_grad, gu_w).astype(bf16).reshape(fs, tok, dim)
    (back_got,) = exchange(8, [(ffn_back, REDUCE, FSDP)], ring_one, hops[0])
    resid_part, gain_ffn_grad = ffn_norm_pull(jnp.sum(back_got.astype(f32), axis=0))
    residual_grad = cotangent[0].astype(f32) + resid_part
    branch_grad = 0.5 * residual_grad
    attn_proj_grad, gain_attn_grad = attn_pull(branch_grad)
    ssm_proj_grad, gain_ssm_grad = ssm_norm_pull(branch_grad)
    branch_low = (attn_proj_grad.astype(bf16), ssm_proj_grad.astype(bf16))
    attn_proj_low, ssm_proj_low = exchange(
        9,
        [(branch_low[0], GATHER, FSDP), (branch_low[1], GATHER, FSDP)],
        ring_one,
        hops[1],
    )
    attn_proj_low = attn_proj_low.reshape(fs * tok, dim)
    ssm_proj_low = ssm_proj_low.reshape(fs * tok, dim)
    att_grad_tp = jnp.einsum(
        "ftd,cd->fct",
        attn_proj_low.reshape(fs, tok, dim),
        w_attn_out,
        preferred_element_type=f32,
    ).astype(bf16)
    (att_grad_got,) = exchange(10, [(att_grad_tp, EACH, FSDP)], ring_one, hops[2])

    def own_pair(held, part):
        piece = lax.dynamic_slice_in_dim(held, ci * (dim // cs), dim // cs, 0)
        return jnp.stack([piece[:, :part], piece[:, part:]])

    qkv_old = lax.dynamic_slice_in_dim(qkv_w, ci * (dim // cs), dim // cs, 0)
    attended_grad = att_grad_got.reshape(heads_dim, tok)

    query_grad, key_grad, value_grad, mamba_in_old = hosted_call(
        functools.partial(attend_back_body, groups),
        (KVH,),
        [q_spec, k_spec, v_spec, bias_spec, total_spec, q_spec],
        [q_spec, k_spec, k_spec],
        [
            jax.ShapeDtypeStruct((heads_dim, tok), bf16),
            jax.ShapeDtypeStruct((kv_dim, seen), f32),
            jax.ShapeDtypeStruct((kv_dim, seen), f32),
        ],
        (queries, key_rows, key_rows, bias, log_totals, attended_grad),
        24,
        Traffic([(own_pair(mi_w, chan_p), PAIR, FSDP)], ring_one, hops[3]),
        16 * MIB,
    )
    kv_grad_all = jnp.concatenate([key_grad, value_grad], axis=0)
    kv_send = jnp.stack(
        [
            kv_grad_all[:, META + (reach - d) * tok : META + (reach - d + 1) * tok]
            for d in range(1, reach + 1)
        ]
    ).astype(bf16)
    meta_send = kv_grad_all[:, :META].T.astype(bf16).reshape(cs, metas, 2 * kv_dim)
    kv_back, meta_back, down_got = exchange(
        13,
        [
            (kv_send, BACK, CTX),
            (meta_send, EACH, CTX),
            (down_part, REDUCE, FSDP),
        ],
        ring_one,
        hops[4],
        reach,
    )
    output = residual + jnp.sum(down_got.astype(f32), axis=0)
    own_kv_grad = kv_grad_all[:, META + reach * tok :]
    for d in range(1, reach + 1):
        own_kv_grad = own_kv_grad + jnp.where(ci + d < cs, kv_back[d - 1].astype(f32), 0.0)
    meta_kv_grad = jnp.sum(meta_back.astype(f32), axis=0).astype(bf16)
    meta_grad_parts = column_parts(
        jnp.pad(meta_kv_grad, ((0, 0), (heads_dim, 0))), 1, fs, qkv_w.shape[1]
    )
    qkv_grad = jnp.concatenate([query_grad, own_kv_grad.astype(bf16)], axis=0)
    qkv_grad_tp, meta_grad_tp = exchange(
        14,
        [
            (qkv_grad.reshape(fs, -1, tok), EACH, FSDP),
            (meta_grad_parts, EACH, FSDP),
        ],
        ring_one,
        hops[5],
    )

    mixture_grad = dense_nt(ssm_proj_low, mo_w).reshape(fs, tok, chan_p)
    read_grad = mixture_grad * gate_silu
    gate_grad = mixture_grad * pre_mix * (gate_s * (1.0 + gate_z * (1.0 - gate_s)))
    gate_low = gate_grad.astype(bf16).reshape(fs * tok, chan_p)
    qkv_full = jnp.einsum("ftd,fct->dc", normed_rows, qkv_grad_tp, preferred_element_type=f32)
    qkv_full = qkv_full + jnp.einsum(
        "md,fmc->dc", meta_low, meta_grad_tp, preferred_element_type=f32
    )
    ring_two = Ring(
        [
            row_chunks(normed_all, gate_low),
            qkv_full.astype(bf16).reshape(cs, 1, dim // cs, qkv_w.shape[1]),
            column_chunks(att_tp, attn_proj_low),
            column_chunks(mixture_low[:, :chan], ssm_proj_low, 2),
        ],
        [(0, 0, 1), (1, 0, -1), (2, 0, -1), (3, 0, 1), (3, 1, -1)],
    )
    hops = spread_hops([1, 2, 2, 2])
    gate_sum, up_sum, down_top, down_low = ring_one.finish()
    first_adj, gate_up_old = scan_call(
        adjoint_head_body,
        (step_far, read_grad, c_wide, rate2),
        (SEQ, SEQ, SPREAD, RATE),
        (STATE,),
        *sizes,
        cid=21,
        plan=Traffic([(own_pair(gu_w, ffw_p), PAIR, FSDP)], ring_two, hops[0]),
    )
    adj_after, gate_up_sum = exchange(
        11,
        [
            (first_adj.astype(bf16), PREV, CTX),
            (jnp.stack([gate_sum, up_sum]).astype(bf16), PAIR, FSDP),
        ],
        ring_two,
        hops[1],
        reach,
    )
    gate_up_old = unpaired(gate_up_old, ffw)
    mamba_in_old = unpaired(mamba_in_old, chan)
    later = jnp.zeros((fs, DS, chan_p), f32)
    for d in range(reach, 0, -1):
        there = jnp.where(ci + d < cs, adj_after[d - 1].astype(f32), 0.0)
        later = decay_of(ci + d) * later + there
    drive_grad, exp_grad, b_acc, c_acc, rate_grad = scan_call(
        adjoint_full_body,
        (step_far, drive, read_grad, b_wide, c_wide, rate2, hist, later),
        (SEQ, SEQ, SEQ, SPREAD, SPREAD, RATE, HIST, STATE),
        (SEQ, SEQ, SPREAD, SPREAD, DRATE),
        *sizes,
        cid=22,
        plan=Traffic([], ring_two, hops[2]),
        later=(3,) if hops[2] == 2 else (),
    )
    cross = [
        (f * cs + c, (c // halves) * cs + halves * f + c % halves)
        for f in range(fs)
        for c in range(cs)
    ]
    down_both = jnp.concatenate([down_top, down_low], axis=0).astype(bf16)
    drive_grad, down_both = together(drive_grad, down_both)
    down_sum = lax.ppermute(down_both, (FSDP, CTX), cross)
    step_grad = drive_grad * inner_x + exp_grad * LN2
    pre_delta_grad = step_grad * jax.nn.sigmoid(pre_delta)
    inner_grad = drive_grad * step + skip * read_grad
    small_grad = jnp.concatenate(
        [
            jnp.sum(pre_delta_grad, axis=(0, 1))[None],
            jnp.sum(inner_x * read_grad, axis=(0, 1))[None],
            jnp.sum(rate_grad, axis=0) * rate,
        ],
        axis=0,
    )
    pre_delta_low = pre_delta_grad.astype(bf16).reshape(fs * tok, chan_p)
    xgrad_part = jnp.concatenate(
        [
            lax.dot_general(
                dt_w, pre_delta_low, (((0,), (1,)), ((), ())), preferred_element_type=f32
            ),
            jnp.sum(b_acc, axis=-1).reshape(fs * tok, DS).T,
            jnp.sum(c_acc, axis=-1).reshape(fs * tok, DS).T,
        ],
        axis=0,
    )
    (xgrad_got,) = exchange(12, [(xgrad_part, GATHER, FSDP)], ring_two, hops[3])
    xproj_grad = jnp.sum(xgrad_got, axis=0).T.astype(bf16)
    inner_grad = inner_grad + dense_nt(xproj_grad, xp_w).reshape(fs, tok, chan_p)
    ext_grad, taps_grad = conv_pull(inner_grad)
    returned = lax.ppermute(ext_grad[:, : CONV - 1].astype(bf16), CTX, down_ring).astype(f32)
    inner_pre_grad = ext_grad[:, CONV - 1 :] + jnp.pad(
        returned, ((0, 0), (tok - (CONV - 1), 0), (0, 0))
    )
    inner_pre_low = inner_pre_grad.astype(bf16).reshape(fs * tok, chan_p)
    mamba_in_grad = jnp.concatenate([inner_pre_low, gate_low], axis=1)
    split = ceil_to(chan_p * 9 // 16, 128)
    ring_three = Ring(
        [
            row_chunks(normed_all, inner_pre_low[:, :split]),
            row_chunks(normed_all, inner_pre_low[:, split:]),
            column_chunks(
                jnp.concatenate([inner_low[:, :chan], pre_delta_low[:, :chan]], axis=0),
                jnp.concatenate(
                    [
                        jnp.pad(xproj_grad, ((0, 0), (0, DTR))),
                        jnp.pad(delta_low, ((0, 0), (xdim, 0))),
                    ],
                    axis=0,
                ),
            ),
        ],
        [(0, 0, 1), (1, 0, -1), (2, 0, -1)],
    )
    vec_grad = jnp.concatenate([taps_grad, small_grad], axis=0)
    token_back = jnp.einsum("fct,dc->ftd", qkv_grad_tp, qkv_w, preferred_element_type=f32)
    token_back = token_back + dense_nt(mamba_in_grad, mi_w).reshape(fs, tok, dim)
    meta_back_rows = jnp.einsum("fmc,dc->fmd", meta_grad_tp, qkv_w, preferred_element_type=f32)
    normed_back = jnp.concatenate([token_back.astype(bf16), meta_back_rows.astype(bf16)], axis=1)
    hops = spread_hops([3, 2, 2])
    (normed_got,) = exchange(15, [(normed_back, REDUCE, FSDP)], ring_three, hops[0])
    normed_grad = jnp.sum(normed_got.astype(f32), axis=0)
    source_part, gain_in_grad = norm_pull(normed_grad[:tok])
    source_grad = residual_grad + source_part
    meta_grad, gain_in_meta = meta_pull(normed_grad[tok:])
    embed_part = jnp.concatenate(
        [
            meta_grad,
            jnp.stack([gain_in_grad + gain_in_meta, gain_attn_grad, gain_ssm_grad, gain_ffn_grad]),
        ],
        axis=0,
    )
    (embed_rows,) = exchange(17, [(embed_part, GATHER, FSDP)], ring_three, hops[1])
    embed_got, vec_got = exchange(
        18,
        [
            (jnp.sum(embed_rows, axis=0).astype(bf16), LINE, CTX),
            (vec_grad.astype(bf16), LINE, CTX),
        ],
        ring_three,
        hops[2],
    )
    embed_got = embed_got.astype(f32)
    vec_part = jnp.sum(vec_got.astype(f32), axis=0)
    embed_total = jnp.concatenate(
        [embed_got[:, :metas].reshape(META, dim), jnp.sum(embed_got[:, metas:], axis=0)], axis=0
    )
    gate_half, qkv_gradient, attn_sum, out_top, out_low = ring_two.finish()
    inner_a, inner_b, proj_sum = ring_three.finish()
    mamba_in_sum, attn_sum, mamba_out_sum, proj_sum, vec_all = exchange(
        23,
        [
            (
                jnp.stack([jnp.concatenate([inner_a, inner_b], axis=1), gate_half]).astype(bf16),
                PAIR,
                FSDP,
            ),
            (attn_sum.astype(bf16), CROSS, BOTH),
            (jnp.concatenate([out_top, out_low], axis=0).astype(bf16), CROSS, BOTH),
            (proj_sum.astype(bf16), CROSS, BOTH),
            (vec_part, GATHER, FSDP),
        ],
    )
    ssm_total = jnp.concatenate([vec_all[j, :, :chan] for j in range(fs)], axis=1)
    gate_up_gradient = unpaired(gate_up_sum, ffw)
    mamba_in_gradient = unpaired(mamba_in_sum, chan)
    ffn_down_gradient = down_sum.astype(f32)
    attn_gradient = attn_sum.astype(f32)
    mamba_out_gradient = mamba_out_sum.astype(f32)
    ssm_proj_gradient = proj_sum.astype(f32)

    def adam_block(gradient, moments_old, weight):
        return adam_step(gradient, moments_old, weight.astype(f32))

    qkv_moments, qkv_update = adam_block(qkv_gradient, m_qkv, qkv_old)
    attn_moments, attn_update = adam_block(attn_gradient, m_attn_out, attn_old)
    mamba_in_moments, mamba_in_update = adam_block(mamba_in_gradient, m_mamba_in, mamba_in_old)
    ssm_proj_moments, ssm_proj_update = adam_block(ssm_proj_gradient, m_ssm_proj, ssm_proj_old)
    mamba_out_moments, mamba_out_update = adam_block(
        mamba_out_gradient, m_mamba_out, mamba_out_old
    )
    gate_up_moments, gate_up_update = adam_block(gate_up_gradient, m_gate_up, gate_up_old)
    ffn_down_moments, ffn_down_update = adam_block(ffn_down_gradient, m_ffn_down, ffn_down_old)
    ssm_vec_moments, ssm_vec_update = adam_step(ssm_total, m_ssm_vec, ssm_vec)
    embed_moments, embed_update = adam_step(embed_total, m_embed_small, embed_small)
    return (
        output.astype(jnp.bfloat16)[None],
        source_grad[None],
        qkv_gradient,
        qkv_moments,
        qkv_update,
        attn_gradient,
        attn_moments,
        attn_update,
        mamba_in_gradient,
        mamba_in_moments,
        mamba_in_update,
        ssm_proj_gradient,
        ssm_proj_moments,
        ssm_proj_update,
        mamba_out_gradient,
        mamba_out_moments,
        mamba_out_update,
        gate_up_gradient,
        gate_up_moments,
        gate_up_update,
        ffn_down_gradient,
        ffn_down_moments,
        ffn_down_update,
        ssm_total,
        ssm_vec_moments,
        ssm_vec_update,
        embed_total,
        embed_moments,
        embed_update,
    )


def solution(mesh):
    in_specs = (
        P(FSDP, CTX, None),
        P(FSDP, CTX, None),
        P(FSDP, None),
        P(FSDP, None),
        P(None, CTX, FSDP),
        P(FSDP, None),
        P(None, CTX, FSDP),
        P(FSDP, None),
        P(None, CTX, FSDP),
        P(FSDP, None),
        P(None, CTX, FSDP),
        P(FSDP, None),
        P(None, CTX, FSDP),
        P(FSDP, None),
        P(None, CTX, FSDP),
        P(FSDP, None),
        P(None, CTX, FSDP),
        P(),
        P(),
        P(),
        P(),
    )
    out_specs = (
        P(FSDP, CTX, None),
        P(FSDP, CTX, None),
        P(CTX, FSDP),
        P(CTX, FSDP),
        P(CTX, FSDP),
        P(CTX, FSDP),
        P(CTX, FSDP),
        P(CTX, FSDP),
        P(CTX, FSDP),
        P(CTX, FSDP),
        P(CTX, FSDP),
        P(CTX, FSDP),
        P(CTX, FSDP),
        P(CTX, FSDP),
        P(CTX, FSDP),
        P(CTX, FSDP),
        P(CTX, FSDP),
        P(CTX, FSDP),
        P(CTX, FSDP),
        P(CTX, FSDP),
        P(CTX, FSDP),
        P(CTX, FSDP),
        P(CTX, FSDP),
        P(),
        P(),
        P(),
        P(),
        P(),
        P(),
    )
    return jax.shard_map(shards, mesh=mesh, in_specs=in_specs, out_specs=out_specs, check_vma=False)
```

time: 1830 us -> 1230 us (0.67)
  waiting for transfers between devices: 588 us -> 0.01 us
  Pallas kernels: 638 us -> 751 us
  matrix products: 174 us -> 88.4 us
  local copies, waits for them, and re-layouts: 196 us -> 259 us
  starting transfers between devices: 62.7 us -> 9.5 us
  other arithmetic: 134 us -> 106 us
    reduce_scatter x3 -> x0, waiting for transfers between devices: 268 us -> none  [summed(): return lax.psum_scatter(value, 'ctx', scatter_dimension=0, tiled=True)]
    unnamed x12 -> x0, waiting for transfers between devices: 185 us -> none
    pallas_call x20 -> x25, Pallas kernels: 638 us -> 751 us  [the longest x19 581 us: exchange(): pl.pallas_call(body, out_shape=tuple(plan.outs), in_specs=[ANY] * ins, ou...]
    ppermute x17 -> x3, waiting for transfers between devices: 96.3 us -> 0.01 us  [the longest x1 0.01 us: shards(): tail_rows = lax.ppermute(inner_pre[:, tok - (CONV - 1):], CTX, up_ring)]
    unnamed x354 -> x635, local copies, waits for them, and re-layouts: 83.5 us -> 146 us
    dot_general x34 -> x12, matrix products: 73.8 us -> 27 us  [the longest x4 11.6 us: column_chunks(): jnp.einsum('tr,jtn->jrn', operand, pieces, preferred_element_type=f32)]
    ppermute x17 -> x3, starting transfers between devices: 53.8 us -> 9.5 us  [the longest x1 5.41 us: shards(): down_sum = lax.ppermute(down_both, (FSDP, CTX), cross)]
    psum x1 -> x0, waiting for transfers between devices: 38.8 us -> none  [shards(): ssm_total, embed_total = lax.psum((vec_grad, embed_grad), ('fsdp', 'ctx'))]
  transfers between devices with their start and end apart: 26 -> 3, of which waited for: 12 -> 0; matrix products, arithmetic and copies ran while one was open for 15% -> 11% of each run, Pallas kernels for 15% -> 16%
where the time goes in v2:
time: 1230 us; the launch traced here: 1220 us
  Pallas kernels  751 us (61%)
  local copies, waits for them, and re-layouts  259 us (21%)
  other arithmetic  106 us (9%)
  matrix products  88.4 us (7%)
    pallas_call x19, Pallas kernels, exchange(): pl.pallas_call(body, out_shape=tuple(plan.outs), in_specs=[ANY] * ins, ou...  581 us
    pallas_call x6, Pallas kernels, hosted_call(): pl.pallas_call(hosted, grid=grid, in_specs=in_specs + [ANY] * x_in, out_s...  170 us
    unnamed x635, local copies, waits for them, and re-layouts  146 us
  transfers between devices with their start and end apart: 3, of which 0 were waited for; matrix products, arithmetic and copies ran while one was open for 11% of the time, Pallas kernels for 16%

profile of v2, /device:TPU:2, one launch (start us, length us, event | category | flops | bytes accessed | tf_op | source)
XLA Modules:
  0.0 1218.5 jit_solution(15116901145693064998)
XLA Ops:
  0.7 6.6 fusion.254
  16.7 61.9 %shard_map.428 = (bf16[4,128,1600]{2,1,0:T(8,128)(2,1)S(1)}, s32[4,1,1024]{2,1,0:T(1,128)S(1)}, bf16[4,2,5,40,1792]{4,3,2,1,0:T(8,128)(2,1)S(1)}, bf16[4,2,5,40,560]{4,3,2,1,0:T(8,128)(2,1)S(1)}) custom-call(bf16[128,1600]{1,0:T(8,128)(2,1)S(1)} %fusion.115.refs_0_, s32[1,1024]{1,0:T(1,128)S(1)} %copy-done.139, ...), custom_call_target="tpu_custom_call" | custom-call | tf_op jit(solution)/shard_map/pallas_call | solution.py:508
  92.0 10.5 shard_map.429
  103.7 5.4 fusion.253
  113.2 22.7 %shard_map.430 = (bf16[4,640,128]{2,1,0:T(8,128)(2,1)S(1)}, bf16[8,16,640]{2,1,0:T(8,128)(2,1)S(1)}, bf16[4,2,1,40,2816]{4,3,2,1,0:T(8,128)(2,1)S(1)}) custom-call(bf16[640,128]{1,0:T(8,128)(2,1)S(1)} %slice.643.refs_0_, bf16[16,640]{1,0:T(8,128)(2,1)S(1)} %pad_maximum_fusion.18.refs_1_, bf16[4,2,5,40,2816]{4,3,2,1,0:T(8,128)(2,1)S(1)} %pad_maximum_fusion.refs_2_.refs_4_.refs_1_), custom_call_target="tpu_custom_call" | custom-call | tf_op jit(solution)/shard_map/pallas_call | solution.py:508
  141.7 25.6 %shard_map.431 = (bf16[1600,128]{1,0:T(8,128)(2,1)S(1)}, f32[5,5,128]{2,1,0:T(8,128)S(1)}, bf16[4,2,1,40,2816]{4,3,2,1,0:T(8,128)(2,1)S(1)}) custom-call(bf16[1600,128]{1,0:T(8,128)(2,1)S(1)} %slice.642.refs_0_, bf16[640,768]{1,0:T(8,128)(2,1)S(1)} %constant_dynamic-update-slice_fusion.refs_1_.refs_2_, ...), custom_call_target="tpu_custom_call" | custom-call | tf_op jit(solution)/shard_map/pallas_call | solution.py:642
  168.5 24.2 %shard_map.432 = (bf16[4,400,128]{2,1,0:T(8,128)(2,1)S(1)}, bf16[4,2,1,40,2816]{4,3,2,1,0:T(8,128)(2,1)S(1)}) custom-call(bf16[4,400,128]{2,1,0:T(8,128)(2,1)S(1)} %bitcast.645, bf16[4,2,5,40,2816]{4,3,2,1,0:T(8,128)(2,1)S(1)} %copy-done.5), custom_call_target="tpu_custom_call" | custom-call | tf_op jit(solution)/shard_map/pallas_call | solution.py:508
  193.9 4.9 fusion.257
  211.7 5.2 copy.246
  222.8 15.1 %copy.241 = bf16[512,1600]{1,0:T(8,128)(2,1)} copy(bf16[512,1600]{0,1:T(8,128)(2,1)} %convolution_convert_fusion.6) | data formatting | bytes 3276800 | tf_op jit(solution)/shard_map/convert_element_type | solution.py:1070
  246.9 5.8 fusion.239
  253.3 26.4 %shard_map.433 = (f32[4,132,512]{2,1,0:T(8,128)S(1)}, bf16[200,400]{1,0:T(8,128)(2,1)S(1)}, bf16[400,58]{1,0:T(8,128)(2,1)S(1)}) custom-call(f32[132,512]{1,0:T(8,128)S(1)} %fusion.156.refs_0_, bf16[200,400]{1,0:T(8,128)(2,1)S(1)} %dynamic_slice.107.refs_1_, bf16[400,58]{1,0:T(8,128)(2,1)S(1)} %dynamic_slice.108.refs_2_), custom_call_target="tpu_custom_call" | custom-call | tf_op jit(solution)/shard_map/pallas_call | solution.py:508
  288.5 20.5 %shard_map.434 = (f32[4,16,896]{2,1,0:T(8,128)S(1)}, bf16[400,400]{1,0:T(8,128)(2,1)S(1)}) custom-call(f32[4,128,896]{2,1,0:T(8,128)S(1)} %get-tuple-element.432.refs_0_, f32[4,128,896]{2,1,0:T(8,128)S(1)} %get-tuple-element.470.refs_1_, f32[4,128,16,128]{3,2,1,0:T(8,128)S(1)} %broadcast_in_dim.186.refs_2_.refs_3_, ...), custom_call_target="tpu_custom_call" | custom-call | tf_op jit(solution)/shard_map/pallas_call | solution.py:642
  314.1 31.1 %shard_map.435 = (bf16[4,4,16,896]{3,2,1,0:T(8,128)(2,1)S(1)}, f32[8,4,896]{2,1,0:T(4,128)S(1)}, bf16[4,2,2,40,2816]{4,3,2,1,0:T(8,128)(2,1)S(1)}) custom-call(bf16[4,16,896]{2,1,0:T(8,128)(2,1)S(1)} %convert_element_type.429.refs_0_, f32[4,896]{1,0:T(4,128)S(1)} %get-tuple-element.431.refs_1_, bf16[4,2,5,40,2816]{4,3,2,1,0:T(8,128)(2,1)S(1)} %copy-done.6), custom_call_target="tpu_custom_call" | custom-call | tf_op jit(solution)/shard_map/pallas_call | solution.py:508
  350.1 36.5 %shard_map.436 = (f32[4,128,896]{2,1,0:T(8,128)S(1)}, f32[4,128,16,896]{3,2,1,0:T(8,128)}, bf16[688,400]{1,0:T(8,128)(2,1)S(1)}) custom-call(f32[4,128,896]{2,1,0:T(8,128)S(1)} %get-tuple-element.432.refs_0_, f32[4,128,896]{2,1,0:T(8,128)S(1)} %copy-done.28, f32[4,128,16,128]{3,2,1,0:T(8,128)S(1)} %copy-done.20, ...), custom_call_target="tpu_custom_call" | custom-call | tf_op jit(solution)/shard_map/pallas_call | solution.py:642
  392.9 3.7 copy.247
  398.0 23.6 %shard_map.437 = (bf16[2,128,1600]{2,1,0:T(8,128)(2,1)S(1)}, bf16[2,128,1600]{2,1,0:T(8,128)(2,1)S(1)}) custom-call(bf16[4,128,1600]{2,1,0:T(8,128)(2,1)S(1)} %bitcast.627, bf16[4,128,1600]{2,1,0:T(8,128)(2,1)S(1)} %bitcast.628), custom_call_target="tpu_custom_call" | custom-call | tf_op jit(solution)/shard_map/pallas_call | solution.py:508
  423.7 23.3 %shard_map.438 = (bf16[4,128,1600]{2,1,0:T(8,128)(2,1)S(1)}, bf16[4,128,1600]{2,1,0:T(8,128)(2,1)S(1)}) custom-call(bf16[128,1600]{1,0:T(8,128)(2,1)S(1)} %multiply_convert_fusion.2.refs_0_, bf16[128,1600]{1,0:T(8,128)(2,1)S(1)} %bitcast.631), custom_call_target="tpu_custom_call" | custom-call | tf_op jit(solution)/shard_map/pallas_call | solution.py:508
  454.4 5.4 fusion.266
  463.2 4.8 convolution_convert_fusion
  468.0 4.8 convolution_convert_fusion.1
  472.7 6.1 convolution_convert_fusion.7
  486.8 6.3 convolution_convert_fusion.4
  493.1 4.6 fusion.7
  497.7 8.0 copy.256
  517.9 23.6 %shard_map.439 = (bf16[2,128,1600]{2,1,0:T(8,128)(2,1)S(1)}, bf16[200,1408]{1,0:T(8,128)(2,1)S(1)}, bf16[200,1408]{1,0:T(8,128)(2,1)S(1)}, bf16[344,400]{1,0:T(8,128)(2,1)S(1)}, bf16[344,400]{1,0:T(8,128)(2,1)S(1)}) custom-call(bf16[4,128,1600]{2,1,0:T(8,128)(2,1)S(1)} %bitcast.630, bf16[8,1,200,1408]{3,2,1,0:T(8,128)(2,1)S(1)} %bitcast.581, ...), custom_call_target="tpu_custom_call" | custom-call | tf_op jit(solution)/shard_map/pallas_call | solution.py:508
  547.6 25.0 %shard_map.440 = (bf16[4,128,1600]{2,1,0:T(8,128)(2,1)S(1)}, bf16[4,128,1600]{2,1,0:T(8,128)(2,1)S(1)}, bf16[200,1408]{1,0:T(8,128)(2,1)S(1)}, bf16[200,1408]{1,...) custom-call(bf16[128,1600]{1,0:T(8,128)(2,1)S(1)} %get-tuple-element.499.refs_0_, ...), custom_call_target="tpu_custom_call" | custom-call | tf_op jit(solution)/shard_map/pallas_call | solution.py:508
  576.6 24.2 %shard_map.441 = (bf16[4,400,128]{2,1,0:T(8,128)(2,1)S(1)}, bf16[200,1408]{1,0:T(8,128)(2,1)S(1)}, bf16[200,1408]{1,0:T(8,128)(2,1)S(1)}, bf16[344,400]{1,0:T(8,128)(2,1)S(1)}, bf16[344,400]{1,0:T(8,128)(2,1)S(1)}) custom-call(bf16[4,400,128]{2,1,0:T(8,128)(2,1)S(1)} %fusion.93.refs_0_, bf16[8,1,200,1408]{3,2,1,0:T(8,128)(2,1)S(1)} %bitcast.583, ...), custom_call_target="tpu_custom_call" | custom-call | tf_op jit(solution)/shard_map/pallas_call | solution.py:508
  600.9 24.4 %shard_map.442 = (bf16[1600,128]{1,0:T(8,128)(2,1)S(1)}, f32[320,768]{1,0:T(8,128)S(1)}, f32[320,768]{1,0:T(8,128)S(1)}, bf16[2,200,896]{2,1,0:T(8,128)(2,1)S(1)...) custom-call(bf16[1600,128]{1,0:T(8,128)(2,1)S(1)} %copy-done.45, ...), custom_call_target="tpu_custom_call" | custom-call | tf_op jit(solution)/shard_map/pallas_call | solution.py:642
  641.5 70.0 %shard_map.443 = (bf16[4,640,128]{2,1,0:T(8,128)(2,1)S(1)}, bf16[8,16,640]{2,1,0:T(8,128)(2,1)S(1)}, bf16[2,128,1600]{2,1,0:T(8,128)(2,1)S(1)}, bf16[200,1408]{1...) custom-call(bf16[4,640,128]{2,1,0:T(8,128)(2,1)S(1)} %pad_maximum_fu, ...), custom_call_target="tpu_custom_call" | custom-call | tf_op jit(solution)/shard_map/pallas_call | solution.py:508
  725.5 23.1 %shard_map.444 = (bf16[4,560,128]{2,1,0:T(8,128)(2,1)S(1)}, bf16[4,16,560]{2,1,0:T(8,128)(2,1)S(1)}, bf16[200,1408]{1,0:T(8,128)(2,1)S(1)}, bf16[200,1408]{1,0:T...) custom-call(bf16[4,560,128]{2,1,0:T(8,128)(2,1)S(1)} %bitcast.636, ...), custom_call_target="tpu_custom_call" | custom-call | tf_op jit(solution)/shard_map/pallas_call | solution.py:508
  755.5 5.1 multiply_reduce_fusion
  764.4 4.4 convert_bitcast_fusion
  772.4 4.9 fusion.259
  790.9 3.8 copy.264
  805.7 19.6 %shard_map.445 = (f32[4,16,896]{2,1,0:T(8,128)S(1)}, bf16[2,200,1408]{2,1,0:T(8,128)(2,1)S(1)}, bf16[200,896]{1,0:T(8,128)(2,1)S(1)}, bf16[200,560]{1,0:T(8,128)...) custom-call(f32[4,128,896]{2,1,0:T(8,128)S(1)} %copy-done.26, ...), custom_call_target="tpu_custom_call" | custom-call | tf_op jit(solution)/shard_map/pallas_call | solution.py:642
  828.2 48.1 %shard_map.446 = (bf16[4,4,16,896]{3,2,1,0:T(8,128)(2,1)S(1)}, bf16[2,200,1408]{2,1,0:T(8,128)(2,1)S(1)}, bf16[200,896]{1,0:T(8,128)(2,1)}, bf16[200,896]{1,0:T(...) custom-call(bf16[4,16,896]{2,1,0:T(8,128)(2,1)S(1)} %convert_element, ...), custom_call_target="tpu_custom_call" | custom-call | tf_op jit(solution)/shard_map/pallas_call | solution.py:508
  879.0 43.9 %shard_map.447 = (f32[4,128,896]{2,1,0:T(8,128)S(1)}, f32[4,128,896]{2,1,0:T(8,128)S(1)}, f32[4,128,16,128]{3,2,1,0:T(8,128)}, f32[4,128,16,128]{3,2,1,0:T(8,128...) custom-call(f32[4,128,896]{2,1,0:T(8,128)} %copy-done.25, ...), custom_call_target="tpu_custom_call" | custom-call | tf_op jit(solution)/shard_map/pallas_call | solution.py:642
  932.1 4.2 reduce_sum.415
  947.6 36.4 %shard_map.448 = (f32[4,132,512]{2,1,0:T(8,128)S(1)}, bf16[200,896]{1,0:T(8,128)(2,1)}, bf16[200,896]{1,0:T(8,128)(2,1)S(1)}, bf16[200,560]{1,0:T(8,128)(2,1)}, ...) custom-call(f32[132,512]{1,0:T(8,128)S(1)} %pad_maximum_fusion.15.re, ...), custom_call_target="tpu_custom_call" | custom-call | tf_op jit(solution)/shard_map/pallas_call | solution.py:508
  991.6 7.7 multiply_reduce_fusion.3
  1015.0 5.4 collective-permute-start.2
  1028.9 6.6 fusion.32
  1058.1 25.8 %shard_map.449 = (bf16[2,144,1600]{2,1,0:T(8,128)(2,1)S(1)}, bf16[200,512]{1,0:T(8,128)(2,1)}, bf16[200,512]{1,0:T(8,128)(2,1)}, bf16[200,512]{1,0:T(8,128)(2,1)...) custom-call(bf16[4,144,1600]{2,1,0:T(8,128)(2,1)S(1)} %pad_maximum_f, ...), custom_call_target="tpu_custom_call" | custom-call | tf_op jit(solution)/shard_map/pallas_call | solution.py:508
  1092.5 17.6 %shard_map.450 = (f32[4,20,1600]{2,1,0:T(8,128)S(1)}, bf16[200,512]{1,0:T(8,128)(2,1)}, bf16[200,512]{1,0:T(8,128)(2,1)S(1)}, bf16[200,384]{1,0:T(8,128)(2,1)}, ...) custom-call(f32[20,1600]{1,0:T(8,128)S(1)} %concatenate.130.refs_0_, ...), custom_call_target="tpu_custom_call" | custom-call | tf_op jit(solution)/shard_map/pallas_call | solution.py:508
  1119.6 27.3 %shard_map.451 = (bf16[8,20,1600]{2,1,0:T(8,128)(2,1)S(1)}, bf16[8,22,896]{2,1,0:T(8,128)(2,1)S(1)}, bf16[200,512]{1,0:T(8,128)(2,1)}, bf16[200,512]{1,0:T(8,128...) custom-call(bf16[20,1600]{1,0:T(8,128)(2,1)S(1)} %copy-done.105, ...), custom_call_target="tpu_custom_call" | custom-call | tf_op jit(solution)/shard_map/pallas_call | solution.py:508
  1149.3 35.7 %shard_map.452 = (bf16[2,200,896]{2,1,0:T(8,128)(2,1)S(1)}, bf16[200,400]{1,0:T(8,128)(2,1)S(1)}, bf16[400,400]{1,0:T(8,128)(2,1)S(1)}, bf16[400,58]{1,0:T(8,128)(2,1)S(1)}, f32[4,22,896]{2,1,0:T(8,128)S(1)}) custom-call(bf16[2,200,896]{2,1,0:T(8,128)(2,1)S(1)} %pad_maximum_fusion.10.refs_0_, bf16[200,400]{1,0:T(8,128)(2,1)S(1)} %fusion.163.refs_1_, ...), custom_call_target="tpu_custom_call" | custom-call | tf_op jit(solution)/shard_map/pallas_call | solution.py:508
  1209.5 4.1 fusion.79
  (840 shorter events, 330.0 us)
Async XLA Ops:
  9.5 81.1 %copy-start.212 = (f32[1600]{0:T(1024)}, f32[1600]{0:T(1024)S(1)}, u32[]{:S(2)}) copy-start(f32[1600]{0:T(1024)S(1)} %get-tuple-element.394) | copy-start | bytes 19204
  9.5 412.8 %copy-start.233 = (f32[1600]{0:T(1024)}, f32[1600]{0:T(1024)S(1)}, u32[]{:S(2)}) copy-start(f32[1600]{0:T(1024)S(1)} %get-tuple-element.392) | copy-start | bytes 19204
  9.5 412.8 %copy-start.235 = (f32[1600]{0:T(1024)}, f32[1600]{0:T(1024)S(1)}, u32[]{:S(2)}) copy-start(f32[1600]{0:T(1024)S(1)} %get-tuple-element.393) | copy-start | bytes 19204
  83.9 163.0 %collective-permute-start = (f32[4,3,896]{2,1,0:T(4,128)}, f32[4,3,896]{2,1,0:T(4,128)S(1)}, u32[]{:S(2)}, u32[]{:S(2)}) collective-permute-start(f32[4,3,896]{2,1,0:T(4,128)} %slice.648), channel_id=1, source_target_pairs={{0,1},{1,2},{2,3},{3,4},{4,5},{5,6},{6,7},{8,9},{9,10},{10,11},{11... | collective-permute-start | bytes 129032 | tf_op jit(solution)/shard_map/ppermute | solution.py:942
  102.5 35.5 %copy-start.44 = (bf16[1600,128]{1,0:T(8,128)(2,1)}, bf16[1600,128]{1,0:T(8,128)(2,1)S(1)}, u32[]{:S(2)}) copy-start(bf16[1600,128]{1,0:T(8,128)(2,1)S(1)} %slice.642.refs_0_) | copy-start | bytes 1228804
  103.7 143.1 %copy-start.197 = (f32[22,800]{1,0:T(8,128)}, f32[22,800]{1,0:T(8,128)S(1)}, u32[]{:S(2)}) copy-start(f32[22,800]{1,0:T(8,128)S(1)} %constant_dynamic-slice_fusion) | copy-start | bytes 211204
  141.7 25.6 %copy-start.48 = (f32[768,128]{1,0:T(8,128)}, f32[768,128]{1,0:T(8,128)S(1)}, u32[]{:S(2)}) copy-start(f32[768,128]{1,0:T(8,128)S(1)} %pad_select_fusion.refs_3_) | copy-start | bytes 1179652
  141.7 26.8 %copy-start.5 = (bf16[4,2,5,40,2816]{4,3,2,1,0:T(8,128)(2,1)S(1)}, bf16[4,2,5,40,2816]{4,3,2,1,0:T(8,128)(2,1)}, u32[]{:S(2)}) copy-start(bf16[4,2,5,40,2816]{4,3,2,1,0:T(8,128)(2,1)} %copy-done.3) | copy-start | bytes 27033604
  208.0 38.9 %copy-start.270 = (pred[4,128]{1,0:T(4,128)(4,1)}, pred[4,128]{1,0:T(4,128)(4,1)S(1)}, u32[]{:S(2)}) copy-start(pred[4,128]{1,0:T(4,128)(4,1)S(1)} %get-tuple-element.533) | copy-start | bytes 1540
  208.0 38.9 %copy-start.272 = (pred[4,128]{1,0:T(4,128)(4,1)}, pred[4,128]{1,0:T(4,128)(4,1)S(1)}, u32[]{:S(2)}) copy-start(pred[4,128]{1,0:T(4,128)(4,1)S(1)} %get-tuple-element.534) | copy-start | bytes 1540
  208.0 38.9 %copy-start.274 = (pred[4,128]{1,0:T(4,128)(4,1)}, pred[4,128]{1,0:T(4,128)(4,1)S(1)}, u32[]{:S(2)}) copy-start(pred[4,128]{1,0:T(4,128)(4,1)S(1)} %get-tuple-element.535) | copy-start | bytes 1540
  246.9 36.6 %copy-start.244 = (f32[896]{0:T(1024)}, f32[896]{0:T(1024)S(1)}, u32[]{:S(2)}) copy-start(f32[896]{0:T(1024)S(1)} %get-tuple-element.401) | copy-start | bytes 10756
  252.8 26.9 %copy-start.164 = (bf16[4,128,896]{2,1,0:T(8,128)(2,1)}, bf16[4,128,896]{2,1,0:T(8,128)(2,1)S(1)}, u32[]{:S(2)}) copy-start(bf16[4,128,896]{2,1,0:T(8,128)(2,1)S(1)} %get-tuple-element.433) | copy-start | bytes 2752516
  287.1 61.9 %copy-start.25 = (f32[4,128,896]{2,1,0:T(8,128)}, f32[4,128,896]{2,1,0:T(8,128)S(1)}, u32[]{:S(2)}) copy-start(f32[4,128,896]{2,1,0:T(8,128)S(1)} %get-tuple-element.432.refs_0_) | copy-start | bytes 5505028
  314.1 33.8 %copy-start.202 = (f32[512,16]{1,0:T(8,128)S(1)}, f32[512,16]{1,0:T(8,128)}, u32[]{:S(2)}) copy-start(f32[512,16]{1,0:T(8,128)} %copy.313) | copy-start | bytes 98308
  314.1 34.9 %copy-start.28 = (f32[4,128,896]{2,1,0:T(8,128)S(1)}, f32[4,128,896]{2,1,0:T(8,128)}, u32[]{:S(2)}) copy-start(f32[4,128,896]{2,1,0:T(8,128)} %copy-done.27) | copy-start | bytes 5505028
  350.1 36.6 %copy-start.17 = (f32[4,128,16,128]{3,2,1,0:T(8,128)}, f32[4,128,16,128]{3,2,1,0:T(8,128)S(1)}, u32[]{:S(2)}) copy-start(f32[4,128,16,128]{3,2,1,0:T(8,128)S(1)} %broadcast_in_dim.188.refs_3_.refs_2_.refs_4_) | copy-start | bytes 12582916
  350.1 36.6 %copy-start.140 = (f32[4,128,896]{2,1,0:T(8,128)S(1)}, f32[4,128,896]{2,1,0:T(8,128)}, u32[]{:S(2)}) copy-start(f32[4,128,896]{2,1,0:T(8,128)} %get-tuple-element.434) | copy-start | bytes 5505028
  350.1 36.6 %copy-start.161 = (f32[4,128,1792]{2,1,0:T(8,128)S(1)}, f32[4,128,1792]{2,1,0:T(8,128)}, u32[]{:S(2)}) copy-start(f32[4,128,1792]{2,1,0:T(8,128)} %copy-done.160) | copy-start | bytes 11010052
  398.0 49.0 %slice-start.8 = ((s8[4505600]{0:T(1024)(128)(4,1)}), s8[4194304]{0:T(1024)(128)(4,1)S(1)}, s32[]{:S(2)}) async-start(s8[4505600]{0:T(1024)(128)(4,1)} %bitcast.712), calls=%async_computation.8 | async-start | bytes 8388608
  421.9 122.5 %copy-start.263 = (f32[128]{0:T(128)}, f32[128]{0:T(128)S(1)}, u32[]{:S(2)}) copy-start(f32[128]{0:T(128)S(1)} %fusion.222) | copy-start | bytes 1540
  421.9 25.1 %slice-start.9 = ((s8[4505600]{0:T(1024)(128)(4,1)}), s8[311296]{0:T(1024)(128)(4,1)S(1)}, s32[]{:S(2)}) async-start(s8[4505600]{0:T(1024)(128)(4,1)} %bitcast.712), calls=%async_computation.9 | async-start | bytes 622592
  423.1 121.4 %copy-start.265 = (f32[128]{0:T(128)}, f32[128]{0:T(128)S(1)}, u32[]{:S(2)}) copy-start(f32[128]{0:T(128)S(1)} %fusion.223) | copy-start | bytes 1540
  505.7 39.6 %slice-start.2 = ((s8[4505600]{0:T(1024)(128)(4,1)}), s8[311296]{0:T(1024)(128)(4,1)S(1)}, s32[]{:S(2)}) async-start(s8[4505600]{0:T(1024)(128)(4,1)} %bitcast.574), calls=%async_computation.2 | async-start | bytes 622592
  517.9 27.4 %slice-start.3 = ((s8[4505600]{0:T(1024)(128)(4,1)}), s8[4194304]{0:T(1024)(128)(4,1)S(1)}, s32[]{:S(2)}) async-start(s8[4505600]{0:T(1024)(128)(4,1)} %bitcast.574), calls=%async_computation.3 | async-start | bytes 8388608
  517.9 82.9 %slice-start.4 = ((s8[4505600]{0:T(1024)(128)(4,1)}), s8[311296]{0:T(1024)(128)(4,1)S(1)}, s32[]{:S(2)}) async-start(s8[4505600]{0:T(1024)(128)(4,1)} %bitcast.584), calls=%async_computation.4 | async-start | bytes 622592
  547.6 25.0 %copy-start.262 = (bf16[400,1600]{1,0:T(8,128)(2,1)S(1)}, bf16[400,1600]{1,0:T(8,128)(2,1)}, u32[]{:S(2)}) copy-start(bf16[400,1600]{1,0:T(8,128)(2,1)} %param.26) | copy-start | bytes 3840004
  547.6 53.2 %slice-start.5 = ((s8[4505600]{0:T(1024)(128)(4,1)}), s8[4194304]{0:T(1024)(128)(4,1)S(1)}, s32[]{:S(2)}) async-start(s8[4505600]{0:T(1024)(128)(4,1)} %bitcast.584), calls=%async_computation.5 | async-start | bytes 8388608
  576.6 24.3 %copy-start.45 = (bf16[1600,128]{1,0:T(8,128)(2,1)S(1)}, bf16[1600,128]{1,0:T(8,128)(2,1)}, u32[]{:S(2)}) copy-start(bf16[1600,128]{1,0:T(8,128)(2,1)} %copy-done.44) | copy-start | bytes 1228804
  576.6 24.3 %copy-start.49 = (f32[768,128]{1,0:T(8,128)S(1)}, f32[768,128]{1,0:T(8,128)}, u32[]{:S(2)}) copy-start(f32[768,128]{1,0:T(8,128)} %copy-done.48) | copy-start | bytes 1179652
  576.6 24.3 %copy-start.50 = (bf16[2,200,896]{2,1,0:T(8,128)(2,1)S(1)}, bf16[2,200,896]{2,1,0:T(8,128)(2,1)}, u32[]{:S(2)}) copy-start(bf16[2,200,896]{2,1,0:T(8,128)(2,1)} %pad_maximum_fusion.9.refs_6_) | copy-start | bytes 2150404
  715.4 33.3 %copy-start.72 = (bf16[2,128,1600]{2,1,0:T(8,128)(2,1)}, bf16[2,128,1600]{2,1,0:T(8,128)(2,1)S(1)}, u32[]{:S(2)}) copy-start(bf16[2,128,1600]{2,1,0:T(8,128)(2,1)S(1)} %get-tuple-element.190) | copy-start | bytes 2457604
  725.5 25.5 %copy-start.38 = (bf16[4,2,5,40,560]{4,3,2,1,0:T(8,128)(2,1)S(1)}, bf16[4,2,5,40,560]{4,3,2,1,0:T(8,128)(2,1)}, u32[]{:S(2)}) copy-start(bf16[4,2,5,40,560]{4,3,2,1,0:T(8,128)(2,1)} %copy-done.37) | copy-start | bytes 5376004
  725.5 29.9 %copy-start.162 = (f32[4,128,1792]{2,1,0:T(8,128)S(1)}, f32[4,128,1792]{2,1,0:T(8,128)}, u32[]{:S(2)}) copy-start(f32[4,128,1792]{2,1,0:T(8,128)} %copy-done.160) | copy-start | bytes 11010052
  725.5 29.9 %copy-start.176 = (bf16[800,1600]{0,1:T(8,128)(2,1)S(1)}, bf16[800,1600]{0,1:T(8,128)(2,1)}, u32[]{:S(2)}) copy-start(bf16[800,1600]{0,1:T(8,128)(2,1)} %copy.246) | copy-start | bytes 7680004
  772.4 55.7 %copy-start.15 = (bf16[4,800,400]{2,1,0:T(8,128)(2,1)}, bf16[4,800,400]{2,1,0:T(8,128)(2,1)S(1)}, u32[]{:S(2)}) copy-start(bf16[4,800,400]{2,1,0:T(8,128)(2,1)S(1)} %copy.274) | copy-start | bytes 7680004
  798.3 29.8 %copy-start.23 = (bf16[1600,896]{1,0:T(8,128)(2,1)}, bf16[1600,896]{1,0:T(8,128)(2,1)S(1)}, u32[]{:S(2)}) copy-start(bf16[1600,896]{1,0:T(8,128)(2,1)S(1)} %bitcast_convert_fusion) | copy-start | bytes 8601604
  802.2 25.9 %copy-start.29 = (bf16[4,400,400]{1,2,0:T(8,128)(2,1)}, bf16[4,400,400]{1,2,0:T(8,128)(2,1)S(1)}, u32[]{:S(2)}) copy-start(bf16[4,400,400]{1,2,0:T(8,128)(2,1)S(1)} %convolution_convert_fusion.10) | copy-start | bytes 3840004
  828.1 49.2 %copy-start.246 = (f32[4,896]{1,0:T(4,128)S(1)}, f32[4,896]{1,0:T(4,128)}, u32[]{:S(2)}) copy-start(f32[4,896]{1,0:T(4,128)} %get-tuple-element.520) | copy-start | bytes 43012
  828.1 49.2 %copy-start.247 = (f32[4,896]{1,0:T(4,128)S(1)}, f32[4,896]{1,0:T(4,128)}, u32[]{:S(2)}) copy-start(f32[4,896]{1,0:T(4,128)} %get-tuple-element.521) | copy-start | bytes 43012
  828.1 49.2 %copy-start.248 = (f32[4,896]{1,0:T(4,128)S(1)}, f32[4,896]{1,0:T(4,128)}, u32[]{:S(2)}) copy-start(f32[4,896]{1,0:T(4,128)} %get-tuple-element.522) | copy-start | bytes 43012
  828.2 49.2 %copy-start.249 = (f32[4,896]{1,0:T(4,128)S(1)}, f32[4,896]{1,0:T(4,128)}, u32[]{:S(2)}) copy-start(f32[4,896]{1,0:T(4,128)} %get-tuple-element.523) | copy-start | bytes 43012
  879.0 45.2 %copy-start.142 = (f32[4,128,896]{2,1,0:T(8,128)S(1)}, f32[4,128,896]{2,1,0:T(8,128)}, u32[]{:S(2)}) copy-start(f32[4,128,896]{2,1,0:T(8,128)} %get-tuple-element.434) | copy-start | bytes 5505028
  879.0 45.2 %copy-start.149 = (f32[512,896]{1,0:T(8,128)S(1)}, f32[512,896]{1,0:T(8,128)}, u32[]{:S(2)}) copy-start(f32[512,896]{1,0:T(8,128)} %fusion.194) | copy-start | bytes 5505028
  879.0 45.2 %copy-start.245 = (f32[896]{0:T(1024)S(1)}, f32[896]{0:T(1024)}, u32[]{:S(2)}) copy-start(f32[896]{0:T(1024)} %copy-done.244) | copy-start | bytes 10756
  1008.5 31.1 %collective-permute-start.1 = (bf16[4,3,896]{2,1,0:T(4,128)(2,1)}, bf16[4,3,896]{2,1,0:T(4,128)(2,1)}, u32[]{:S(2)}, u32[]{:S(2)}) collective-permute-start(bf16[4,3,896]{2,1,0:T(4,128)(2,1)} %slice.879), channel_id=1, source_target_pairs={{1,0},{2,1},{3,2},{4,3},{5,4},{6,5},{7,6},{9,8},{10,9},{11,10},{12... | collective-permute-start | bytes 64520 | tf_op jit(solution)/shard_map/ppermute | solution.py:1275
  1015.0 191.8 %collective-permute-start.2 = (bf16[688,400]{0,1:T(8,128)(2,1)}, bf16[688,400]{0,1:T(8,128)(2,1)}, u32[]{:S(2)}, u32[]{:S(2)}) collective-permute-start(bf16[688,400]{0,1:T(8,128)(2,1)} %copy.284), channel_id=1, source_target_pairs={{0,0},{1,1},{2,8},{3,9},{4,16},{5,17},{6,24},{7,25},{8,2},{9,3},{1... | collective-permute-start | bytes 1651208 | tf_op jit(solution)/shard_map/ppermute | solution.py:1248
  1149.2 37.3 %copy-start.133 = (bf16[400,58]{1,0:T(8,128)(2,1)S(1)}, bf16[400,58]{1,0:T(8,128)(2,1)}, u32[]{:S(2)}) copy-start(bf16[400,58]{1,0:T(8,128)(2,1)} %copy-done.132) | copy-start | bytes 139204
  (254 other events, 860.3 us)

commit v3 on v2

--- a/solution.py
+++ b/solution.py
@@ -87,16 +87,47 @@
         pl.when(condition)(action)
 
 
+def in_hbm(value):
+    return pltpu.with_memory_space_constraint(value, pltpu.HBM)
+
+
+def piece_edges(mode):
+    count = mode[2] - mode[1]
+    groups = 5 if count > 10 else 3
+    edges = [count * k // groups for k in range(groups + 1)]
+    return list(zip(edges[:-1], edges[1:]))
+
+
+def chunk_shape(value, cs):
+    lead, _, rows, cols = value.shape
+    return (rows, cols if lead == cs else cols * lead // cs)
+
+
+def chunk_ref(ref, block, part, cs):
+    lead = ref.shape[0]
+    if lead == cs:
+        return ref.at[block, part]
+    cols = ref.shape[3] * lead // cs
+    columns = pl.ds(pl.multiple_of(block // lead * cols, 128), cols)
+    return ref.at[lax.rem(block, lead), part, :, columns]
+
+
 class Ring:
     def __init__(self, chunks, uses):
         self.chunks, self.uses = chunks, uses
         self.got, self.hop = [], 0
 
     def finish(self):
-        block = lax.axis_index(CTX)
+        cs, block = span_of(CTX)
         sums = []
         for (k, part, _), got in zip(self.uses, self.got):
-            own = lax.dynamic_index_in_dim(self.chunks[k], block, 0, keepdims=False)[part]
+            value = self.chunks[k]
+            if value.shape[0] == cs:
+                own = lax.dynamic_index_in_dim(value, block, 0, keepdims=False)[part]
+            else:
+                rows, cols = chunk_shape(value, cs)
+                at = (block % value.shape[0], part, 0, block // value.shape[0] * cols)
+                own = lax.dynamic_slice(value, at, (1, 1, rows, cols))[0, 0]
             sums.append(got.astype(f32) + own.astype(f32))
         return sums
 
@@ -128,17 +159,17 @@
                 shape = (fs // 2,) + shape[1:]
                 own_scratch(k, [pltpu.VMEM(shape, value.dtype)] * 2 + [dma((fs // 2,))])
             elif mode[0] == HALF:
-                pieces = mode[2] - mode[1]
-                shape = shape[:2] + (pieces,) + shape[3:]
+                pieces = len(piece_edges(mode))
+                shape = shape[:2] + (mode[2] - mode[1],) + shape[3:]
                 own_scratch(k, [dma((pieces, 2 * fs)), dma((pieces, 2 * fs))])
             self.outs.append(jax.ShapeDtypeStruct(shape, value.dtype))
         if self.hops:
-            self.ins += list(ring.chunks) + list(ring.got)
+            self.ins += [in_hbm(value) for value in ring.chunks + ring.got]
             uses = len(ring.uses)
             shapes = [dma((uses, self.hops)), dma((uses, self.hops)), dma((uses, self.hops, 2))]
             for k, _, _ in ring.uses:
-                shape = ring.chunks[k].shape[2:]
-                self.outs += [jax.ShapeDtypeStruct(shape, bf16)] * self.hops
+                shape = chunk_shape(ring.chunks[k], cs)
+                self.outs += [pltpu.HBM(shape, bf16)] * self.hops
                 shapes.append(pltpu.VMEM((self.hops, 2) + shape, bf16))
             own_scratch(RING, shapes)
 
@@ -318,7 +349,7 @@
                 piece_send, piece_take = self.sems[self.places[k] : self.places[k] + 2]
                 side = lax.rem(ci, 2)
                 across = {CTX: ci + 1 - 2 * side}
-                for q in range(mode[2] - mode[1]):
+                for q, (low, high) in enumerate(piece_edges(mode)):
                     for d in range(1, chips):
                         for b in range(2):
                             to = 2 * lax.rem(chip + d, chips) + lax.rem(core + b, 2)
@@ -326,15 +357,15 @@
                             e = 2 * d + b
                             relay(
                                 self.remote(
-                                    src.at[to, side, mode[1] + q],
-                                    dst.at[fi, side, q],
+                                    src.at[to, side, mode[1] + low : mode[1] + high],
+                                    dst.at[fi, side, low:high],
                                     piece_send.at[q, e],
                                     piece_take.at[q, e],
                                     {FSDP: to},
                                 ),
                                 self.remote(
-                                    dst.at[came, side, q],
-                                    dst.at[came, side, q],
+                                    dst.at[came, side, low:high],
+                                    dst.at[came, side, low:high],
                                     piece_send.at[q, fs + e],
                                     piece_take.at[q, fs + e],
                                     across,
@@ -427,7 +458,9 @@
         k, part, way = self.ring.uses[u]
         send, take, _, buffer, outs = self.ring_refs(u)
         if self.ring.hop + t == 0:
-            source = self.in_refs[len(self.items) + k].at[ring_block(spot - way, cs), part]
+            source = chunk_ref(
+                self.in_refs[len(self.items) + k], ring_block(spot - way, cs), part, cs
+            )
         else:
             source = buffer.at[t, 1]
         return self.remote(
@@ -440,7 +473,9 @@
         _, _, load, buffer, _ = self.ring_refs(u)
         block = ring_block(ring_spot(ci, cs) - way * (self.ring.hop + t + 1), cs)
         return pltpu.make_async_copy(
-            self.in_refs[len(self.items) + k].at[block, part], buffer.at[t, 1], load.at[u, t, 1]
+            chunk_ref(self.in_refs[len(self.items) + k], block, part, cs),
+            buffer.at[t, 1],
+            load.at[u, t, 1],
         )
 
     def load_got(self, u, t):
@@ -733,6 +768,29 @@
         else:
             dk_ref[...] += dk
             dv_ref[...] += dv
+
+
+def rows_matmul(values, weight, swapped=False):
+    count, tokens, depth = values.shape
+    if swapped:
+        tokens, depth = depth, tokens
+    real, width = weight.shape
+
+    def body(value_ref, weight_ref, out_ref):
+        value = value_ref[0].T if swapped else value_ref[0][:, :real]
+        out_ref[0] = jnp.dot(value, weight_ref[...], preferred_element_type=f32).astype(bf16)
+
+    return pl.pallas_call(
+        body,
+        grid=(count,),
+        in_specs=[
+            pl.BlockSpec((1,) + values.shape[1:], lambda r: (r, 0, 0)),
+            pl.BlockSpec(weight.shape, lambda r: (0, 0), pipeline_mode=pl.Buffered(buffer_count=1)),
+        ],
+        out_specs=pl.BlockSpec((1, tokens, width), lambda r: (r, 0, 0)),
+        out_shape=jax.ShapeDtypeStruct((count, tokens, width), bf16),
+        compiler_params=pltpu.CompilerParams(vmem_limit_bytes=24 * MIB),
+    )(values, weight)
 
 
 def rms_norm(values, gain_row):
@@ -865,12 +923,23 @@
 
     def column_chunks(operand, partner, parts=1):
         cols = partner.shape[1] // fs
-        pieces = jnp.stack([partner[:, j * cols : (j + 1) * cols] for j in range(fs)])
-        grad = jnp.einsum("tr,jtn->jrn", operand, pieces, preferred_element_type=f32)
-        return grad.astype(bf16).reshape(cs, parts, operand.shape[1] // halves // parts, cols)
+        wide = jnp.concatenate(
+            [
+                pad_last(partner[:, j * cols : (j + 1) * cols], ceil_to(cols, 128))
+                for j in range(fs)
+            ],
+            axis=1,
+        )
+        grad = dense_tn(operand, wide).astype(bf16)
+        return grad.reshape(halves, parts, -1, grad.shape[1])
+
+    def by_rows(value):
+        return value.astype(bf16).reshape(fs, tok, -1)
+
+    blocks = 25
 
     def in_blocks(value):
-        return value.reshape(fs, 2, 5, value.shape[1] // 10, value.shape[2])
+        return value.reshape(fs, 2, blocks, value.shape[1] // (2 * blocks), value.shape[2])
 
     mi_send = column_parts(w_mamba_in, 2, fs, chan_p)
     qkv_send = column_parts(w_qkv, 1, fs, w_qkv.shape[1] // fs)
@@ -882,7 +951,6 @@
     meta_f, meta_pull = jax.vjp(rms_norm, meta_rows, gain_rows[0])
     meta_low = meta_f.astype(bf16)
 
-    blocks = 5
     normed_all, seg_all, mi_w, qkv_w = exchange(
         0,
         [
@@ -892,7 +960,7 @@
             (in_blocks(qkv_send), (HALF, 0, blocks), WEIGHTS),
         ],
     )
-    gu_send = in_blocks(column_parts(w_gate_up, 2, fs, ffw_p))
+    gu_send = in_hbm(in_blocks(column_parts(w_gate_up, 2, fs, ffw_p)))
     mi_w = mi_w.reshape(dim, 2 * chan_p)
     qkv_w = qkv_w.reshape(dim, -1)
     seg_all = seg_all.reshape(fs, row_len)
@@ -920,7 +988,7 @@
         [
             (keyval, NEXT, CTX),
             (meta_own, ALL, CTX),
-            (gu_send, (HALF, 0, 1), WEIGHTS),
+            (gu_send, (HALF, 0, 5), WEIGHTS),
         ],
         reach=reach,
     )
@@ -995,7 +1063,7 @@
         [
             (last_state.astype(bf16), NEXT, CTX),
             (step_sum, ALL, CTX),
-            (gu_send, (HALF, 2, 4), WEIGHTS),
+            (gu_send, (HALF, 10, 19), WEIGHTS),
         ],
         reach=reach,
     )
@@ -1022,7 +1090,7 @@
     gate_s = jax.nn.sigmoid(gate_z)
     gate_silu = gate_z * gate_s
     mixture_low = (pre_mix * gate_silu).astype(bf16).reshape(fs * tok, chan_p)
-    ssm_part = dense(mixture_low, mo_w).astype(bf16).reshape(fs, tok, dim)
+    ssm_part = rows_matmul(mixture_low.reshape(fs, tok, chan_p), w_mamba_out)
 
     key_span = (reach + 1) * tok
     padded_seg = jnp.concatenate([jnp.full((reach * tok,), -1, jnp.int32), seg_row])
@@ -1054,7 +1122,7 @@
         ],
         (queries, key_rows, key_rows, bias),
         16,
-        Traffic([(gu_send, (HALF, 1, 2), WEIGHTS)]),
+        Traffic([(gu_send, (HALF, 5, 10), WEIGHTS)]),
         12 * MIB,
     )
     wide = heads_dim // fs
@@ -1062,12 +1130,12 @@
         5,
         [
             (attended.reshape(fs, wide, tok), EACH, FSDP),
-            (gu_send, (HALF, 4, 5), WEIGHTS),
+            (gu_send, (HALF, 19, 25), WEIGHTS),
         ],
     )
     gu_w = jnp.concatenate([gu_0, gu_1, gu_2, gu_3], axis=2).reshape(dim, 2 * ffw_p)
     att_tp = jnp.swapaxes(att_got, 1, 2).reshape(fs * tok, wide)
-    attn_part = dense(att_tp, w_attn_out).astype(bf16).reshape(fs, tok, dim)
+    attn_part = rows_matmul(att_got, w_attn_out, True)
     attn_got, ssm_got = exchange(
         6, [(attn_part, REDUCE, FSDP), (ssm_part, REDUCE, FSDP)]
     )
@@ -1087,8 +1155,9 @@
     hidden_f, glu_pull = jax.vjp(
         lambda values: jax.nn.silu(values[:, :ffw_p]) * values[:, ffw_p:], gate_up
     )
-    hidden = hidden_f.astype(bf16)[:, :ffw]
-    down_part = dense(hidden, w_ffn_down).astype(bf16).reshape(fs, tok, dim)
+    hidden_wide = hidden_f.astype(bf16)
+    hidden = hidden_wide[:, :ffw]
+    down_part = rows_matmul(hidden_wide.reshape(fs, tok, ffw_p), w_ffn_down)
     hidden_grad = pad_last(dense_nt(cot_all, w_ffn_down), ffw_p)
     gate_up_grad = glu_pull(hidden_grad)[0].astype(bf16)
     ring_one = Ring(
@@ -1100,7 +1169,7 @@
         [(0, 0, 1), (1, 0, -1), (2, 0, 1), (2, 1, -1)],
     )
     hops = spread_hops([1, 1, 1, 1, 2, 1])
-    ffn_back = dense_nt(gate_up_grad, gu_w).astype(bf16).reshape(fs, tok, dim)
+    ffn_back = by_rows(dense_nt(gate_up_grad, gu_w))
     (back_got,) = exchange(8, [(ffn_back, REDUCE, FSDP)], ring_one, hops[0])
     resid_part, gain_ffn_grad = ffn_norm_pull(jnp.sum(back_got.astype(f32), axis=0))
     residual_grad = cotangent[0].astype(f32) + resid_part
@@ -1197,9 +1266,9 @@
             row_chunks(normed_all, gate_low),
             qkv_full.astype(bf16).reshape(cs, 1, dim // cs, qkv_w.shape[1]),
             column_chunks(att_tp, attn_proj_low),
-            column_chunks(mixture_low[:, :chan], ssm_proj_low, 2),
-        ],
-        [(0, 0, 1), (1, 0, -1), (2, 0, -1), (3, 0, 1), (3, 1, -1)],
+            column_chunks(mixture_low[:, :chan], ssm_proj_low),
+        ],
+        [(0, 0, 1), (1, 0, 1), (2, 0, -1), (3, 0, -1)],
     )
     hops = spread_hops([1, 2, 2, 2])
     gate_sum, up_sum, down_top, down_low = ring_one.finish()
@@ -1300,13 +1369,17 @@
     token_back = jnp.einsum("fct,dc->ftd", qkv_grad_tp, qkv_w, preferred_element_type=f32)
     token_back = token_back + dense_nt(mamba_in_grad, mi_w).reshape(fs, tok, dim)
     meta_back_rows = jnp.einsum("fmc,dc->fmd", meta_grad_tp, qkv_w, preferred_element_type=f32)
-    normed_back = jnp.concatenate([token_back.astype(bf16), meta_back_rows.astype(bf16)], axis=1)
+    token_back = by_rows(token_back)
     hops = spread_hops([3, 2, 2])
-    (normed_got,) = exchange(15, [(normed_back, REDUCE, FSDP)], ring_three, hops[0])
-    normed_grad = jnp.sum(normed_got.astype(f32), axis=0)
-    source_part, gain_in_grad = norm_pull(normed_grad[:tok])
+    token_got, meta_rows_got = exchange(
+        15,
+        [(token_back, REDUCE, FSDP), (meta_back_rows.astype(bf16), REDUCE, FSDP)],
+        ring_three,
+        hops[0],
+    )
+    source_part, gain_in_grad = norm_pull(jnp.sum(token_got.astype(f32), axis=0))
     source_grad = residual_grad + source_part
-    meta_grad, gain_in_meta = meta_pull(normed_grad[tok:])
+    meta_grad, gain_in_meta = meta_pull(jnp.sum(meta_rows_got.astype(f32), axis=0))
     embed_part = jnp.concatenate(
         [
             meta_grad,
@@ -1329,7 +1402,7 @@
     embed_total = jnp.concatenate(
         [embed_got[:, :metas].reshape(META, dim), jnp.sum(embed_got[:, metas:], axis=0)], axis=0
     )
-    gate_half, qkv_gradient, attn_sum, out_top, out_low = ring_two.finish()
+    gate_half, qkv_gradient, attn_sum, mamba_out_sum = ring_two.finish()
     inner_a, inner_b, proj_sum = ring_three.finish()
     mamba_in_sum, attn_sum, mamba_out_sum, proj_sum, vec_all = exchange(
         23,
@@ -1340,7 +1413,7 @@
                 FSDP,
             ),
             (attn_sum.astype(bf16), CROSS, BOTH),
-            (jnp.concatenate([out_top, out_low], axis=0).astype(bf16), CROSS, BOTH),
+            (mamba_out_sum.astype(bf16), CROSS, BOTH),
             (proj_sum.astype(bf16), CROSS, BOTH),
             (vec_part, GATHER, FSDP),
         ],
@@ -1348,10 +1421,10 @@
     ssm_total = jnp.concatenate([vec_all[j, :, :chan] for j in range(fs)], axis=1)
     gate_up_gradient = unpaired(gate_up_sum, ffw)
     mamba_in_gradient = unpaired(mamba_in_sum, chan)
-    ffn_down_gradient = down_sum.astype(f32)
-    attn_gradient = attn_sum.astype(f32)
-    mamba_out_gradient = mamba_out_sum.astype(f32)
-    ssm_proj_gradient = proj_sum.astype(f32)
+    ffn_down_gradient = down_sum[:, : dim // fs].astype(f32)
+    attn_gradient = attn_sum[:, : dim // fs].astype(f32)
+    mamba_out_gradient = mamba_out_sum[:, : dim // fs].astype(f32)
+    ssm_proj_gradient = proj_sum[:, : w_ssm_proj.shape[1] // fs].astype(f32)
 
     def adam_block(gradient, moments_old, weight):
         return adam_step(gradient, moments_old, weight.astype(f32))

time: 1230 us -> 1100 us (0.89)
  local copies, waits for them, and re-layouts: 259 us -> 130 us
    unnamed x635 -> x475, local copies, waits for them, and re-layouts: 146 us -> 63.9 us
    convert_element_type x7 -> x1, local copies, waits for them, and re-layouts: 38.4 us -> 3.55 us  [by_rows(): return value.astype(bf16).reshape(fs, tok, -1)]
    dot_general x5 -> x9, matrix products: 17.9 us -> 35.7 us  [dense_tn(): lax.dot_general(operand, partner, (((0,), (0,)), ((), ())), preferred_ele...]
  transfers between devices with their start and end apart: 3 -> 3, of which waited for: 0 -> 0; matrix products, arithmetic and copies ran while one was open for 11% -> 12% of each run, Pallas kernels for 16% -> 18%
where the time goes in v3:
time: 1100 us; the launch traced here: 1090 us
  Pallas kernels  756 us (69%)
  local copies, waits for them, and re-layouts  130 us (12%)
  other arithmetic  110 us (10%)
  matrix products  79.5 us (7%)
    pallas_call x19, Pallas kernels, exchange(): pl.pallas_call(body, out_shape=tuple(plan.outs), in_specs=[ANY] * ins, ou...  578 us
    pallas_call x6, Pallas kernels, hosted_call(): pl.pallas_call(hosted, grid=grid, in_specs=in_specs + [ANY] * x_in, out_s...  171 us
    unnamed x475, local copies, waits for them, and re-layouts  63.9 us
    dot_general x9, matrix products, dense_tn(): lax.dot_general(operand, partner, (((0,), (0,)), ((), ())), preferred_ele...  35.7 us
    mul x9, other arithmetic, adam_step(): return (second_moment, -learn_rate * (corrected + decay_rate * weight_now))  23.1 us
  transfers between devices with their start and end apart: 3, of which 0 were waited for; matrix products, arithmetic and copies ran while one was open for 12% of the time, Pallas kernels for 18%

profile of v3, /device:TPU:2, one launch (start us, length us, event | category | flops | bytes accessed | tf_op | source)
XLA Modules:
  0.0 1089.9 jit_solution(2144674750398253426)
XLA Ops:
  3.8 5.1 fusion.314
  14.0 61.9 %shard_map.428 = (bf16[4,128,1600]{2,1,0:T(8,128)(2,1)S(1)}, s32[4,1,1024]{2,1,0:T(1,128)S(1)}, bf16[4,2,25,8,1792]{4,3,2,1,0:T(8,128)(2,1)S(1)}, bf16[4,2,25,8,560]{4,3,2,1,0:T(8,128)(2,1)S(1)}) custom-call(bf16[128,1600]{1,0:T(8,128)(2,1)S(1)} %fusion.164.refs_0_, s32[1,1024]{1,0:T(1,128)S(1)} %copy-done.69, ...), custom_call_target="tpu_custom_call" | custom-call | tf_op jit(solution)/shard_map/pallas_call | solution.py:543
  85.8 7.2 fusion.313
  101.0 10.5 shard_map.429
  114.8 4.3 pad_maximum_fusion.refs_2_.refs_4_.refs_1_
  119.1 20.6 %shard_map.430 = (bf16[4,640,128]{2,1,0:T(8,128)(2,1)S(1)}, bf16[8,16,640]{2,1,0:T(8,128)(2,1)S(1)}, bf16[4,2,5,8,2816]{4,3,2,1,0:T(8,128)(2,1)S(1)}) custom-call(bf16[640,128]{1,0:T(8,128)(2,1)S(1)} %slice.635.refs_0_, bf16[16,640]{1,0:T(8,128)(2,1)S(1)} %pad_maximum_fusion.16.refs_1_, bf16[4,2,25,8,2816]{4,3,2,1,0:T(8,128)(2,1)} %pad_maximum_fusion.refs_2_.refs_4_.refs_1_), custom_call_target="tpu_custom_call" | custom-call | tf_op jit(solution)/shard_map/pallas_call | solution.py:543
  156.5 5.3 copy.186
  164.0 7.1 copy.177.weight_ref
  171.1 26.3 %shard_map.431 = (bf16[1600,128]{1,0:T(8,128)(2,1)S(1)}, f32[5,5,128]{2,1,0:T(8,128)S(1)}, bf16[4,2,5,8,2816]{4,3,2,1,0:T(8,128)(2,1)S(1)}) custom-call(bf16[1600,128]{1,0:T(8,128)(2,1)S(1)} %slice.634.refs_0_, bf16[640,768]{1,0:T(8,128)(2,1)S(1)} %constant_dynamic-update-slice_fusion.refs_1_.refs_2_, ...), custom_call_target="tpu_custom_call" | custom-call | tf_op jit(solution)/shard_map/pallas_call | solution.py:677
  198.6 24.4 %shard_map.432 = (bf16[4,400,128]{2,1,0:T(8,128)(2,1)S(1)}, bf16[4,2,6,8,2816]{4,3,2,1,0:T(8,128)(2,1)S(1)}) custom-call(bf16[4,400,128]{2,1,0:T(8,128)(2,1)S(1)} %bitcast.535, bf16[4,2,25,8,2816]{4,3,2,1,0:T(8,128)(2,1)} %pad_maximum_fusion.refs_2_.refs_4_.refs_1_), custom_call_target="tpu_custom_call" | custom-call | tf_op jit(solution)/shard_map/pallas_call | solution.py:543
  239.5 5.8 fusion.297
  246.8 26.2 %shard_map.434 = (f32[4,132,512]{2,1,0:T(8,128)S(1)}, bf16[200,400]{1,0:T(8,128)(2,1)S(1)}, bf16[400,58]{1,0:T(8,128)(2,1)S(1)}) custom-call(f32[132,512]{1,0:T(8,128)S(1)} %fusion.201.refs_0_, bf16[200,400]{1,0:T(8,128)(2,1)S(1)} %dynamic_slice.104.refs_1_, bf16[400,58]{1,0:T(8,128)(2,1)S(1)} %dynamic_slice.105.refs_2_), custom_call_target="tpu_custom_call" | custom-call | tf_op jit(solution)/shard_map/pallas_call | solution.py:543
  277.3 3.7 fusion.312
  282.3 20.8 %shard_map.435 = (f32[4,16,896]{2,1,0:T(8,128)S(1)}, bf16[400,400]{1,0:T(8,128)(2,1)S(1)}) custom-call(f32[4,128,896]{2,1,0:T(8,128)S(1)} %get-tuple-element.430.refs_0_, f32[4,128,896]{2,1,0:T(8,128)S(1)} %get-tuple-element.465.refs_1_, f32[4,128,16,128]{3,2,1,0:T(8,128)S(1)} %broadcast_in_dim.186.refs_2_.refs_3_, ...), custom_call_target="tpu_custom_call" | custom-call | tf_op jit(solution)/shard_map/pallas_call | solution.py:677
  303.1 28.6 %shard_map.436 = (bf16[4,4,16,896]{3,2,1,0:T(8,128)(2,1)S(1)}, f32[8,4,896]{2,1,0:T(4,128)S(1)}, bf16[4,2,9,8,2816]{4,3,2,1,0:T(8,128)(2,1)S(1)}) custom-call(bf16[4,16,896]{2,1,0:T(8,128)(2,1)S(1)} %convert_element_type.425.refs_0_, f32[4,896]{1,0:T(4,128)S(1)} %get-tuple-element.429.refs_1_, ...), custom_call_target="tpu_custom_call" | custom-call | tf_op jit(solution)/shard_map/pallas_call | solution.py:543
  333.9 36.8 %shard_map.437 = (f32[4,128,896]{2,1,0:T(8,128)S(1)}, f32[4,128,16,896]{3,2,1,0:T(8,128)}, bf16[688,400]{1,0:T(8,128)(2,1)S(1)}) custom-call(f32[4,128,896]{2,1,0:T(8,128)S(1)} %get-tuple-element.430.refs_0_, f32[4,128,896]{2,1,0:T(8,128)S(1)} %get-tuple-element.465.refs_1_, f32[4,128,16,128]{3,2,1,0:T(8,128)S(1)} %broadcast_in_dim.186.refs_2_.refs_3_, ...), custom_call_target="tpu_custom_call" | custom-call | tf_op jit(solution)/shard_map/pallas_call | solution.py:677
  376.0 23.6 %shard_map.439 = (bf16[2,128,1600]{2,1,0:T(8,128)(2,1)S(1)}, bf16[2,128,1600]{2,1,0:T(8,128)(2,1)S(1)}) custom-call(bf16[4,128,1600]{2,1,0:T(8,128)(2,1)S(1)} %copy-done.15, bf16[4,128,1600]{2,1,0:T(8,128)(2,1)S(1)} %shard_map.438.refs_1_), custom_call_target="tpu_custom_call" | custom-call | tf_op jit(solution)/shard_map/pallas_call | solution.py:543
  401.8 23.3 %shard_map.440 = (bf16[4,128,1600]{2,1,0:T(8,128)(2,1)S(1)}, bf16[4,128,1600]{2,1,0:T(8,128)(2,1)S(1)}) custom-call(bf16[128,1600]{1,0:T(8,128)(2,1)S(1)} %multiply_convert_fusion.3.refs_0_, bf16[128,1600]{1,0:T(8,128)(2,1)S(1)} %bitcast.516), custom_call_target="tpu_custom_call" | custom-call | tf_op jit(solution)/shard_map/pallas_call | solution.py:543
  430.0 5.4 fusion.327
  438.3 6.1 convolution_convert_fusion.5
  444.4 4.9 convolution_convert_fusion.2
  449.3 4.9 convolution_convert_fusion.1
  456.0 3.5 copy.180
  460.6 7.4 convolution_convert_fusion
  468.1 23.9 %shard_map.441 = (bf16[2,128,1600]{2,1,0:T(8,128)(2,1)S(1)}, bf16[200,1408]{1,0:T(8,128)(2,1)}, bf16[200,1408]{1,0:T(8,128)(2,1)}, bf16[344,512]{1,0:T(8,128)(2,1)}, bf16[344,512]{1,0:T(8,128)(2,1)}) custom-call(bf16[4,128,1600]{2,1,0:T(8,128)(2,1)S(1)} %bitcast.517, bf16[8,1,200,1408]{3,2,1,0:T(8,128)(2,1)} %bitcast.553, ...), custom_call_target="tpu_custom_call" | custom-call | tf_op jit(solution)/shard_map/pallas_call | solution.py:543
  495.6 26.5 %shard_map.442 = (bf16[4,128,1600]{2,1,0:T(8,128)(2,1)S(1)}, bf16[4,128,1600]{2,1,0:T(8,128)(2,1)S(1)}, bf16[200,1408]{1,0:T(8,128)(2,1)}, bf16[200,1408]{1,0:T(...) custom-call(bf16[128,1600]{1,0:T(8,128)(2,1)S(1)} %get-tuple-element.491.refs_0_, ...), custom_call_target="tpu_custom_call" | custom-call | tf_op jit(solution)/shard_map/pallas_call | solution.py:543
  528.0 25.0 %shard_map.443 = (bf16[4,400,128]{2,1,0:T(8,128)(2,1)S(1)}, bf16[200,1408]{1,0:T(8,128)(2,1)}, bf16[200,1408]{1,0:T(8,128)(2,1)}, bf16[344,512]{1,0:T(8,128)(2,1)}, bf16[344,512]{1,0:T(8,128)(2,1)}) custom-call(bf16[4,400,128]{2,1,0:T(8,128)(2,1)S(1)} %fusion.130.refs_0_, bf16[8,1,200,1408]{3,2,1,0:T(8,128)(2,1)} %bitcast.555, ...), custom_call_target="tpu_custom_call" | custom-call | tf_op jit(solution)/shard_map/pallas_call | solution.py:543
  553.0 25.0 %shard_map.444 = (bf16[1600,128]{1,0:T(8,128)(2,1)S(1)}, f32[320,768]{1,0:T(8,128)S(1)}, f32[320,768]{1,0:T(8,128)S(1)}, bf16[2,200,896]{2,1,0:T(8,128)(2,1)S(1)...) custom-call(bf16[1600,128]{1,0:T(8,128)(2,1)S(1)} %copy-done.19, ...), custom_call_target="tpu_custom_call" | custom-call | tf_op jit(solution)/shard_map/pallas_call | solution.py:677
  585.3 3.6 shard_map.445.refs_2_
  589.1 69.2 %shard_map.446 = (bf16[4,640,128]{2,1,0:T(8,128)(2,1)S(1)}, bf16[8,16,640]{2,1,0:T(8,128)(2,1)S(1)}, bf16[2,128,1600]{2,1,0:T(8,128)(2,1)S(1)}, bf16[200,1408]{1...) custom-call(bf16[4,640,128]{2,1,0:T(8,128)(2,1)S(1)} %pad_maximum_fu, ...), custom_call_target="tpu_custom_call" | custom-call | tf_op jit(solution)/shard_map/pallas_call | solution.py:543
  663.4 25.4 %shard_map.447 = (bf16[4,560,128]{2,1,0:T(8,128)(2,1)S(1)}, bf16[4,16,560]{2,1,0:T(8,128)(2,1)S(1)}, bf16[200,1408]{1,0:T(8,128)(2,1)}, bf16[200,1408]{1,0:T(8,1...) custom-call(bf16[4,560,128]{2,1,0:T(8,128)(2,1)S(1)} %bitcast.527, ...), custom_call_target="tpu_custom_call" | custom-call | tf_op jit(solution)/shard_map/pallas_call | solution.py:543
  691.3 4.9 multiply_reduce_fusion
  698.7 3.7 bitcast_convert_fusion
  706.5 3.8 copy.190
  715.5 4.9 convolution_convert_fusion.3
  720.5 17.6 %shard_map.448 = (f32[4,16,896]{2,1,0:T(8,128)S(1)}, bf16[2,200,1408]{2,1,0:T(8,128)(2,1)S(1)}, bf16[200,896]{1,0:T(8,128)(2,1)}, bf16[200,560]{1,0:T(8,128)(2,1...) custom-call(f32[4,128,896]{2,1,0:T(8,128)S(1)} %get-tuple-element.430.refs_0_, f32[4,128,896]{2,1,0:T(8,128)S(1)} %copy-done.6, ...), custom_call_target="tpu_custom_call" | custom-call | tf_op jit(solution)/shard_map/pallas_call | solution.py:677
  743.5 46.1 %shard_map.449 = (bf16[4,4,16,896]{3,2,1,0:T(8,128)(2,1)S(1)}, bf16[2,200,1408]{2,1,0:T(8,128)(2,1)S(1)}, bf16[200,896]{1,0:T(8,128)(2,1)}, bf16[200,896]{1,0:T(...) custom-call(bf16[4,16,896]{2,1,0:T(8,128)(2,1)S(1)} %convert_element, ...), custom_call_target="tpu_custom_call" | custom-call | tf_op jit(solution)/shard_map/pallas_call | solution.py:543
  790.9 43.9 %shard_map.450 = (f32[4,128,896]{2,1,0:T(8,128)S(1)}, f32[4,128,896]{2,1,0:T(8,128)S(1)}, f32[4,128,16,128]{3,2,1,0:T(8,128)}, f32[4,128,16,128]{3,2,1,0:T(8,128...) custom-call(f32[4,128,896]{2,1,0:T(8,128)S(1)} %get-tuple-element.43, ...), custom_call_target="tpu_custom_call" | custom-call | tf_op jit(solution)/shard_map/pallas_call | solution.py:677
  844.4 4.3 fusion.307
  849.6 33.4 %shard_map.451 = (f32[4,132,512]{2,1,0:T(8,128)S(1)}, bf16[200,896]{1,0:T(8,128)(2,1)}, bf16[200,896]{1,0:T(8,128)(2,1)}, bf16[200,560]{1,0:T(8,128)(2,1)}, bf16...) custom-call(f32[132,512]{1,0:T(8,128)S(1)} %pad_maximum_fusion.13.re, ...), custom_call_target="tpu_custom_call" | custom-call | tf_op jit(solution)/shard_map/pallas_call | solution.py:543
  885.5 6.6 multiply_reduce_fusion.3
  902.4 5.3 collective-permute-start.2
  910.0 4.9 fusion.40
  931.4 28.0 %shard_map.452 = (bf16[2,128,1600]{2,1,0:T(8,128)(2,1)S(1)}, bf16[2,16,1600]{2,1,0:T(8,128)(2,1)S(1)}, bf16[200,512]{1,0:T(8,128)(2,1)}, bf16[200,512]{1,0:T(8,1...) custom-call(bf16[4,128,1600]{2,1,0:T(8,128)(2,1)S(1)} %copy.194.refs, ...), custom_call_target="tpu_custom_call" | custom-call | tf_op jit(solution)/shard_map/pallas_call | solution.py:543
  963.1 18.3 %shard_map.453 = (f32[4,20,1600]{2,1,0:T(8,128)S(1)}, bf16[200,512]{1,0:T(8,128)(2,1)}, bf16[200,512]{1,0:T(8,128)(2,1)}, bf16[200,384]{1,0:T(8,128)(2,1)}, bf16...) custom-call(f32[20,1600]{1,0:T(8,128)S(1)} %concatenate.138.refs_0_, ...), custom_call_target="tpu_custom_call" | custom-call | tf_op jit(solution)/shard_map/pallas_call | solution.py:543
  981.4 27.4 %shard_map.454 = (bf16[8,20,1600]{2,1,0:T(8,128)(2,1)S(1)}, bf16[8,22,896]{2,1,0:T(8,128)(2,1)S(1)}, bf16[200,512]{1,0:T(8,128)(2,1)}, bf16[200,512]{1,0:T(8,128...) custom-call(bf16[20,1600]{1,0:T(8,128)(2,1)S(1)} %reduce_sum.441.ref, ...), custom_call_target="tpu_custom_call" | custom-call | tf_op jit(solution)/shard_map/pallas_call | solution.py:543
  1019.8 35.6 %shard_map.455 = (bf16[2,200,896]{2,1,0:T(8,128)(2,1)S(1)}, bf16[200,512]{1,0:T(8,128)(2,1)S(1)}, bf16[400,512]{1,0:T(8,128)(2,1)S(1)}, bf16[400,128]{1,0:T(8,128)(2,1)S(1)}, f32[4,22,896]{2,1,0:T(8,128)S(1)}) custom-call(bf16[2,200,896]{2,1,0:T(8,128)(2,1)S(1)} %pad_maximum_fusion.9.refs_0_, bf16[200,512]{1,0:T(8,128)(2,1)S(1)} %fusion.206.refs_1_, ...), custom_call_target="tpu_custom_call" | custom-call | tf_op jit(solution)/shard_map/pallas_call | solution.py:543
  1081.2 3.8 fusion.114
  (670 shorter events, 220.5 us)
Async XLA Ops:
  3.0 96.6 %copy-start.143 = (f32[1600]{0:T(1024)}, f32[1600]{0:T(1024)S(1)}, u32[]{:S(2)}) copy-start(f32[1600]{0:T(1024)S(1)} %get-tuple-element.388) | copy-start | bytes 19204
  3.1 397.2 %copy-start.161 = (f32[1600]{0:T(1024)}, f32[1600]{0:T(1024)S(1)}, u32[]{:S(2)}) copy-start(f32[1600]{0:T(1024)S(1)} %get-tuple-element.386) | copy-start | bytes 19204
  3.1 397.2 %copy-start.163 = (f32[1600]{0:T(1024)}, f32[1600]{0:T(1024)S(1)}, u32[]{:S(2)}) copy-start(f32[1600]{0:T(1024)S(1)} %get-tuple-element.387) | copy-start | bytes 19204
  75.9 23.7 %copy-start.9 = (bf16[4,2,25,8,560]{4,3,2,1,0:T(8,128)(2,1)}, bf16[4,2,25,8,560]{4,3,2,1,0:T(8,128)(2,1)S(1)}, u32[]{:S(2)}) copy-start(bf16[4,2,25,8,560]{4,3,2,1,0:T(8,128)(2,1)S(1)} %get-tuple-element.142) | copy-start | bytes 5376004
  81.3 158.2 %collective-permute-start = (f32[4,3,896]{2,1,0:T(4,128)}, f32[4,3,896]{2,1,0:T(4,128)}, u32[]{:S(2)}, u32[]{:S(2)}) collective-permute-start(f32[4,3,896]{2,1,0:T(4,128)} %slice.640), channel_id=1, source_target_pairs={{0,1},{1,2},{2,3},{3,4},{4,5},{5,6},{6,7},{8,9},{9,10},{10,11},{11... | collective-permute-start | bytes 129032 | tf_op jit(solution)/shard_map/ppermute | solution.py:1010
  141.8 29.3 %copy-start.22 = (f32[768,128]{1,0:T(8,128)}, f32[768,128]{1,0:T(8,128)S(1)}, u32[]{:S(2)}) copy-start(f32[768,128]{1,0:T(8,128)S(1)} %pad_select_fusion.refs_3_) | copy-start | bytes 1179652
  153.4 86.1 %copy-start.198 = (pred[4,128]{1,0:T(4,128)(4,1)}, pred[4,128]{1,0:T(4,128)(4,1)S(1)}, u32[]{:S(2)}) copy-start(pred[4,128]{1,0:T(4,128)(4,1)S(1)} %get-tuple-element.522) | copy-start | bytes 1540
  153.4 86.1 %copy-start.200 = (pred[4,128]{1,0:T(4,128)(4,1)}, pred[4,128]{1,0:T(4,128)(4,1)S(1)}, u32[]{:S(2)}) copy-start(pred[4,128]{1,0:T(4,128)(4,1)S(1)} %get-tuple-element.523) | copy-start | bytes 1540
  153.4 86.1 %copy-start.202 = (pred[4,128]{1,0:T(4,128)(4,1)}, pred[4,128]{1,0:T(4,128)(4,1)S(1)}, u32[]{:S(2)}) copy-start(pred[4,128]{1,0:T(4,128)(4,1)S(1)} %get-tuple-element.524) | copy-start | bytes 1540
  156.5 117.3 %copy-start.117 = (bf16[800,100]{1,0:T(8,128)(2,1)}, bf16[800,100]{1,0:T(8,128)(2,1)S(1)}, u32[]{:S(2)}) copy-start(bf16[800,100]{1,0:T(8,128)(2,1)S(1)} %slice.528) | copy-start | bytes 480004
  198.6 25.7 %copy-start.38 = (bf16[400,1600]{1,0:T(8,128)(2,1)S(1)}, bf16[400,1600]{1,0:T(8,128)(2,1)}, u32[]{:S(2)}) copy-start(bf16[400,1600]{1,0:T(8,128)(2,1)} %weight_ref.3) | copy-start | bytes 3840004
  239.5 37.8 %copy-start.168 = (f32[896]{0:T(1024)}, f32[896]{0:T(1024)S(1)}, u32[]{:S(2)}) copy-start(f32[896]{0:T(1024)S(1)} %get-tuple-element.395) | copy-start | bytes 10756
  280.9 52.9 %copy-start.3 = (f32[4,128,896]{2,1,0:T(8,128)}, f32[4,128,896]{2,1,0:T(8,128)S(1)}, u32[]{:S(2)}) copy-start(f32[4,128,896]{2,1,0:T(8,128)S(1)} %get-tuple-element.465.refs_1_) | copy-start | bytes 5505028
  282.3 51.6 %copy-start.2 = (f32[4,128,16,128]{3,2,1,0:T(8,128)}, f32[4,128,16,128]{3,2,1,0:T(8,128)S(1)}, u32[]{:S(2)}) copy-start(f32[4,128,16,128]{3,2,1,0:T(8,128)S(1)} %broadcast_in_dim.186.refs_2_.refs_3_) | copy-start | bytes 12582916
  303.1 28.7 %copy-start.58 = (bf16[400,400]{1,0:T(8,128)(2,1)}, bf16[400,400]{1,0:T(8,128)(2,1)S(1)}, u32[]{:S(2)}) copy-start(bf16[400,400]{1,0:T(8,128)(2,1)S(1)} %get-tuple-element.248) | copy-start | bytes 960004
  303.1 29.6 %copy-start.130 = (f32[512,16]{1,0:T(8,128)S(1)}, f32[512,16]{1,0:T(8,128)}, u32[]{:S(2)}) copy-start(f32[512,16]{1,0:T(8,128)} %copy.224) | copy-start | bytes 98308
  333.9 36.9 %copy-start = (f32[4,128,16,128]{3,2,1,0:T(8,128)}, f32[4,128,16,128]{3,2,1,0:T(8,128)S(1)}, u32[]{:S(2)}) copy-start(f32[4,128,16,128]{3,2,1,0:T(8,128)S(1)} %broadcast_in_dim.188.refs_3_.refs_2_.refs_4_) | copy-start | bytes 12582916
  333.9 36.9 %copy-start.70 = (f32[4,128,896]{2,1,0:T(8,128)S(1)}, f32[4,128,896]{2,1,0:T(8,128)}, u32[]{:S(2)}) copy-start(f32[4,128,896]{2,1,0:T(8,128)} %get-tuple-element.432) | copy-start | bytes 5505028
  333.9 36.9 %copy-start.87 = (f32[4,128,1792]{2,1,0:T(8,128)S(1)}, f32[4,128,1792]{2,1,0:T(8,128)}, u32[]{:S(2)}) copy-start(f32[4,128,1792]{2,1,0:T(8,128)} %copy-done.86) | copy-start | bytes 11010052
  333.9 36.9 %copy-start.183 = (f32[896]{0:T(1024)S(1)}, f32[896]{0:T(1024)}, u32[]{:S(2)}) copy-start(f32[896]{0:T(1024)} %get-tuple-element.391) | copy-start | bytes 10756
  376.0 49.1 %slice-start.4 = ((s8[4505600]{0:T(1024)(128)(4,1)}), s8[311296]{0:T(1024)(128)(4,1)S(1)}, s32[]{:S(2)}) async-start(s8[4505600]{0:T(1024)(128)(4,1)} %bitcast.612), calls=%async_computation.4 | async-start | bytes 622592
  400.0 95.2 %copy-start.189 = (f32[128]{0:T(128)}, f32[128]{0:T(128)S(1)}, u32[]{:S(2)}) copy-start(f32[128]{0:T(128)S(1)} %fusion.272) | copy-start | bytes 1540
  400.0 25.2 %slice-start.5 = ((s8[4505600]{0:T(1024)(128)(4,1)}), s8[4194304]{0:T(1024)(128)(4,1)S(1)}, s32[]{:S(2)}) async-start(s8[4505600]{0:T(1024)(128)(4,1)} %bitcast.612), calls=%async_computation.5 | async-start | bytes 8388608
  401.1 94.1 %copy-start.191 = (f32[128]{0:T(128)}, f32[128]{0:T(128)S(1)}, u32[]{:S(2)}) copy-start(f32[128]{0:T(128)S(1)} %fusion.271) | copy-start | bytes 1540
  401.6 91.4 %copy-start.193 = (f32[128]{0:T(128)}, f32[128]{0:T(128)S(1)}, u32[]{:S(2)}) copy-start(f32[128]{0:T(128)S(1)} %fusion.273) | copy-start | bytes 1540
  425.1 29.0 %copy-start.28 = (bf16[4,128,1600]{2,1,0:T(8,128)(2,1)}, bf16[4,128,1600]{2,1,0:T(8,128)(2,1)S(1)}, u32[]{:S(2)}) copy-start(bf16[4,128,1600]{2,1,0:T(8,128)(2,1)S(1)} %get-tuple-element.165) | copy-start | bytes 4915204
  468.1 24.1 %copy-start.84 = (f32[128,1600]{1,0:T(8,128)S(1)}, f32[128,1600]{1,0:T(8,128)}, u32[]{:S(2)}) copy-start(f32[128,1600]{1,0:T(8,128)} %copy-done.83) | copy-start | bytes 2457604
  495.6 26.6 %copy-start.39 = (bf16[400,1600]{1,0:T(8,128)(2,1)S(1)}, bf16[400,1600]{1,0:T(8,128)(2,1)}, u32[]{:S(2)}) copy-start(bf16[400,1600]{1,0:T(8,128)(2,1)} %weight_ref.3) | copy-start | bytes 3840004
  528.0 25.0 %copy-start.19 = (bf16[1600,128]{1,0:T(8,128)(2,1)S(1)}, bf16[1600,128]{1,0:T(8,128)(2,1)}, u32[]{:S(2)}) copy-start(bf16[1600,128]{1,0:T(8,128)(2,1)} %copy-done.18) | copy-start | bytes 1228804
  528.0 25.0 %copy-start.23 = (f32[768,128]{1,0:T(8,128)S(1)}, f32[768,128]{1,0:T(8,128)}, u32[]{:S(2)}) copy-start(f32[768,128]{1,0:T(8,128)} %copy-done.22) | copy-start | bytes 1179652
  528.0 25.0 %copy-start.24 = (bf16[2,200,896]{2,1,0:T(8,128)(2,1)S(1)}, bf16[2,200,896]{2,1,0:T(8,128)(2,1)}, u32[]{:S(2)}) copy-start(bf16[2,200,896]{2,1,0:T(8,128)(2,1)} %pad_maximum_fusion.8.refs_6_) | copy-start | bytes 2150404
  663.4 25.5 %copy-start.10 = (bf16[4,2,25,8,560]{4,3,2,1,0:T(8,128)(2,1)S(1)}, bf16[4,2,25,8,560]{4,3,2,1,0:T(8,128)(2,1)}, u32[]{:S(2)}) copy-start(bf16[4,2,25,8,560]{4,3,2,1,0:T(8,128)(2,1)} %copy-done.9) | copy-start | bytes 5376004
  663.4 27.9 %copy-start.32 = (f32[4,128,896]{2,1,0:T(8,128)S(1)}, f32[4,128,896]{2,1,0:T(8,128)}, u32[]{:S(2)}) copy-start(f32[4,128,896]{2,1,0:T(8,128)} %copy-done.31) | copy-start | bytes 5505028
  663.4 27.9 %copy-start.71 = (f32[4,128,896]{2,1,0:T(8,128)S(1)}, f32[4,128,896]{2,1,0:T(8,128)}, u32[]{:S(2)}) copy-start(f32[4,128,896]{2,1,0:T(8,128)} %get-tuple-element.432) | copy-start | bytes 5505028
  663.4 27.9 %copy-start.88 = (f32[4,128,1792]{2,1,0:T(8,128)S(1)}, f32[4,128,1792]{2,1,0:T(8,128)}, u32[]{:S(2)}) copy-start(f32[4,128,1792]{2,1,0:T(8,128)} %copy-done.86) | copy-start | bytes 11010052
  663.4 27.9 %copy-start.113 = (bf16[800,1600]{0,1:T(8,128)(2,1)S(1)}, bf16[800,1600]{0,1:T(8,128)(2,1)}, u32[]{:S(2)}) copy-start(bf16[800,1600]{0,1:T(8,128)(2,1)} %copy.186) | copy-start | bytes 7680004
  743.5 47.1 %copy-start.171 = (f32[4,896]{1,0:T(4,128)S(1)}, f32[4,896]{1,0:T(4,128)}, u32[]{:S(2)}) copy-start(f32[4,896]{1,0:T(4,128)} %get-tuple-element.509) | copy-start | bytes 43012
  743.5 47.1 %copy-start.172 = (f32[4,896]{1,0:T(4,128)S(1)}, f32[4,896]{1,0:T(4,128)}, u32[]{:S(2)}) copy-start(f32[4,896]{1,0:T(4,128)} %get-tuple-element.510) | copy-start | bytes 43012
  743.5 47.1 %copy-start.173 = (f32[4,896]{1,0:T(4,128)S(1)}, f32[4,896]{1,0:T(4,128)}, u32[]{:S(2)}) copy-start(f32[4,896]{1,0:T(4,128)} %get-tuple-element.511) | copy-start | bytes 43012
  743.5 47.2 %copy-start.174 = (f32[4,896]{1,0:T(4,128)S(1)}, f32[4,896]{1,0:T(4,128)}, u32[]{:S(2)}) copy-start(f32[4,896]{1,0:T(4,128)} %get-tuple-element.512) | copy-start | bytes 43012
  743.5 47.4 %copy-start.4 = (f32[4,128,896]{2,1,0:T(8,128)S(1)}, f32[4,128,896]{2,1,0:T(8,128)}, u32[]{:S(2)}) copy-start(f32[4,128,896]{2,1,0:T(8,128)} %copy-done.3) | copy-start | bytes 5505028
  893.7 23.5 %collective-permute-start.1 = (bf16[4,3,896]{2,1,0:T(4,128)(2,1)S(1)}, bf16[4,3,896]{2,1,0:T(4,128)(2,1)S(1)}, u32[]{:S(2)}, u32[]{:S(2)}) collective-permute-start(bf16[4,3,896]{2,1,0:T(4,128)(2,1)S(1)} %slice.868), channel_id=1, source_target_pairs={{1,0},{2,1},{3,2},{4,3},{5,4},{6,5},{7,6},{9,8},{10,9},{11,10},{12... | collective-permute-start | bytes 64520 | tf_op jit(solution)/shard_map/ppermute | solution.py:1344
  902.4 173.4 %collective-permute-start.2 = (bf16[688,512]{1,0:T(8,128)(2,1)}, bf16[688,512]{1,0:T(8,128)(2,1)}, u32[]{:S(2)}, u32[]{:S(2)}) collective-permute-start(bf16[688,512]{1,0:T(8,128)(2,1)} %pad_maximum_fusion.10), channel_id=1, source_target_pairs={{0,0},{1,1},{2,8},{3,9},{4,16},{5,17},{6,24},{7,25},{8,2},{9,3},{1... | collective-permute-start | bytes 2113544 | tf_op jit(solution)/shard_map/ppermute | solution.py:1317
  931.4 28.2 %copy-start.206 = (f32[128]{0:T(128)S(1)}, f32[128]{0:T(128)}, u32[]{:S(2)}) copy-start(f32[128]{0:T(128)} %copy-done.205) | copy-start | bytes 1540
  981.4 29.7 %copy-start.109 = (f32[128,1600]{1,0:T(8,128)S(1)}, f32[128,1600]{1,0:T(8,128)}, u32[]{:S(2)}) copy-start(f32[128,1600]{1,0:T(8,128)} %convert_reduce_fusion.1) | copy-start | bytes 2457604
  1019.8 37.4 %copy-start.67 = (bf16[400,58]{1,0:T(8,128)(2,1)S(1)}, bf16[400,58]{1,0:T(8,128)(2,1)}, u32[]{:S(2)}) copy-start(bf16[400,58]{1,0:T(8,128)(2,1)} %copy-done.66) | copy-start | bytes 139204
  1019.8 37.3 %copy-start.134 = (f32[1,400,58]{2,1,0:T(8,128)S(1)}, f32[1,400,58]{2,1,0:T(8,128)}, u32[]{:S(2)}) copy-start(f32[1,400,58]{2,1,0:T(8,128)} %copy.231) | copy-start | bytes 278404
  1019.8 37.3 %copy-start.135 = (f32[1,400,58]{2,1,0:T(8,128)S(1)}, f32[1,400,58]{2,1,0:T(8,128)}, u32[]{:S(2)}) copy-start(f32[1,400,58]{2,1,0:T(8,128)} %copy.230) | copy-start | bytes 278404
  (181 other events, 693.3 us)

commit v4 on v3

--- a/solution.py
+++ b/solution.py
@@ -429,21 +429,62 @@
                 peer = {FSDP: ci // halves, CTX: halves * fi + lax.rem(ci, halves)}
                 add(self.remote(src, dst, send_sem.at[k, 0], take_sem.at[k, 0], peer), away, away)
                 keep(pltpu.make_async_copy(src, dst, own_sem.at[k, 0]), ci // halves == fi)
+            elif mode in (NEXT, PREV):
+                reach = self.reach
+                m = ci if mode == NEXT else cs - 1 - ci
+                odd = lax.rem(m, 2)
+
+                def at(spot):
+                    spot = lax.rem(spot + cs, cs)
+                    return {CTX: spot if mode == NEXT else cs - 1 - spot}
+
+                def on_line(e, m=m, src=src, dst=dst, k=k, at=at):
+                    source = src if e == 2 else dst.at[e - 3]
+                    return self.remote(
+                        source, dst.at[e - 1], send_sem.at[k, e], take_sem.at[k, e], at(m + 2)
+                    )
+
+                def to_mate(g, e, m=m, odd=odd, src=src, dst=dst, k=k, at=at, reach=reach):
+                    source = src if e == 0 else dst.at[e - 1]
+                    spot = reach + 1 + g
+                    return self.remote(
+                        source,
+                        dst.at[g - 1],
+                        send_sem.at[k, spot],
+                        take_sem.at[k, spot],
+                        at(m + 1 - 2 * odd),
+                    )
+
+                starts.append((on_line(2).start, m + 2 < cs))
+                waits.append((on_line(2).wait_send, m + 2 < cs))
+                starts.append((to_mate(1, 0).start, odd == 0))
+                waits.append((to_mate(1, 0).wait_send, odd == 0))
+                for e in range(2, reach + 1, 2):
+                    here = m - e >= 0
+                    relays.append((on_line(e).wait_recv, here))
+                    if e + 2 <= reach:
+                        goes = here & (m + 2 < cs)
+                        relays.append((on_line(e + 2).start, goes))
+                        waits.append((on_line(e + 2).wait_send, goes))
+                    if e + 1 < reach:
+                        relays.append((to_mate(e + 1, e).start, here & (odd == 0)))
+                        waits.append((to_mate(e + 1, e).wait_send, here & (odd == 0)))
+                    relays.append((to_mate(e - 1, e).start, here & (odd == 1)))
+                    waits.append((to_mate(e - 1, e).wait_send, here & (odd == 1)))
+                for g in range(1, reach, 2):
+                    waits.append((to_mate(g, 0).wait_recv, m - g >= 0))
             else:
                 for d in range(1, self.reach + 1):
-                    up = mode == NEXT
-                    peer = ci + d if up else ci - d
-                    source = src.at[d - 1] if mode == BACK else src
                     add(
                         self.remote(
-                            source,
+                            src.at[d - 1],
                             dst.at[d - 1],
                             send_sem.at[k, d],
                             take_sem.at[k, d],
-                            {CTX: lax.rem(peer + cs, cs)},
+                            {CTX: lax.rem(ci - d + cs, cs)},
                         ),
-                        peer < cs if up else peer >= 0,
-                        ci - d >= 0 if up else ci + d < cs,
+                        ci - d >= 0,
+                        ci + d < cs,
                     )
         return starts, relays, waits
 
@@ -775,10 +816,14 @@
     if swapped:
         tokens, depth = depth, tokens
     real, width = weight.shape
+    turned = real > tokens * 8
+    if turned:
+        weight = weight.T
 
     def body(value_ref, weight_ref, out_ref):
         value = value_ref[0].T if swapped else value_ref[0][:, :real]
-        out_ref[0] = jnp.dot(value, weight_ref[...], preferred_element_type=f32).astype(bf16)
+        product = dense_nt if turned else dense
+        out_ref[0] = product(value, weight_ref[...]).astype(bf16)
 
     return pl.pallas_call(
         body,
@@ -968,7 +1013,6 @@
     normed_all = normed_all.reshape(fs * tok, dim)
     xp_w = jnp.pad(w_ssm_proj[:, :xdim], ((0, chan_p - chan), (0, 0)))
     dt_w = jnp.pad(w_ssm_proj[:, xdim:], ((0, chan_p - chan), (0, 0)))
-    mo_w = jnp.pad(w_mamba_out, ((0, chan_p - chan), (0, 0)))
     vec = pad_last(lax.dynamic_slice_in_dim(ssm_vec, fi * chan, chan, 1), chan_p)
 
     normed_rows = normed_all.reshape(fs, tok, dim)
@@ -1025,12 +1069,11 @@
     xproj_part = lax.dot_general(
         xp_w, inner_low, (((0,), (1,)), ((), ())), preferred_element_type=f32
     )
-    xproj_got, attn_old, ssm_proj_old = exchange(
+    xproj_got, attn_old = exchange(
         3,
         [
             (xproj_part, GATHER, FSDP),
             (row_block(w_attn_out), CROSS, BOTH),
-            (row_block(w_ssm_proj), CROSS, BOTH),
         ],
     )
     xproj = jnp.sum(xproj_got, axis=0).T
@@ -1048,14 +1091,14 @@
     rate = -jnp.exp(vec[CONV + 2 :])
     rate2 = rate * LOG2E
     sizes = (fs, tok, chan_p)
-    last_state, mamba_out_old = scan_call(
+    last_state, ssm_proj_old = scan_call(
         scan_tail_body,
         (step_far, drive, b_wide, rate2),
         (SEQ, SEQ, SPREAD, RATE),
         (STATE,),
         *sizes,
         cid=19,
-        plan=Traffic([(row_block(w_mamba_out), CROSS, BOTH)]),
+        plan=Traffic([(row_block(w_ssm_proj), CROSS, BOTH)]),
     )
     step_sum = jnp.sum(step_far, axis=1)
     state_before, sums, gu_2 = exchange(
@@ -1076,14 +1119,14 @@
     for d in range(reach, 0, -1):
         there = jnp.where(ci >= d, state_before[d - 1].astype(f32), 0.0)
         entry = decay_of(ci - d) * entry + there
-    readout, hist, ffn_down_old = scan_call(
+    readout, hist, mamba_out_old = scan_call(
         scan_full_body,
         (step_far, drive, b_wide, c_wide, rate2, entry),
         (SEQ, SEQ, SPREAD, SPREAD, RATE, STATE),
         (SEQ, HIST),
         *sizes,
         cid=20,
-        plan=Traffic([(row_block(w_ffn_down), CROSS, BOTH)]),
+        plan=Traffic([(row_block(w_mamba_out), CROSS, BOTH)]),
     )
     skip = vec[CONV + 1]
     pre_mix = readout + skip * inner_x
@@ -1111,7 +1154,7 @@
     v_spec = pl.BlockSpec((HD, seen), lambda g: (g + KVH, 0))
     bias_spec = pl.BlockSpec((seen, tok), lambda g: (0, 0))
     total_spec = pl.BlockSpec((1, groups, tok), lambda g: (g, 0, 0))
-    attended, log_totals, gu_1 = hosted_call(
+    attended, log_totals, gu_1, ffn_down_old = hosted_call(
         functools.partial(attend_body, groups),
         (KVH,),
         [q_spec, k_spec, v_spec, bias_spec],
@@ -1122,7 +1165,7 @@
         ],
         (queries, key_rows, key_rows, bias),
         16,
-        Traffic([(gu_send, (HALF, 5, 10), WEIGHTS)]),
+        Traffic([(gu_send, (HALF, 5, 10), WEIGHTS), (row_block(w_ffn_down), CROSS, BOTH)]),
         12 * MIB,
     )
     wide = heads_dim // fs
@@ -1253,7 +1296,7 @@
         hops[5],
     )
 
-    mixture_grad = dense_nt(ssm_proj_low, mo_w).reshape(fs, tok, chan_p)
+    mixture_grad = pad_last(dense_nt(ssm_proj_low, w_mamba_out), chan_p).reshape(fs, tok, chan_p)
     read_grad = mixture_grad * gate_silu
     gate_grad = mixture_grad * pre_mix * (gate_s * (1.0 + gate_z * (1.0 - gate_s)))
     gate_low = gate_grad.astype(bf16).reshape(fs * tok, chan_p)

time: 1100 us -> 1070 us (0.973)
  Pallas kernels: 756 us -> 731 us
  local copies, waits for them, and re-layouts: 130 us -> 117 us
    pallas_call x19, Pallas kernels: 578 us -> 554 us  [exchange(): pl.pallas_call(body, out_shape=tuple(plan.outs), in_specs=[ANY] * ins, ou...]
    unnamed x475 -> x468, local copies, waits for them, and re-layouts: 63.9 us -> 51 us
  transfers between devices with their start and end apart: 3 -> 3, of which waited for: 0 -> 0; matrix products, arithmetic and copies ran while one was open for 12% -> 11% of each run, Pallas kernels for 18% -> 19%
where the time goes in v4:
time: 1070 us; the launch traced here: 1060 us
  Pallas kernels  731 us (68%)
  local copies, waits for them, and re-layouts  117 us (11%)
  other arithmetic  113 us (11%)
  matrix products  79 us (7%)
  starting transfers between devices  11.6 us (1%)
    pallas_call x19, Pallas kernels, exchange(): pl.pallas_call(body, out_shape=tuple(plan.outs), in_specs=[ANY] * ins, ou...  554 us
    pallas_call x6, Pallas kernels, hosted_call(): pl.pallas_call(hosted, grid=grid, in_specs=in_specs + [ANY] * x_in, out_s...  167 us
    unnamed x468, local copies, waits for them, and re-layouts  51 us
    dot_general x9, matrix products, dense_tn(): lax.dot_general(operand, partner, (((0,), (0,)), ((), ())), preferred_ele...  35.5 us
    mul x9, other arithmetic, adam_step(): return (second_moment, -learn_rate * (corrected + decay_rate * weight_now))  23.2 us
  transfers between devices with their start and end apart: 3, of which 0 were waited for; matrix products, arithmetic and copies ran while one was open for 11% of the time, Pallas kernels for 19%

profile of v4, /device:TPU:2, one launch (start us, length us, event | category | flops | bytes accessed | tf_op | source)
XLA Modules:
  0.0 1055.5 jit_solution(13733557784395578152)
XLA Ops:
  3.8 5.1 fusion.310
  14.1 61.9 %shard_map.428 = (bf16[4,128,1600]{2,1,0:T(8,128)(2,1)S(1)}, s32[4,1,1024]{2,1,0:T(1,128)S(1)}, bf16[4,2,25,8,1792]{4,3,2,1,0:T(8,128)(2,1)S(1)}, bf16[4,2,25,8,560]{4,3,2,1,0:T(8,128)(2,1)S(1)}) custom-call(bf16[128,1600]{1,0:T(8,128)(2,1)S(1)} %fusion.161.refs_0_, s32[1,1024]{1,0:T(1,128)S(1)} %copy-done.67, ...), custom_call_target="tpu_custom_call" | custom-call | tf_op jit(solution)/shard_map/pallas_call | solution.py:584
  76.0 3.5 fusion.322
  81.3 3.4 collective-permute-start
  85.8 7.2 fusion.309
  101.0 10.5 shard_map.429
  114.8 4.5 pad_maximum_fusion.refs_2_.refs_4_.refs_1_
  119.3 20.6 %shard_map.430 = (bf16[4,640,128]{2,1,0:T(8,128)(2,1)S(1)}, bf16[8,16,640]{2,1,0:T(8,128)(2,1)S(1)}, bf16[4,2,5,8,2816]{4,3,2,1,0:T(8,128)(2,1)S(1)}) custom-call(bf16[640,128]{1,0:T(8,128)(2,1)S(1)} %slice.635.refs_0_, bf16[16,640]{1,0:T(8,128)(2,1)S(1)} %pad_maximum_fusion.16.refs_1_, bf16[4,2,25,8,2816]{4,3,2,1,0:T(8,128)(2,1)} %pad_maximum_fusion.refs_2_.refs_4_.refs_1_), custom_call_target="tpu_custom_call" | custom-call | tf_op jit(solution)/shard_map/pallas_call | solution.py:584
  160.9 44.5 %shard_map.431 = (bf16[1600,128]{1,0:T(8,128)(2,1)S(1)}, f32[5,5,128]{2,1,0:T(8,128)S(1)}, bf16[4,2,5,8,2816]{4,3,2,1,0:T(8,128)(2,1)S(1)}, bf16[688,400]{1,0:T(8,128)(2,1)S(1)}) custom-call(bf16[1600,128]{1,0:T(8,128)(2,1)S(1)} %slice.634.refs_0_, bf16[640,768]{1,0:T(8,128)(2,1)S(1)} %constant_dynamic-update-slice_fusion.refs_1_.refs_2_, ...), custom_call_target="tpu_custom_call" | custom-call | tf_op jit(solution)/shard_map/pallas_call | solution.py:718
  207.5 22.6 %shard_map.432 = (bf16[4,400,128]{2,1,0:T(8,128)(2,1)S(1)}, bf16[4,2,6,8,2816]{4,3,2,1,0:T(8,128)(2,1)S(1)}) custom-call(bf16[4,400,128]{2,1,0:T(8,128)(2,1)S(1)} %bitcast.538, bf16[4,2,25,8,2816]{4,3,2,1,0:T(8,128)(2,1)} %pad_maximum_fusion.refs_2_.refs_4_.refs_1_), custom_call_target="tpu_custom_call" | custom-call | tf_op jit(solution)/shard_map/pallas_call | solution.py:584
  243.2 6.0 fusion.293
  250.6 16.3 %shard_map.434 = (f32[4,132,512]{2,1,0:T(8,128)S(1)}, bf16[200,400]{1,0:T(8,128)(2,1)S(1)}) custom-call(f32[132,512]{1,0:T(8,128)S(1)} %fusion.198.refs_0_, bf16[200,400]{1,0:T(8,128)(2,1)S(1)} %dynamic_slice.105.refs_1_), custom_call_target="tpu_custom_call" | custom-call | tf_op jit(solution)/shard_map/pallas_call | solution.py:584
  271.6 3.7 fusion.308
  276.4 8.7 shard_map.435
  285.2 29.1 %shard_map.436 = (bf16[4,4,16,896]{3,2,1,0:T(8,128)(2,1)S(1)}, f32[8,4,896]{2,1,0:T(4,128)S(1)}, bf16[4,2,9,8,2816]{4,3,2,1,0:T(8,128)(2,1)S(1)}) custom-call(bf16[4,16,896]{2,1,0:T(8,128)(2,1)S(1)} %convert_element_type.425.refs_0_, f32[4,896]{1,0:T(4,128)S(1)} %get-tuple-element.429.refs_1_, ...), custom_call_target="tpu_custom_call" | custom-call | tf_op jit(solution)/shard_map/pallas_call | solution.py:584
  316.4 23.8 %shard_map.437 = (f32[4,128,896]{2,1,0:T(8,128)S(1)}, f32[4,128,16,896]{3,2,1,0:T(8,128)}, bf16[400,400]{1,0:T(8,128)(2,1)S(1)}) custom-call(f32[4,128,896]{2,1,0:T(8,128)S(1)} %get-tuple-element.430.refs_0_, f32[4,128,896]{2,1,0:T(8,128)S(1)} %get-tuple-element.465.refs_1_, f32[4,128,16,128]{3,2,1,0:T(8,128)S(1)} %broadcast_in_dim.186.refs_2_.refs_3_, ...), custom_call_target="tpu_custom_call" | custom-call | tf_op jit(solution)/shard_map/pallas_call | solution.py:718
  345.3 23.6 %shard_map.439 = (bf16[2,128,1600]{2,1,0:T(8,128)(2,1)S(1)}, bf16[2,128,1600]{2,1,0:T(8,128)(2,1)S(1)}) custom-call(bf16[4,128,1600]{2,1,0:T(8,128)(2,1)S(1)} %copy-done.15, bf16[4,128,1600]{2,1,0:T(8,128)(2,1)S(1)} %shard_map.438.refs_1_), custom_call_target="tpu_custom_call" | custom-call | tf_op jit(solution)/shard_map/pallas_call | solution.py:584
  371.0 23.3 %shard_map.440 = (bf16[4,128,1600]{2,1,0:T(8,128)(2,1)S(1)}, bf16[4,128,1600]{2,1,0:T(8,128)(2,1)S(1)}) custom-call(bf16[128,1600]{1,0:T(8,128)(2,1)S(1)} %multiply_convert_fusion.3.refs_0_, bf16[128,1600]{1,0:T(8,128)(2,1)S(1)} %bitcast.515), custom_call_target="tpu_custom_call" | custom-call | tf_op jit(solution)/shard_map/pallas_call | solution.py:584
  399.0 5.4 fusion.323
  407.3 6.3 convolution_convert_fusion.5
  413.7 4.8 convolution_convert_fusion.2
  418.5 4.9 convolution_convert_fusion.1
  425.3 3.5 copy.174
  429.9 7.5 convolution_convert_fusion
  437.4 23.9 %shard_map.441 = (bf16[2,128,1600]{2,1,0:T(8,128)(2,1)S(1)}, bf16[200,1408]{1,0:T(8,128)(2,1)}, bf16[200,1408]{1,0:T(8,128)(2,1)}, bf16[344,512]{1,0:T(8,128)(2,1)}, bf16[344,512]{1,0:T(8,128)(2,1)}) custom-call(bf16[4,128,1600]{2,1,0:T(8,128)(2,1)S(1)} %bitcast.516, bf16[8,1,200,1408]{3,2,1,0:T(8,128)(2,1)} %bitcast.556, ...), custom_call_target="tpu_custom_call" | custom-call | tf_op jit(solution)/shard_map/pallas_call | solution.py:584
  465.0 25.9 %shard_map.442 = (bf16[4,128,1600]{2,1,0:T(8,128)(2,1)S(1)}, bf16[4,128,1600]{2,1,0:T(8,128)(2,1)S(1)}, bf16[200,1408]{1,0:T(8,128)(2,1)}, bf16[200,1408]{1,0:T(...) custom-call(bf16[128,1600]{1,0:T(8,128)(2,1)S(1)} %get-tuple-element.491.refs_0_, ...), custom_call_target="tpu_custom_call" | custom-call | tf_op jit(solution)/shard_map/pallas_call | solution.py:584
  499.9 24.9 %shard_map.443 = (bf16[4,400,128]{2,1,0:T(8,128)(2,1)S(1)}, bf16[200,1408]{1,0:T(8,128)(2,1)}, bf16[200,1408]{1,0:T(8,128)(2,1)}, bf16[344,512]{1,0:T(8,128)(2,1)}, bf16[344,512]{1,0:T(8,128)(2,1)}) custom-call(bf16[4,400,128]{2,1,0:T(8,128)(2,1)S(1)} %fusion.127.refs_0_, bf16[8,1,200,1408]{3,2,1,0:T(8,128)(2,1)} %bitcast.558, ...), custom_call_target="tpu_custom_call" | custom-call | tf_op jit(solution)/shard_map/pallas_call | solution.py:584
  524.9 25.0 %shard_map.444 = (bf16[1600,128]{1,0:T(8,128)(2,1)S(1)}, f32[320,768]{1,0:T(8,128)S(1)}, f32[320,768]{1,0:T(8,128)S(1)}, bf16[2,200,896]{2,1,0:T(8,128)(2,1)S(1)...) custom-call(bf16[1600,128]{1,0:T(8,128)(2,1)S(1)} %copy-done.20, ...), custom_call_target="tpu_custom_call" | custom-call | tf_op jit(solution)/shard_map/pallas_call | solution.py:718
  557.2 6.1 shard_map.445.refs_2_
  563.4 70.2 %shard_map.446 = (bf16[4,640,128]{2,1,0:T(8,128)(2,1)S(1)}, bf16[8,16,640]{2,1,0:T(8,128)(2,1)S(1)}, bf16[2,128,1600]{2,1,0:T(8,128)(2,1)S(1)}, bf16[200,1408]{1...) custom-call(bf16[4,640,128]{2,1,0:T(8,128)(2,1)S(1)} %pad_maximum_fu, ...), custom_call_target="tpu_custom_call" | custom-call | tf_op jit(solution)/shard_map/pallas_call | solution.py:584
  638.8 24.6 %shard_map.447 = (bf16[4,560,128]{2,1,0:T(8,128)(2,1)S(1)}, bf16[4,16,560]{2,1,0:T(8,128)(2,1)S(1)}, bf16[200,1408]{1,0:T(8,128)(2,1)}, bf16[200,1408]{1,0:T(8,1...) custom-call(bf16[4,560,128]{2,1,0:T(8,128)(2,1)S(1)} %bitcast.530, ...), custom_call_target="tpu_custom_call" | custom-call | tf_op jit(solution)/shard_map/pallas_call | solution.py:584
  671.8 3.5 bitcast_convert_fusion
  679.4 3.8 copy.182
  688.4 4.9 convolution_convert_fusion.3
  693.3 18.3 %shard_map.448 = (f32[4,16,896]{2,1,0:T(8,128)S(1)}, bf16[2,200,1408]{2,1,0:T(8,128)(2,1)S(1)}, bf16[200,896]{1,0:T(8,128)(2,1)}, bf16[200,560]{1,0:T(8,128)(2,1...) custom-call(f32[4,128,896]{2,1,0:T(8,128)S(1)} %get-tuple-element.430.refs_0_, f32[4,128,896]{2,1,0:T(8,128)S(1)} %copy-done.3, ...), custom_call_target="tpu_custom_call" | custom-call | tf_op jit(solution)/shard_map/pallas_call | solution.py:718
  717.0 37.5 %shard_map.449 = (bf16[4,4,16,896]{3,2,1,0:T(8,128)(2,1)S(1)}, bf16[2,200,1408]{2,1,0:T(8,128)(2,1)S(1)}, bf16[200,896]{1,0:T(8,128)(2,1)}, bf16[200,896]{1,0:T(...) custom-call(bf16[4,16,896]{2,1,0:T(8,128)(2,1)S(1)} %convert_element, ...), custom_call_target="tpu_custom_call" | custom-call | tf_op jit(solution)/shard_map/pallas_call | solution.py:584
  755.8 46.6 %shard_map.450 = (f32[4,128,896]{2,1,0:T(8,128)S(1)}, f32[4,128,896]{2,1,0:T(8,128)S(1)}, f32[4,128,16,128]{3,2,1,0:T(8,128)}, f32[4,128,16,128]{3,2,1,0:T(8,128...) custom-call(f32[4,128,896]{2,1,0:T(8,128)S(1)} %get-tuple-element.43, ...), custom_call_target="tpu_custom_call" | custom-call | tf_op jit(solution)/shard_map/pallas_call | solution.py:718
  808.3 3.5 reduce_sum.428
  811.9 4.3 fusion.303
  817.2 33.3 %shard_map.451 = (f32[4,132,512]{2,1,0:T(8,128)S(1)}, bf16[200,896]{1,0:T(8,128)(2,1)}, bf16[200,896]{1,0:T(8,128)(2,1)}, bf16[200,560]{1,0:T(8,128)(2,1)}, bf16...) custom-call(f32[132,512]{1,0:T(8,128)S(1)} %pad_maximum_fusion.13.re, ...), custom_call_target="tpu_custom_call" | custom-call | tf_op jit(solution)/shard_map/pallas_call | solution.py:584
  852.9 6.9 multiply_reduce_fusion.3
  870.0 6.8 collective-permute-start.2
  879.1 5.1 fusion.37
  900.7 26.5 %shard_map.452 = (bf16[2,128,1600]{2,1,0:T(8,128)(2,1)S(1)}, bf16[2,16,1600]{2,1,0:T(8,128)(2,1)S(1)}, bf16[200,512]{1,0:T(8,128)(2,1)}, bf16[200,512]{1,0:T(8,1...) custom-call(bf16[4,128,1600]{2,1,0:T(8,128)(2,1)S(1)} %copy.186.refs, ...), custom_call_target="tpu_custom_call" | custom-call | tf_op jit(solution)/shard_map/pallas_call | solution.py:584
  930.8 17.0 %shard_map.453 = (f32[4,20,1600]{2,1,0:T(8,128)S(1)}, bf16[200,512]{1,0:T(8,128)(2,1)}, bf16[200,512]{1,0:T(8,128)(2,1)}, bf16[200,384]{1,0:T(8,128)(2,1)}, bf16...) custom-call(f32[20,1600]{1,0:T(8,128)S(1)} %concatenate.138.refs_0_, ...), custom_call_target="tpu_custom_call" | custom-call | tf_op jit(solution)/shard_map/pallas_call | solution.py:584
  947.9 26.5 %shard_map.454 = (bf16[8,20,1600]{2,1,0:T(8,128)(2,1)S(1)}, bf16[8,22,896]{2,1,0:T(8,128)(2,1)S(1)}, bf16[200,512]{1,0:T(8,128)(2,1)}, bf16[200,512]{1,0:T(8,128...) custom-call(bf16[20,1600]{1,0:T(8,128)(2,1)S(1)} %reduce_sum.441.ref, ...), custom_call_target="tpu_custom_call" | custom-call | tf_op jit(solution)/shard_map/pallas_call | solution.py:584
  985.4 35.9 %shard_map.455 = (bf16[2,200,896]{2,1,0:T(8,128)(2,1)S(1)}, bf16[200,512]{1,0:T(8,128)(2,1)S(1)}, bf16[400,512]{1,0:T(8,128)(2,1)S(1)}, bf16[400,128]{1,0:T(8,128)(2,1)S(1)}, f32[4,22,896]{2,1,0:T(8,128)S(1)}) custom-call(bf16[2,200,896]{2,1,0:T(8,128)(2,1)S(1)} %pad_maximum_fusion.9.refs_0_, bf16[200,512]{1,0:T(8,128)(2,1)S(1)} %fusion.203.refs_1_, ...), custom_call_target="tpu_custom_call" | custom-call | tf_op jit(solution)/shard_map/pallas_call | solution.py:584
  1047.1 3.8 fusion.111
  (664 shorter events, 216.2 us)
Async XLA Ops:
  3.0 96.6 %copy-start.141 = (f32[1600]{0:T(1024)}, f32[1600]{0:T(1024)S(1)}, u32[]{:S(2)}) copy-start(f32[1600]{0:T(1024)S(1)} %get-tuple-element.388) | copy-start | bytes 19204
  3.1 366.5 %copy-start.161 = (f32[1600]{0:T(1024)}, f32[1600]{0:T(1024)S(1)}, u32[]{:S(2)}) copy-start(f32[1600]{0:T(1024)S(1)} %get-tuple-element.386) | copy-start | bytes 19204
  3.1 366.5 %copy-start.163 = (f32[1600]{0:T(1024)}, f32[1600]{0:T(1024)S(1)}, u32[]{:S(2)}) copy-start(f32[1600]{0:T(1024)S(1)} %get-tuple-element.387) | copy-start | bytes 19204
  76.0 23.7 %copy-start.7 = (bf16[4,2,25,8,560]{4,3,2,1,0:T(8,128)(2,1)}, bf16[4,2,25,8,560]{4,3,2,1,0:T(8,128)(2,1)S(1)}, u32[]{:S(2)}) copy-start(bf16[4,2,25,8,560]{4,3,2,1,0:T(8,128)(2,1)S(1)} %get-tuple-element.142) | copy-start | bytes 5376004
  81.3 161.9 %collective-permute-start = (f32[4,3,896]{2,1,0:T(4,128)}, f32[4,3,896]{2,1,0:T(4,128)}, u32[]{:S(2)}, u32[]{:S(2)}) collective-permute-start(f32[4,3,896]{2,1,0:T(4,128)} %slice.640), channel_id=1, source_target_pairs={{0,1},{1,2},{2,3},{3,4},{4,5},{5,6},{6,7},{8,9},{9,10},{10,11},{11... | collective-permute-start | bytes 129032 | tf_op jit(solution)/shard_map/ppermute | solution.py:1054
  85.8 156.8 %copy-start.123 = (f32[22,800]{1,0:T(8,128)}, f32[22,800]{1,0:T(8,128)S(1)}, u32[]{:S(2)}) copy-start(f32[22,800]{1,0:T(8,128)S(1)} %constant_dynamic-slice_fusion) | copy-start | bytes 211204
  98.4 13.3 %copy-start.97 = (bf16[400,1376]{1,0:T(8,128)(2,1)S(1)}, bf16[400,1376]{1,0:T(8,128)(2,1)}, u32[]{:S(2)}) copy-start(bf16[400,1376]{1,0:T(8,128)(2,1)} %get-tuple-element.436) | copy-start | bytes 3302404
  142.0 18.8 %copy-start.25 = (f32[768,128]{1,0:T(8,128)}, f32[768,128]{1,0:T(8,128)S(1)}, u32[]{:S(2)}) copy-start(f32[768,128]{1,0:T(8,128)S(1)} %pad_select_fusion.refs_3_) | copy-start | bytes 1179652
  207.5 23.9 %copy-start.36 = (bf16[400,1600]{1,0:T(8,128)(2,1)S(1)}, bf16[400,1600]{1,0:T(8,128)(2,1)}, u32[]{:S(2)}) copy-start(bf16[400,1600]{1,0:T(8,128)(2,1)} %weight_ref.2) | copy-start | bytes 3840004
  243.2 97.0 %copy-start.166 = (f32[896]{0:T(1024)}, f32[896]{0:T(1024)S(1)}, u32[]{:S(2)}) copy-start(f32[896]{0:T(1024)S(1)} %get-tuple-element.391) | copy-start | bytes 10756
  275.3 41.1 %copy-start.5 = (f32[4,128,896]{2,1,0:T(8,128)}, f32[4,128,896]{2,1,0:T(8,128)S(1)}, u32[]{:S(2)}) copy-start(f32[4,128,896]{2,1,0:T(8,128)S(1)} %get-tuple-element.465.refs_1_) | copy-start | bytes 5505028
  276.4 39.9 %copy-start.2 = (f32[4,128,16,128]{3,2,1,0:T(8,128)}, f32[4,128,16,128]{3,2,1,0:T(8,128)S(1)}, u32[]{:S(2)}) copy-start(f32[4,128,16,128]{3,2,1,0:T(8,128)S(1)} %broadcast_in_dim.186.refs_2_.refs_3_) | copy-start | bytes 12582916
  285.2 29.1 %copy-start.64 = (bf16[400,58]{1,0:T(8,128)(2,1)}, bf16[400,58]{1,0:T(8,128)(2,1)S(1)}, u32[]{:S(2)}) copy-start(bf16[400,58]{1,0:T(8,128)(2,1)S(1)} %get-tuple-element.246) | copy-start | bytes 139204
  285.2 30.0 %copy-start.126 = (f32[512,16]{1,0:T(8,128)S(1)}, f32[512,16]{1,0:T(8,128)}, u32[]{:S(2)}) copy-start(f32[512,16]{1,0:T(8,128)} %copy.215) | copy-start | bytes 98308
  316.4 23.8 %copy-start = (f32[4,128,16,128]{3,2,1,0:T(8,128)}, f32[4,128,16,128]{3,2,1,0:T(8,128)S(1)}, u32[]{:S(2)}) copy-start(f32[4,128,16,128]{3,2,1,0:T(8,128)S(1)} %broadcast_in_dim.188.refs_3_.refs_2_.refs_4_) | copy-start | bytes 12582916
  316.4 23.8 %copy-start.68 = (f32[4,128,896]{2,1,0:T(8,128)S(1)}, f32[4,128,896]{2,1,0:T(8,128)}, u32[]{:S(2)}) copy-start(f32[4,128,896]{2,1,0:T(8,128)} %get-tuple-element.432) | copy-start | bytes 5505028
  316.4 23.8 %copy-start.80 = (f32[4,128,1792]{2,1,0:T(8,128)S(1)}, f32[4,128,1792]{2,1,0:T(8,128)}, u32[]{:S(2)}) copy-start(f32[4,128,1792]{2,1,0:T(8,128)} %copy-done.79) | copy-start | bytes 11010052
  345.3 49.1 %slice-start = ((s8[4505600]{0:T(1024)(128)(4,1)}), s8[4194304]{0:T(1024)(128)(4,1)S(1)}, s32[]{:S(2)}) async-start(s8[4505600]{0:T(1024)(128)(4,1)} %bitcast.517), calls=%async_computation | async-start | bytes 8388608
  369.3 95.3 %copy-start.187 = (f32[128]{0:T(128)}, f32[128]{0:T(128)S(1)}, u32[]{:S(2)}) copy-start(f32[128]{0:T(128)S(1)} %fusion.269) | copy-start | bytes 1540
  369.3 25.2 %slice-start.1 = ((s8[4505600]{0:T(1024)(128)(4,1)}), s8[311296]{0:T(1024)(128)(4,1)S(1)}, s32[]{:S(2)}) async-start(s8[4505600]{0:T(1024)(128)(4,1)} %bitcast.517), calls=%async_computation.1 | async-start | bytes 622592
  370.4 94.2 %copy-start.189 = (f32[128]{0:T(128)}, f32[128]{0:T(128)S(1)}, u32[]{:S(2)}) copy-start(f32[128]{0:T(128)S(1)} %fusion.268) | copy-start | bytes 1540
  370.9 23.5 %copy-start.84 = (f32[128,1600]{1,0:T(8,128)}, f32[128,1600]{1,0:T(8,128)S(1)}, u32[]{:S(2)}) copy-start(f32[128,1600]{1,0:T(8,128)S(1)} %get-tuple-element.428) | copy-start | bytes 2457604
  370.9 91.4 %copy-start.191 = (f32[128]{0:T(128)}, f32[128]{0:T(128)S(1)}, u32[]{:S(2)}) copy-start(f32[128]{0:T(128)S(1)} %fusion.270) | copy-start | bytes 1540
  394.4 29.0 %copy-start.28 = (bf16[4,128,1600]{2,1,0:T(8,128)(2,1)}, bf16[4,128,1600]{2,1,0:T(8,128)(2,1)S(1)}, u32[]{:S(2)}) copy-start(bf16[4,128,1600]{2,1,0:T(8,128)(2,1)S(1)} %get-tuple-element.165) | copy-start | bytes 4915204
  437.4 24.0 %copy-start.85 = (f32[128,1600]{1,0:T(8,128)S(1)}, f32[128,1600]{1,0:T(8,128)}, u32[]{:S(2)}) copy-start(f32[128,1600]{1,0:T(8,128)} %copy-done.84) | copy-start | bytes 2457604
  465.0 25.9 %copy-start.24 = (bf16[800,1600]{1,0:T(8,128)(2,1)S(1)}, bf16[800,1600]{1,0:T(8,128)(2,1)}, u32[]{:S(2)}) copy-start(bf16[800,1600]{1,0:T(8,128)(2,1)} %weight_ref.3) | copy-start | bytes 7680004
  499.9 24.9 %copy-start.20 = (bf16[1600,128]{1,0:T(8,128)(2,1)S(1)}, bf16[1600,128]{1,0:T(8,128)(2,1)}, u32[]{:S(2)}) copy-start(bf16[1600,128]{1,0:T(8,128)(2,1)} %copy-done.19) | copy-start | bytes 1228804
  499.9 24.9 %copy-start.26 = (f32[768,128]{1,0:T(8,128)S(1)}, f32[768,128]{1,0:T(8,128)}, u32[]{:S(2)}) copy-start(f32[768,128]{1,0:T(8,128)} %copy-done.25) | copy-start | bytes 1179652
  499.9 25.0 %copy-start.27 = (bf16[2,200,896]{2,1,0:T(8,128)(2,1)S(1)}, bf16[2,200,896]{2,1,0:T(8,128)(2,1)}, u32[]{:S(2)}) copy-start(bf16[2,200,896]{2,1,0:T(8,128)(2,1)} %pad_maximum_fusion.8.refs_6_) | copy-start | bytes 2150404
  638.8 24.7 %copy-start.8 = (bf16[4,2,25,8,560]{4,3,2,1,0:T(8,128)(2,1)S(1)}, bf16[4,2,25,8,560]{4,3,2,1,0:T(8,128)(2,1)}, u32[]{:S(2)}) copy-start(bf16[4,2,25,8,560]{4,3,2,1,0:T(8,128)(2,1)} %copy-done.7) | copy-start | bytes 5376004
  638.8 27.1 %copy-start.69 = (f32[4,128,896]{2,1,0:T(8,128)S(1)}, f32[4,128,896]{2,1,0:T(8,128)}, u32[]{:S(2)}) copy-start(f32[4,128,896]{2,1,0:T(8,128)} %get-tuple-element.432) | copy-start | bytes 5505028
  638.8 27.1 %copy-start.81 = (f32[4,128,1792]{2,1,0:T(8,128)S(1)}, f32[4,128,1792]{2,1,0:T(8,128)}, u32[]{:S(2)}) copy-start(f32[4,128,1792]{2,1,0:T(8,128)} %copy-done.79) | copy-start | bytes 11010052
  638.8 27.1 %copy-start.115 = (f32[512,800]{1,0:T(8,128)S(1)}, f32[512,800]{1,0:T(8,128)}, u32[]{:S(2)}) copy-start(f32[512,800]{1,0:T(8,128)} %fusion.325) | copy-start | bytes 4915204
  693.3 18.3 %copy-start.140 = (bf16[200,1408]{1,0:T(8,128)(2,1)S(1)}, bf16[200,1408]{1,0:T(8,128)(2,1)}, u32[]{:S(2)}) copy-start(bf16[200,1408]{1,0:T(8,128)(2,1)} %get-tuple-element.201) | copy-start | bytes 1689604
  716.9 38.6 %copy-start.172 = (f32[4,896]{1,0:T(4,128)S(1)}, f32[4,896]{1,0:T(4,128)}, u32[]{:S(2)}) copy-start(f32[4,896]{1,0:T(4,128)} %get-tuple-element.509) | copy-start | bytes 43012
  716.9 38.6 %copy-start.173 = (f32[4,896]{1,0:T(4,128)S(1)}, f32[4,896]{1,0:T(4,128)}, u32[]{:S(2)}) copy-start(f32[4,896]{1,0:T(4,128)} %get-tuple-element.510) | copy-start | bytes 43012
  716.9 38.6 %copy-start.174 = (f32[4,896]{1,0:T(4,128)S(1)}, f32[4,896]{1,0:T(4,128)}, u32[]{:S(2)}) copy-start(f32[4,896]{1,0:T(4,128)} %get-tuple-element.511) | copy-start | bytes 43012
  716.9 38.6 %copy-start.175 = (f32[4,896]{1,0:T(4,128)S(1)}, f32[4,896]{1,0:T(4,128)}, u32[]{:S(2)}) copy-start(f32[4,896]{1,0:T(4,128)} %get-tuple-element.512) | copy-start | bytes 43012
  716.9 38.8 %copy-start.6 = (f32[4,128,896]{2,1,0:T(8,128)S(1)}, f32[4,128,896]{2,1,0:T(8,128)}, u32[]{:S(2)}) copy-start(f32[4,128,896]{2,1,0:T(8,128)} %copy-done.5) | copy-start | bytes 5505028
  859.9 19.1 %slice-start.4 = ((s8[4505600]{0:T(1024)(128)(4,1)}), s8[4194304]{0:T(1024)(128)(4,1)S(1)}, s32[]{:S(2)}) async-start(s8[4505600]{0:T(1024)(128)(4,1)} %bitcast.613), calls=%async_computation.4 | async-start | bytes 8388608
  860.6 18.4 %slice-start.5 = ((s8[4505600]{0:T(1024)(128)(4,1)}), s8[311296]{0:T(1024)(128)(4,1)S(1)}, s32[]{:S(2)}) async-start(s8[4505600]{0:T(1024)(128)(4,1)} %bitcast.613), calls=%async_computation.5 | async-start | bytes 622592
  861.4 25.1 %collective-permute-start.1 = (bf16[4,3,896]{2,1,0:T(4,128)(2,1)S(1)}, bf16[4,3,896]{2,1,0:T(4,128)(2,1)S(1)}, u32[]{:S(2)}, u32[]{:S(2)}) collective-permute-start(bf16[4,3,896]{2,1,0:T(4,128)(2,1)S(1)} %slice.868), channel_id=1, source_target_pairs={{1,0},{2,1},{3,2},{4,3},{5,4},{6,5},{7,6},{9,8},{10,9},{11,10},{12... | collective-permute-start | bytes 64520 | tf_op jit(solution)/shard_map/ppermute | solution.py:1387
  870.0 171.6 %collective-permute-start.2 = (bf16[688,512]{1,0:T(8,128)(2,1)}, bf16[688,512]{1,0:T(8,128)(2,1)}, u32[]{:S(2)}, u32[]{:S(2)}) collective-permute-start(bf16[688,512]{1,0:T(8,128)(2,1)} %pad_maximum_fusion.10), channel_id=1, source_target_pairs={{0,0},{1,1},{2,8},{3,9},{4,16},{5,17},{6,24},{7,25},{8,2},{9,3},{1... | collective-permute-start | bytes 2113544 | tf_op jit(solution)/shard_map/ppermute | solution.py:1360
  900.7 26.6 %copy-start.205 = (f32[128]{0:T(128)S(1)}, f32[128]{0:T(128)}, u32[]{:S(2)}) copy-start(f32[128]{0:T(128)} %copy-done.204) | copy-start | bytes 1540
  947.9 28.7 %copy-start.107 = (f32[128,1600]{1,0:T(8,128)S(1)}, f32[128,1600]{1,0:T(8,128)}, u32[]{:S(2)}) copy-start(f32[128,1600]{1,0:T(8,128)} %convert_reduce_fusion.1) | copy-start | bytes 2457604
  985.4 37.7 %copy-start.65 = (bf16[400,58]{1,0:T(8,128)(2,1)S(1)}, bf16[400,58]{1,0:T(8,128)(2,1)}, u32[]{:S(2)}) copy-start(bf16[400,58]{1,0:T(8,128)(2,1)} %copy-done.64) | copy-start | bytes 139204
  985.4 37.7 %copy-start.132 = (f32[1,400,58]{2,1,0:T(8,128)S(1)}, f32[1,400,58]{2,1,0:T(8,128)}, u32[]{:S(2)}) copy-start(f32[1,400,58]{2,1,0:T(8,128)} %copy.223) | copy-start | bytes 278404
  985.4 37.6 %copy-start.133 = (f32[1,400,58]{2,1,0:T(8,128)S(1)}, f32[1,400,58]{2,1,0:T(8,128)}, u32[]{:S(2)}) copy-start(f32[1,400,58]{2,1,0:T(8,128)} %copy.222) | copy-start | bytes 278404
  (178 other events, 616.4 us)

commit v5 on v4

--- a/solution.py
+++ b/solution.py
@@ -1348,7 +1348,7 @@
         *sizes,
         cid=22,
         plan=Traffic([], ring_two, hops[2]),
-        later=(3,) if hops[2] == 2 else (),
+        later=(4,) if hops[2] == 2 else (),
     )
     cross = [
         (f * cs + c, (c // halves) * cs + halves * f + c % halves)
@@ -1464,7 +1464,8 @@
     ssm_total = jnp.concatenate([vec_all[j, :, :chan] for j in range(fs)], axis=1)
     gate_up_gradient = unpaired(gate_up_sum, ffw)
     mamba_in_gradient = unpaired(mamba_in_sum, chan)
-    ffn_down_gradient = down_sum[:, : dim // fs].astype(f32)
+    down_turned, old_turned = together(down_sum[:, : dim // fs].T, ffn_down_old.T)
+    ffn_down_gradient = down_turned.astype(f32)
     attn_gradient = attn_sum[:, : dim // fs].astype(f32)
     mamba_out_gradient = mamba_out_sum[:, : dim // fs].astype(f32)
     ssm_proj_gradient = proj_sum[:, : w_ssm_proj.shape[1] // fs].astype(f32)
@@ -1480,7 +1481,14 @@
         mamba_out_gradient, m_mamba_out, mamba_out_old
     )
     gate_up_moments, gate_up_update = adam_block(gate_up_gradient, m_gate_up, gate_up_old)
-    ffn_down_moments, ffn_down_update = adam_block(ffn_down_gradient, m_ffn_down, ffn_down_old)
+    ffn_down_moments, ffn_down_update = adam_block(
+        ffn_down_gradient, jnp.swapaxes(m_ffn_down, 1, 2), old_turned
+    )
+    ffn_down_gradient, ffn_down_moments, ffn_down_update = (
+        ffn_down_gradient.T,
+        ffn_down_moments.T,
+        ffn_down_update.T,
+    )
     ssm_vec_moments, ssm_vec_update = adam_step(ssm_total, m_ssm_vec, ssm_vec)
     embed_moments, embed_update = adam_step(embed_total, m_embed_small, embed_small)
     return (

time: 1070 us -> 1060 us (level)
    mul x9 -> x8, other arithmetic: 23.2 us -> 19.5 us  [adam_step(): return (second_moment, -learn_rate * (corrected + decay_rate * weight_now))]
    unnamed x468 -> x463, local copies, waits for them, and re-layouts: 51 us -> 50.7 us
  transfers between devices with their start and end apart: 3 -> 3, of which waited for: 0 -> 0; matrix products, arithmetic and copies ran while one was open for 11% -> 10% of each run, Pallas kernels for 19% -> 20%
where the time goes in v5:
time: 1060 us; the launch traced here: 1050 us
  Pallas kernels  731 us (69%)
  local copies, waits for them, and re-layouts  116 us (11%)
  other arithmetic  111 us (10%)
  matrix products  78.9 us (7%)
  starting transfers between devices  12 us (1%)
    pallas_call x19, Pallas kernels, exchange(): pl.pallas_call(body, out_shape=tuple(plan.outs), in_specs=[ANY] * ins, ou...  554 us
    pallas_call x6, Pallas kernels, hosted_call(): pl.pallas_call(hosted, grid=grid, in_specs=in_specs + [ANY] * x_in, out_s...  167 us
    unnamed x463, local copies, waits for them, and re-layouts  50.7 us
    dot_general x9, matrix products, dense_tn(): lax.dot_general(operand, partner, (((0,), (0,)), ((), ())), preferred_ele...  35.5 us
  transfers between devices with their start and end apart: 3, of which 0 were waited for; matrix products, arithmetic and copies ran while one was open for 10% of the time, Pallas kernels for 20%

profile of v5, /device:TPU:2, one launch (start us, length us, event | category | flops | bytes accessed | tf_op | source)
XLA Modules:
  0.0 1054.2 jit_solution(1397527057400921728)
XLA Ops:
  3.8 5.1 fusion.314
  14.1 61.9 %shard_map.428 = (bf16[4,128,1600]{2,1,0:T(8,128)(2,1)S(1)}, s32[4,1,1024]{2,1,0:T(1,128)S(1)}, bf16[4,2,25,8,1792]{4,3,2,1,0:T(8,128)(2,1)S(1)}, bf16[4,2,25,8,560]{4,3,2,1,0:T(8,128)(2,1)S(1)}) custom-call(bf16[128,1600]{1,0:T(8,128)(2,1)S(1)} %fusion.165.refs_0_, s32[1,1024]{1,0:T(1,128)S(1)} %copy-done.67, ...), custom_call_target="tpu_custom_call" | custom-call | tf_op jit(solution)/shard_map/pallas_call | solution.py:584
  76.0 3.5 fusion.325
  85.8 7.2 fusion.313
  101.0 10.5 shard_map.429
  114.8 4.4 pad_maximum_fusion.refs_2_.refs_4_.refs_1_
  119.2 20.6 %shard_map.430 = (bf16[4,640,128]{2,1,0:T(8,128)(2,1)S(1)}, bf16[8,16,640]{2,1,0:T(8,128)(2,1)S(1)}, bf16[4,2,5,8,2816]{4,3,2,1,0:T(8,128)(2,1)S(1)}) custom-call(bf16[640,128]{1,0:T(8,128)(2,1)S(1)} %slice.635.refs_0_, bf16[16,640]{1,0:T(8,128)(2,1)S(1)} %pad_maximum_fusion.16.refs_1_, bf16[4,2,25,8,2816]{4,3,2,1,0:T(8,128)(2,1)} %pad_maximum_fusion.refs_2_.refs_4_.refs_1_), custom_call_target="tpu_custom_call" | custom-call | tf_op jit(solution)/shard_map/pallas_call | solution.py:584
  144.3 4.8 fusion.316
  159.6 44.5 %shard_map.431 = (bf16[1600,128]{1,0:T(8,128)(2,1)S(1)}, f32[5,5,128]{2,1,0:T(8,128)S(1)}, bf16[4,2,5,8,2816]{4,3,2,1,0:T(8,128)(2,1)S(1)}, bf16[688,400]{1,0:T(8,128)(2,1)S(1)}) custom-call(bf16[1600,128]{1,0:T(8,128)(2,1)S(1)} %slice.634.refs_0_, bf16[640,768]{1,0:T(8,128)(2,1)S(1)} %constant_dynamic-update-slice_fusion.refs_1_.refs_2_, ...), custom_call_target="tpu_custom_call" | custom-call | tf_op jit(solution)/shard_map/pallas_call | solution.py:718
  206.2 22.6 %shard_map.432 = (bf16[4,400,128]{2,1,0:T(8,128)(2,1)S(1)}, bf16[4,2,6,8,2816]{4,3,2,1,0:T(8,128)(2,1)S(1)}) custom-call(bf16[4,400,128]{2,1,0:T(8,128)(2,1)S(1)} %bitcast.548, bf16[4,2,25,8,2816]{4,3,2,1,0:T(8,128)(2,1)} %pad_maximum_fusion.refs_2_.refs_4_.refs_1_), custom_call_target="tpu_custom_call" | custom-call | tf_op jit(solution)/shard_map/pallas_call | solution.py:584
  240.9 5.9 fusion.298
  248.2 16.3 %shard_map.434 = (f32[4,132,512]{2,1,0:T(8,128)S(1)}, bf16[200,400]{1,0:T(8,128)(2,1)S(1)}) custom-call(f32[132,512]{1,0:T(8,128)S(1)} %fusion.203.refs_0_, bf16[200,400]{1,0:T(8,128)(2,1)S(1)} %dynamic_slice.105.refs_1_), custom_call_target="tpu_custom_call" | custom-call | tf_op jit(solution)/shard_map/pallas_call | solution.py:584
  269.1 3.7 fusion.312
  274.0 8.7 shard_map.435
  282.8 29.1 %shard_map.436 = (bf16[4,4,16,896]{3,2,1,0:T(8,128)(2,1)S(1)}, f32[8,4,896]{2,1,0:T(4,128)S(1)}, bf16[4,2,9,8,2816]{4,3,2,1,0:T(8,128)(2,1)S(1)}) custom-call(bf16[4,16,896]{2,1,0:T(8,128)(2,1)S(1)} %convert_element_type.425.refs_0_, f32[4,896]{1,0:T(4,128)S(1)} %get-tuple-element.431.refs_1_, ...), custom_call_target="tpu_custom_call" | custom-call | tf_op jit(solution)/shard_map/pallas_call | solution.py:584
  314.0 23.7 %shard_map.437 = (f32[4,128,896]{2,1,0:T(8,128)S(1)}, f32[4,128,16,896]{3,2,1,0:T(8,128)}, bf16[400,400]{1,0:T(8,128)(2,1)S(1)}) custom-call(f32[4,128,896]{2,1,0:T(8,128)S(1)} %get-tuple-element.432.refs_0_, f32[4,128,896]{2,1,0:T(8,128)S(1)} %get-tuple-element.467.refs_1_, f32[4,128,16,128]{3,2,1,0:T(8,128)S(1)} %broadcast_in_dim.186.refs_2_.refs_3_, ...), custom_call_target="tpu_custom_call" | custom-call | tf_op jit(solution)/shard_map/pallas_call | solution.py:718
  342.8 23.6 %shard_map.439 = (bf16[2,128,1600]{2,1,0:T(8,128)(2,1)S(1)}, bf16[2,128,1600]{2,1,0:T(8,128)(2,1)S(1)}) custom-call(bf16[4,128,1600]{2,1,0:T(8,128)(2,1)S(1)} %copy-done.15, bf16[4,128,1600]{2,1,0:T(8,128)(2,1)S(1)} %shard_map.438.refs_1_), custom_call_target="tpu_custom_call" | custom-call | tf_op jit(solution)/shard_map/pallas_call | solution.py:584
  368.6 23.3 %shard_map.440 = (bf16[4,128,1600]{2,1,0:T(8,128)(2,1)S(1)}, bf16[4,128,1600]{2,1,0:T(8,128)(2,1)S(1)}) custom-call(bf16[128,1600]{1,0:T(8,128)(2,1)S(1)} %multiply_convert_fusion.3.refs_0_, bf16[128,1600]{1,0:T(8,128)(2,1)S(1)} %bitcast.524), custom_call_target="tpu_custom_call" | custom-call | tf_op jit(solution)/shard_map/pallas_call | solution.py:584
  396.5 5.4 fusion.326
  404.8 6.3 convolution_convert_fusion.5
  411.2 4.8 convolution_convert_fusion.2
  416.0 4.9 convolution_convert_fusion.1
  422.7 3.5 copy.171
  427.4 7.5 convolution_convert_fusion
  434.9 23.9 %shard_map.441 = (bf16[2,128,1600]{2,1,0:T(8,128)(2,1)S(1)}, bf16[200,1408]{1,0:T(8,128)(2,1)}, bf16[200,1408]{1,0:T(8,128)(2,1)}, bf16[344,512]{1,0:T(8,128)(2,1)}, bf16[344,512]{1,0:T(8,128)(2,1)}) custom-call(bf16[4,128,1600]{2,1,0:T(8,128)(2,1)S(1)} %bitcast.525, bf16[8,1,200,1408]{3,2,1,0:T(8,128)(2,1)} %bitcast.566, ...), custom_call_target="tpu_custom_call" | custom-call | tf_op jit(solution)/shard_map/pallas_call | solution.py:584
  462.5 25.9 %shard_map.442 = (bf16[4,128,1600]{2,1,0:T(8,128)(2,1)S(1)}, bf16[4,128,1600]{2,1,0:T(8,128)(2,1)S(1)}, bf16[200,1408]{1,0:T(8,128)(2,1)}, bf16[200,1408]{1,0:T(...) custom-call(bf16[128,1600]{1,0:T(8,128)(2,1)S(1)} %get-tuple-element.493.refs_0_, ...), custom_call_target="tpu_custom_call" | custom-call | tf_op jit(solution)/shard_map/pallas_call | solution.py:584
  497.4 24.9 %shard_map.443 = (bf16[4,400,128]{2,1,0:T(8,128)(2,1)S(1)}, bf16[200,1408]{1,0:T(8,128)(2,1)}, bf16[200,1408]{1,0:T(8,128)(2,1)}, bf16[344,512]{1,0:T(8,128)(2,1)}, bf16[344,512]{1,0:T(8,128)(2,1)}) custom-call(bf16[4,400,128]{2,1,0:T(8,128)(2,1)S(1)} %fusion.131.refs_0_, bf16[8,1,200,1408]{3,2,1,0:T(8,128)(2,1)} %bitcast.568, ...), custom_call_target="tpu_custom_call" | custom-call | tf_op jit(solution)/shard_map/pallas_call | solution.py:584
  522.4 25.0 %shard_map.444 = (bf16[1600,128]{1,0:T(8,128)(2,1)S(1)}, f32[320,768]{1,0:T(8,128)S(1)}, f32[320,768]{1,0:T(8,128)S(1)}, bf16[2,200,896]{2,1,0:T(8,128)(2,1)S(1)...) custom-call(bf16[1600,128]{1,0:T(8,128)(2,1)S(1)} %copy-done.20, ...), custom_call_target="tpu_custom_call" | custom-call | tf_op jit(solution)/shard_map/pallas_call | solution.py:718
  554.6 6.1 shard_map.445.refs_2_
  560.9 70.2 %shard_map.446 = (bf16[4,640,128]{2,1,0:T(8,128)(2,1)S(1)}, bf16[8,16,640]{2,1,0:T(8,128)(2,1)S(1)}, bf16[2,128,1600]{2,1,0:T(8,128)(2,1)S(1)}, bf16[200,1408]{1...) custom-call(bf16[4,640,128]{2,1,0:T(8,128)(2,1)S(1)} %pad_maximum_fu, ...), custom_call_target="tpu_custom_call" | custom-call | tf_op jit(solution)/shard_map/pallas_call | solution.py:584
  636.3 24.6 %shard_map.447 = (bf16[4,560,128]{2,1,0:T(8,128)(2,1)S(1)}, bf16[4,16,560]{2,1,0:T(8,128)(2,1)S(1)}, bf16[200,1408]{1,0:T(8,128)(2,1)}, bf16[200,1408]{1,0:T(8,1...) custom-call(bf16[4,560,128]{2,1,0:T(8,128)(2,1)S(1)} %bitcast.539, ...), custom_call_target="tpu_custom_call" | custom-call | tf_op jit(solution)/shard_map/pallas_call | solution.py:584
  669.3 3.5 bitcast_convert_fusion
  676.9 3.8 copy.179
  685.8 4.9 convolution_convert_fusion.3
  690.7 18.3 %shard_map.448 = (f32[4,16,896]{2,1,0:T(8,128)S(1)}, bf16[2,200,1408]{2,1,0:T(8,128)(2,1)S(1)}, bf16[200,896]{1,0:T(8,128)(2,1)}, bf16[200,560]{1,0:T(8,128)(2,1...) custom-call(f32[4,128,896]{2,1,0:T(8,128)S(1)} %get-tuple-element.432.refs_0_, f32[4,128,896]{2,1,0:T(8,128)S(1)} %copy-done.3, ...), custom_call_target="tpu_custom_call" | custom-call | tf_op jit(solution)/shard_map/pallas_call | solution.py:718
  714.4 37.5 %shard_map.449 = (bf16[4,4,16,896]{3,2,1,0:T(8,128)(2,1)S(1)}, bf16[2,200,1408]{2,1,0:T(8,128)(2,1)S(1)}, bf16[200,896]{1,0:T(8,128)(2,1)}, bf16[200,896]{1,0:T(...) custom-call(bf16[4,16,896]{2,1,0:T(8,128)(2,1)S(1)} %convert_element, ...), custom_call_target="tpu_custom_call" | custom-call | tf_op jit(solution)/shard_map/pallas_call | solution.py:584
  753.2 46.7 %shard_map.450 = (f32[4,128,896]{2,1,0:T(8,128)S(1)}, f32[4,128,896]{2,1,0:T(8,128)S(1)}, f32[4,128,16,128]{3,2,1,0:T(8,128)}, f32[4,128,16,128]{3,2,1,0:T(8,128...) custom-call(f32[4,128,896]{2,1,0:T(8,128)S(1)} %get-tuple-element.43, ...), custom_call_target="tpu_custom_call" | custom-call | tf_op jit(solution)/shard_map/pallas_call | solution.py:718
  805.9 3.5 reduce_sum.428
  809.5 4.3 fusion.307
  814.7 33.1 %shard_map.451 = (f32[4,132,512]{2,1,0:T(8,128)S(1)}, bf16[200,896]{1,0:T(8,128)(2,1)}, bf16[200,896]{1,0:T(8,128)(2,1)}, bf16[200,560]{1,0:T(8,128)(2,1)}, bf16...) custom-call(f32[132,512]{1,0:T(8,128)S(1)} %pad_maximum_fusion.13.re, ...), custom_call_target="tpu_custom_call" | custom-call | tf_op jit(solution)/shard_map/pallas_call | solution.py:584
  850.4 6.8 multiply_reduce_fusion.3
  867.3 7.2 collective-permute-start.2
  876.8 5.1 fusion.37
  898.4 28.1 %shard_map.452 = (bf16[2,128,1600]{2,1,0:T(8,128)(2,1)S(1)}, bf16[2,16,1600]{2,1,0:T(8,128)(2,1)S(1)}, bf16[200,512]{1,0:T(8,128)(2,1)}, bf16[200,512]{1,0:T(8,1...) custom-call(bf16[4,128,1600]{2,1,0:T(8,128)(2,1)S(1)} %copy.183.refs, ...), custom_call_target="tpu_custom_call" | custom-call | tf_op jit(solution)/shard_map/pallas_call | solution.py:584
  930.2 16.7 %shard_map.453 = (f32[4,20,1600]{2,1,0:T(8,128)S(1)}, bf16[200,512]{1,0:T(8,128)(2,1)}, bf16[200,512]{1,0:T(8,128)(2,1)}, bf16[200,384]{1,0:T(8,128)(2,1)}, bf16...) custom-call(f32[20,1600]{1,0:T(8,128)S(1)} %concatenate.138.refs_0_, ...), custom_call_target="tpu_custom_call" | custom-call | tf_op jit(solution)/shard_map/pallas_call | solution.py:584
  947.0 25.7 %shard_map.454 = (bf16[8,20,1600]{2,1,0:T(8,128)(2,1)S(1)}, bf16[8,22,896]{2,1,0:T(8,128)(2,1)S(1)}, bf16[200,512]{1,0:T(8,128)(2,1)}, bf16[200,512]{1,0:T(8,128...) custom-call(bf16[20,1600]{1,0:T(8,128)(2,1)S(1)} %reduce_sum.441.ref, ...), custom_call_target="tpu_custom_call" | custom-call | tf_op jit(solution)/shard_map/pallas_call | solution.py:584
  983.7 35.7 %shard_map.455 = (bf16[2,200,896]{2,1,0:T(8,128)(2,1)S(1)}, bf16[200,512]{1,0:T(8,128)(2,1)S(1)}, bf16[400,512]{1,0:T(8,128)(2,1)S(1)}, bf16[400,128]{1,0:T(8,128)(2,1)S(1)}, f32[4,22,896]{2,1,0:T(8,128)S(1)}) custom-call(bf16[2,200,896]{2,1,0:T(8,128)(2,1)S(1)} %pad_maximum_fusion.9.refs_0_, bf16[200,512]{1,0:T(8,128)(2,1)S(1)} %fusion.208.refs_1_, ...), custom_call_target="tpu_custom_call" | custom-call | tf_op jit(solution)/shard_map/pallas_call | solution.py:584
  1045.9 3.7 fusion.113
  (659 shorter events, 213.1 us)
Async XLA Ops:
  3.0 96.6 %copy-start.139 = (f32[1600]{0:T(1024)}, f32[1600]{0:T(1024)S(1)}, u32[]{:S(2)}) copy-start(f32[1600]{0:T(1024)S(1)} %get-tuple-element.392) | copy-start | bytes 19204
  3.1 364.0 %copy-start.159 = (f32[1600]{0:T(1024)}, f32[1600]{0:T(1024)S(1)}, u32[]{:S(2)}) copy-start(f32[1600]{0:T(1024)S(1)} %get-tuple-element.390) | copy-start | bytes 19204
  3.1 364.0 %copy-start.161 = (f32[1600]{0:T(1024)}, f32[1600]{0:T(1024)S(1)}, u32[]{:S(2)}) copy-start(f32[1600]{0:T(1024)S(1)} %get-tuple-element.391) | copy-start | bytes 19204
  76.0 23.7 %copy-start.7 = (bf16[4,2,25,8,560]{4,3,2,1,0:T(8,128)(2,1)}, bf16[4,2,25,8,560]{4,3,2,1,0:T(8,128)(2,1)S(1)}, u32[]{:S(2)}) copy-start(bf16[4,2,25,8,560]{4,3,2,1,0:T(8,128)(2,1)S(1)} %get-tuple-element.144) | copy-start | bytes 5376004
  81.3 159.5 %collective-permute-start = (f32[4,3,896]{2,1,0:T(4,128)}, f32[4,3,896]{2,1,0:T(4,128)}, u32[]{:S(2)}, u32[]{:S(2)}) collective-permute-start(f32[4,3,896]{2,1,0:T(4,128)} %slice.640), channel_id=1, source_target_pairs={{0,1},{1,2},{2,3},{3,4},{4,5},{5,6},{6,7},{8,9},{9,10},{10,11},{11... | collective-permute-start | bytes 129032 | tf_op jit(solution)/shard_map/ppermute | solution.py:1054
  85.8 154.4 %copy-start.121 = (f32[22,800]{1,0:T(8,128)}, f32[22,800]{1,0:T(8,128)S(1)}, u32[]{:S(2)}) copy-start(f32[22,800]{1,0:T(8,128)S(1)} %constant_dynamic-slice_fusion) | copy-start | bytes 211204
  98.4 13.3 %copy-start.96 = (bf16[400,1376]{1,0:T(8,128)(2,1)S(1)}, bf16[400,1376]{1,0:T(8,128)(2,1)}, u32[]{:S(2)}) copy-start(bf16[400,1376]{1,0:T(8,128)(2,1)} %get-tuple-element.438) | copy-start | bytes 3302404
  142.0 17.6 %copy-start.25 = (f32[768,128]{1,0:T(8,128)}, f32[768,128]{1,0:T(8,128)S(1)}, u32[]{:S(2)}) copy-start(f32[768,128]{1,0:T(8,128)S(1)} %pad_select_fusion.refs_3_) | copy-start | bytes 1179652
  206.2 23.9 %copy-start.36 = (bf16[400,1600]{1,0:T(8,128)(2,1)S(1)}, bf16[400,1600]{1,0:T(8,128)(2,1)}, u32[]{:S(2)}) copy-start(bf16[400,1600]{1,0:T(8,128)(2,1)} %weight_ref.2) | copy-start | bytes 3840004
  240.8 96.9 %copy-start.164 = (f32[896]{0:T(1024)}, f32[896]{0:T(1024)S(1)}, u32[]{:S(2)}) copy-start(f32[896]{0:T(1024)S(1)} %get-tuple-element.395) | copy-start | bytes 10756
  272.8 41.1 %copy-start.5 = (f32[4,128,896]{2,1,0:T(8,128)}, f32[4,128,896]{2,1,0:T(8,128)S(1)}, u32[]{:S(2)}) copy-start(f32[4,128,896]{2,1,0:T(8,128)S(1)} %get-tuple-element.467.refs_1_) | copy-start | bytes 5505028
  274.0 39.9 %copy-start.2 = (f32[4,128,16,128]{3,2,1,0:T(8,128)}, f32[4,128,16,128]{3,2,1,0:T(8,128)S(1)}, u32[]{:S(2)}) copy-start(f32[4,128,16,128]{3,2,1,0:T(8,128)S(1)} %broadcast_in_dim.186.refs_2_.refs_3_) | copy-start | bytes 12582916
  282.7 29.1 %copy-start.64 = (bf16[400,58]{1,0:T(8,128)(2,1)}, bf16[400,58]{1,0:T(8,128)(2,1)S(1)}, u32[]{:S(2)}) copy-start(bf16[400,58]{1,0:T(8,128)(2,1)S(1)} %get-tuple-element.248) | copy-start | bytes 139204
  282.8 30.0 %copy-start.124 = (f32[512,16]{1,0:T(8,128)S(1)}, f32[512,16]{1,0:T(8,128)}, u32[]{:S(2)}) copy-start(f32[512,16]{1,0:T(8,128)} %copy.211) | copy-start | bytes 98308
  313.9 23.7 %copy-start = (f32[4,128,16,128]{3,2,1,0:T(8,128)}, f32[4,128,16,128]{3,2,1,0:T(8,128)S(1)}, u32[]{:S(2)}) copy-start(f32[4,128,16,128]{3,2,1,0:T(8,128)S(1)} %broadcast_in_dim.188.refs_3_.refs_2_.refs_4_) | copy-start | bytes 12582916
  313.9 23.8 %copy-start.68 = (f32[4,128,896]{2,1,0:T(8,128)S(1)}, f32[4,128,896]{2,1,0:T(8,128)}, u32[]{:S(2)}) copy-start(f32[4,128,896]{2,1,0:T(8,128)} %get-tuple-element.434) | copy-start | bytes 5505028
  314.0 23.8 %copy-start.80 = (f32[4,128,1792]{2,1,0:T(8,128)S(1)}, f32[4,128,1792]{2,1,0:T(8,128)}, u32[]{:S(2)}) copy-start(f32[4,128,1792]{2,1,0:T(8,128)} %copy-done.79) | copy-start | bytes 11010052
  342.8 49.1 %slice-start = ((s8[4505600]{0:T(1024)(128)(4,1)}), s8[4194304]{0:T(1024)(128)(4,1)S(1)}, s32[]{:S(2)}) async-start(s8[4505600]{0:T(1024)(128)(4,1)} %bitcast.526), calls=%async_computation | async-start | bytes 8388608
  366.8 95.3 %copy-start.185 = (f32[128]{0:T(128)}, f32[128]{0:T(128)S(1)}, u32[]{:S(2)}) copy-start(f32[128]{0:T(128)S(1)} %fusion.274) | copy-start | bytes 1540
  366.8 25.2 %slice-start.1 = ((s8[4505600]{0:T(1024)(128)(4,1)}), s8[311296]{0:T(1024)(128)(4,1)S(1)}, s32[]{:S(2)}) async-start(s8[4505600]{0:T(1024)(128)(4,1)} %bitcast.526), calls=%async_computation.1 | async-start | bytes 622592
  367.9 94.2 %copy-start.187 = (f32[128]{0:T(128)}, f32[128]{0:T(128)S(1)}, u32[]{:S(2)}) copy-start(f32[128]{0:T(128)S(1)} %fusion.273) | copy-start | bytes 1540
  368.4 23.5 %copy-start.84 = (f32[128,1600]{1,0:T(8,128)}, f32[128,1600]{1,0:T(8,128)S(1)}, u32[]{:S(2)}) copy-start(f32[128,1600]{1,0:T(8,128)S(1)} %get-tuple-element.430) | copy-start | bytes 2457604
  368.4 91.4 %copy-start.189 = (f32[128]{0:T(128)}, f32[128]{0:T(128)S(1)}, u32[]{:S(2)}) copy-start(f32[128]{0:T(128)S(1)} %fusion.275) | copy-start | bytes 1540
  391.9 29.0 %copy-start.28 = (bf16[4,128,1600]{2,1,0:T(8,128)(2,1)}, bf16[4,128,1600]{2,1,0:T(8,128)(2,1)S(1)}, u32[]{:S(2)}) copy-start(bf16[4,128,1600]{2,1,0:T(8,128)(2,1)S(1)} %get-tuple-element.167) | copy-start | bytes 4915204
  434.9 24.0 %copy-start.85 = (f32[128,1600]{1,0:T(8,128)S(1)}, f32[128,1600]{1,0:T(8,128)}, u32[]{:S(2)}) copy-start(f32[128,1600]{1,0:T(8,128)} %copy-done.84) | copy-start | bytes 2457604
  462.5 25.9 %copy-start.24 = (bf16[800,1600]{1,0:T(8,128)(2,1)S(1)}, bf16[800,1600]{1,0:T(8,128)(2,1)}, u32[]{:S(2)}) copy-start(bf16[800,1600]{1,0:T(8,128)(2,1)} %weight_ref.3) | copy-start | bytes 7680004
  497.4 24.9 %copy-start.20 = (bf16[1600,128]{1,0:T(8,128)(2,1)S(1)}, bf16[1600,128]{1,0:T(8,128)(2,1)}, u32[]{:S(2)}) copy-start(bf16[1600,128]{1,0:T(8,128)(2,1)} %copy-done.19) | copy-start | bytes 1228804
  497.4 25.0 %copy-start.26 = (f32[768,128]{1,0:T(8,128)S(1)}, f32[768,128]{1,0:T(8,128)}, u32[]{:S(2)}) copy-start(f32[768,128]{1,0:T(8,128)} %copy-done.25) | copy-start | bytes 1179652
  497.4 25.0 %copy-start.27 = (bf16[2,200,896]{2,1,0:T(8,128)(2,1)S(1)}, bf16[2,200,896]{2,1,0:T(8,128)(2,1)}, u32[]{:S(2)}) copy-start(bf16[2,200,896]{2,1,0:T(8,128)(2,1)} %pad_maximum_fusion.8.refs_6_) | copy-start | bytes 2150404
  636.2 24.7 %copy-start.8 = (bf16[4,2,25,8,560]{4,3,2,1,0:T(8,128)(2,1)S(1)}, bf16[4,2,25,8,560]{4,3,2,1,0:T(8,128)(2,1)}, u32[]{:S(2)}) copy-start(bf16[4,2,25,8,560]{4,3,2,1,0:T(8,128)(2,1)} %copy-done.7) | copy-start | bytes 5376004
  636.3 27.1 %copy-start.69 = (f32[4,128,896]{2,1,0:T(8,128)S(1)}, f32[4,128,896]{2,1,0:T(8,128)}, u32[]{:S(2)}) copy-start(f32[4,128,896]{2,1,0:T(8,128)} %get-tuple-element.434) | copy-start | bytes 5505028
  636.3 27.1 %copy-start.81 = (f32[4,128,1792]{2,1,0:T(8,128)S(1)}, f32[4,128,1792]{2,1,0:T(8,128)}, u32[]{:S(2)}) copy-start(f32[4,128,1792]{2,1,0:T(8,128)} %copy-done.79) | copy-start | bytes 11010052
  636.3 27.1 %copy-start.114 = (f32[512,800]{1,0:T(8,128)S(1)}, f32[512,800]{1,0:T(8,128)}, u32[]{:S(2)}) copy-start(f32[512,800]{1,0:T(8,128)} %fusion.328) | copy-start | bytes 4915204
  690.7 18.3 %copy-start.138 = (bf16[200,1408]{1,0:T(8,128)(2,1)S(1)}, bf16[200,1408]{1,0:T(8,128)(2,1)}, u32[]{:S(2)}) copy-start(bf16[200,1408]{1,0:T(8,128)(2,1)} %get-tuple-element.203) | copy-start | bytes 1689604
  714.4 38.6 %copy-start.170 = (f32[4,896]{1,0:T(4,128)S(1)}, f32[4,896]{1,0:T(4,128)}, u32[]{:S(2)}) copy-start(f32[4,896]{1,0:T(4,128)} %get-tuple-element.511) | copy-start | bytes 43012
  714.4 38.6 %copy-start.171 = (f32[4,896]{1,0:T(4,128)S(1)}, f32[4,896]{1,0:T(4,128)}, u32[]{:S(2)}) copy-start(f32[4,896]{1,0:T(4,128)} %get-tuple-element.512) | copy-start | bytes 43012
  714.4 38.6 %copy-start.172 = (f32[4,896]{1,0:T(4,128)S(1)}, f32[4,896]{1,0:T(4,128)}, u32[]{:S(2)}) copy-start(f32[4,896]{1,0:T(4,128)} %get-tuple-element.513) | copy-start | bytes 43012
  714.4 38.6 %copy-start.173 = (f32[4,896]{1,0:T(4,128)S(1)}, f32[4,896]{1,0:T(4,128)}, u32[]{:S(2)}) copy-start(f32[4,896]{1,0:T(4,128)} %get-tuple-element.514) | copy-start | bytes 43012
  714.4 38.8 %copy-start.6 = (f32[4,128,896]{2,1,0:T(8,128)S(1)}, f32[4,128,896]{2,1,0:T(8,128)}, u32[]{:S(2)}) copy-start(f32[4,128,896]{2,1,0:T(8,128)} %copy-done.5) | copy-start | bytes 5505028
  857.2 19.5 %slice-start.4 = ((s8[4505600]{0:T(1024)(128)(4,1)}), s8[4194304]{0:T(1024)(128)(4,1)S(1)}, s32[]{:S(2)}) async-start(s8[4505600]{0:T(1024)(128)(4,1)} %bitcast.624), calls=%async_computation.4 | async-start | bytes 8388608
  857.9 18.8 %slice-start.5 = ((s8[4505600]{0:T(1024)(128)(4,1)}), s8[311296]{0:T(1024)(128)(4,1)S(1)}, s32[]{:S(2)}) async-start(s8[4505600]{0:T(1024)(128)(4,1)} %bitcast.624), calls=%async_computation.5 | async-start | bytes 622592
  858.7 25.5 %collective-permute-start.1 = (bf16[4,3,896]{2,1,0:T(4,128)(2,1)S(1)}, bf16[4,3,896]{2,1,0:T(4,128)(2,1)S(1)}, u32[]{:S(2)}, u32[]{:S(2)}) collective-permute-start(bf16[4,3,896]{2,1,0:T(4,128)(2,1)S(1)} %slice.880), channel_id=1, source_target_pairs={{1,0},{2,1},{3,2},{4,3},{5,4},{6,5},{7,6},{9,8},{10,9},{11,10},{12... | collective-permute-start | bytes 64520 | tf_op jit(solution)/shard_map/ppermute | solution.py:1387
  867.3 172.3 %collective-permute-start.2 = (bf16[688,512]{1,0:T(8,128)(2,1)}, bf16[688,512]{1,0:T(8,128)(2,1)}, u32[]{:S(2)}, u32[]{:S(2)}) collective-permute-start(bf16[688,512]{1,0:T(8,128)(2,1)} %pad_maximum_fusion.10), channel_id=1, source_target_pairs={{0,0},{1,1},{2,8},{3,9},{4,16},{5,17},{6,24},{7,25},{8,2},{9,3},{1... | collective-permute-start | bytes 2113544 | tf_op jit(solution)/shard_map/ppermute | solution.py:1360
  898.4 28.3 %copy-start.203 = (f32[128]{0:T(128)S(1)}, f32[128]{0:T(128)}, u32[]{:S(2)}) copy-start(f32[128]{0:T(128)} %copy-done.202) | copy-start | bytes 1540
  946.9 27.9 %copy-start.106 = (f32[128,1600]{1,0:T(8,128)S(1)}, f32[128,1600]{1,0:T(8,128)}, u32[]{:S(2)}) copy-start(f32[128,1600]{1,0:T(8,128)} %convert_reduce_fusion.1) | copy-start | bytes 2457604
  983.7 37.4 %copy-start.65 = (bf16[400,58]{1,0:T(8,128)(2,1)S(1)}, bf16[400,58]{1,0:T(8,128)(2,1)}, u32[]{:S(2)}) copy-start(bf16[400,58]{1,0:T(8,128)(2,1)} %copy-done.64) | copy-start | bytes 139204
  983.7 37.4 %copy-start.130 = (f32[1,400,58]{2,1,0:T(8,128)S(1)}, f32[1,400,58]{2,1,0:T(8,128)}, u32[]{:S(2)}) copy-start(f32[1,400,58]{2,1,0:T(8,128)} %copy.219) | copy-start | bytes 278404
  983.7 37.4 %copy-start.131 = (f32[1,400,58]{2,1,0:T(8,128)S(1)}, f32[1,400,58]{2,1,0:T(8,128)}, u32[]{:S(2)}) copy-start(f32[1,400,58]{2,1,0:T(8,128)} %copy.218) | copy-start | bytes 278404
  (176 other events, 607.6 us)

commit v6 on v5

--- a/solution.py
+++ b/solution.py
@@ -1119,14 +1119,14 @@
     for d in range(reach, 0, -1):
         there = jnp.where(ci >= d, state_before[d - 1].astype(f32), 0.0)
         entry = decay_of(ci - d) * entry + there
-    readout, hist, mamba_out_old = scan_call(
+    readout, hist, mamba_out_old, cot_all = scan_call(
         scan_full_body,
         (step_far, drive, b_wide, c_wide, rate2, entry),
         (SEQ, SEQ, SPREAD, SPREAD, RATE, STATE),
         (SEQ, HIST),
         *sizes,
         cid=20,
-        plan=Traffic([(row_block(w_mamba_out), CROSS, BOTH)]),
+        plan=Traffic([(row_block(w_mamba_out), CROSS, BOTH), (cotangent[0], GATHER, FSDP)]),
     )
     skip = vec[CONV + 1]
     pre_mix = readout + skip * inner_x
@@ -1188,9 +1188,7 @@
     ssm_branch, ssm_norm_pull = jax.vjp(rms_norm, ssm_proj, gain_rows[2])
     residual = source + 0.5 * (attn_branch + ssm_branch)
     ffn_in_f, ffn_norm_pull = jax.vjp(rms_norm, residual, gain_rows[3])
-    ffn_in, cot_all = exchange(
-        7, [(ffn_in_f.astype(bf16), GATHER, FSDP), (cotangent[0], GATHER, FSDP)]
-    )
+    (ffn_in,) = exchange(7, [(ffn_in_f.astype(bf16), GATHER, FSDP)])
     cot_all = cot_all.reshape(fs * tok, dim)
     ffn_in = ffn_in.reshape(fs * tok, dim)
 

time: 1060 us -> 1070 us (level)
    unnamed x463 -> x459, local copies, waits for them, and re-layouts: 50.7 us -> 52.4 us
  transfers between devices with their start and end apart: 3 -> 3, of which waited for: 0 -> 0; matrix products, arithmetic and copies ran while one was open for 10% -> 11% of each run, Pallas kernels for 20% -> 20%
where the time goes in v6:
time: 1070 us; the launch traced here: 1060 us
  Pallas kernels  727 us (68%)
  local copies, waits for them, and re-layouts  120 us (11%)
  other arithmetic  112 us (10%)
  matrix products  83.5 us (8%)
  starting transfers between devices  12.2 us (1%)
    pallas_call x19, Pallas kernels, exchange(): pl.pallas_call(body, out_shape=tuple(plan.outs), in_specs=[ANY] * ins, ou...  546 us
    pallas_call x6, Pallas kernels, hosted_call(): pl.pallas_call(hosted, grid=grid, in_specs=in_specs + [ANY] * x_in, out_s...  171 us
    unnamed x459, local copies, waits for them, and re-layouts  52.4 us
    dot_general x9, matrix products, dense_tn(): lax.dot_general(operand, partner, (((0,), (0,)), ((), ())), preferred_ele...  35.5 us
  transfers between devices with their start and end apart: 3, of which 0 were waited for; matrix products, arithmetic and copies ran while one was open for 11% of the time, Pallas kernels for 20%

profile of v6, /device:TPU:2, one launch (start us, length us, event | category | flops | bytes accessed | tf_op | source)
XLA Modules:
  0.0 1059.5 jit_solution(15710983512332374358)
XLA Ops:
  3.8 5.1 fusion.314
  14.0 61.9 %shard_map.428 = (bf16[4,128,1600]{2,1,0:T(8,128)(2,1)S(1)}, s32[4,1,1024]{2,1,0:T(1,128)S(1)}, bf16[4,2,25,8,1792]{4,3,2,1,0:T(8,128)(2,1)S(1)}, bf16[4,2,25,8,560]{4,3,2,1,0:T(8,128)(2,1)S(1)}) custom-call(bf16[128,1600]{1,0:T(8,128)(2,1)S(1)} %fusion.165.refs_0_, s32[1,1024]{1,0:T(1,128)S(1)} %copy-done.69, ...), custom_call_target="tpu_custom_call" | custom-call | tf_op jit(solution)/shard_map/pallas_call | solution.py:584
  85.8 7.2 fusion.313
  95.3 3.8 fusion.130.refs_0_
  101.7 10.5 shard_map.429
  116.4 4.3 pad_maximum_fusion.refs_2_.refs_4_.refs_1_
  120.7 20.6 %shard_map.430 = (bf16[4,640,128]{2,1,0:T(8,128)(2,1)S(1)}, bf16[8,16,640]{2,1,0:T(8,128)(2,1)S(1)}, bf16[4,2,5,8,2816]{4,3,2,1,0:T(8,128)(2,1)S(1)}) custom-call(bf16[640,128]{1,0:T(8,128)(2,1)S(1)} %slice.635.refs_0_, bf16[16,640]{1,0:T(8,128)(2,1)S(1)} %pad_maximum_fusion.16.refs_1_, bf16[4,2,25,8,2816]{4,3,2,1,0:T(8,128)(2,1)} %pad_maximum_fusion.refs_2_.refs_4_.refs_1_), custom_call_target="tpu_custom_call" | custom-call | tf_op jit(solution)/shard_map/pallas_call | solution.py:584
  147.2 4.8 fusion.316
  165.6 44.9 %shard_map.431 = (bf16[1600,128]{1,0:T(8,128)(2,1)S(1)}, f32[5,5,128]{2,1,0:T(8,128)S(1)}, bf16[4,2,5,8,2816]{4,3,2,1,0:T(8,128)(2,1)S(1)}, bf16[688,400]{1,0:T(8,128)(2,1)S(1)}) custom-call(bf16[1600,128]{1,0:T(8,128)(2,1)S(1)} %slice.634.refs_0_, bf16[640,768]{1,0:T(8,128)(2,1)S(1)} %constant_dynamic-update-slice_fusion.refs_1_.refs_2_, ...), custom_call_target="tpu_custom_call" | custom-call | tf_op jit(solution)/shard_map/pallas_call | solution.py:718
  212.6 22.6 %shard_map.432 = (bf16[4,400,128]{2,1,0:T(8,128)(2,1)S(1)}, bf16[4,2,6,8,2816]{4,3,2,1,0:T(8,128)(2,1)S(1)}) custom-call(bf16[4,400,128]{2,1,0:T(8,128)(2,1)S(1)} %bitcast.551, bf16[4,2,25,8,2816]{4,3,2,1,0:T(8,128)(2,1)} %pad_maximum_fusion.refs_2_.refs_4_.refs_1_), custom_call_target="tpu_custom_call" | custom-call | tf_op jit(solution)/shard_map/pallas_call | solution.py:584
  247.2 5.9 fusion.298
  254.5 16.3 %shard_map.434 = (f32[4,132,512]{2,1,0:T(8,128)S(1)}, bf16[200,400]{1,0:T(8,128)(2,1)S(1)}) custom-call(f32[132,512]{1,0:T(8,128)S(1)} %fusion.203.refs_0_, bf16[200,400]{1,0:T(8,128)(2,1)S(1)} %dynamic_slice.105.refs_1_), custom_call_target="tpu_custom_call" | custom-call | tf_op jit(solution)/shard_map/pallas_call | solution.py:584
  275.4 3.7 fusion.312
  280.3 8.7 shard_map.435
  289.1 29.1 %shard_map.436 = (bf16[4,4,16,896]{3,2,1,0:T(8,128)(2,1)S(1)}, f32[8,4,896]{2,1,0:T(4,128)S(1)}, bf16[4,2,9,8,2816]{4,3,2,1,0:T(8,128)(2,1)S(1)}) custom-call(bf16[4,16,896]{2,1,0:T(8,128)(2,1)S(1)} %convert_element_type.425.refs_0_, f32[4,896]{1,0:T(4,128)S(1)} %get-tuple-element.429.refs_1_, ...), custom_call_target="tpu_custom_call" | custom-call | tf_op jit(solution)/shard_map/pallas_call | solution.py:584
  320.3 27.4 %shard_map.437 = (f32[4,128,896]{2,1,0:T(8,128)S(1)}, f32[4,128,16,896]{3,2,1,0:T(8,128)}, bf16[400,400]{1,0:T(8,128)(2,1)S(1)}, bf16[4,128,1600]{2,1,0:T(8,128)(2,1)S(1)}) custom-call(f32[4,128,896]{2,1,0:T(8,128)S(1)} %get-tuple-element.430.refs_0_, f32[4,128,896]{2,1,0:T(8,128)S(1)} %get-tuple-element.465.refs_1_, ...), custom_call_target="tpu_custom_call" | custom-call | tf_op jit(solution)/shard_map/pallas_call | solution.py:718
  353.5 23.6 %shard_map.439 = (bf16[2,128,1600]{2,1,0:T(8,128)(2,1)S(1)}, bf16[2,128,1600]{2,1,0:T(8,128)(2,1)S(1)}) custom-call(bf16[4,128,1600]{2,1,0:T(8,128)(2,1)S(1)} %copy-done.15, bf16[4,128,1600]{2,1,0:T(8,128)(2,1)S(1)} %shard_map.438.refs_1_), custom_call_target="tpu_custom_call" | custom-call | tf_op jit(solution)/shard_map/pallas_call | solution.py:584
  381.4 13.9 %shard_map.440 = bf16[4,128,1600]{2,1,0:T(8,128)(2,1)S(1)} custom-call(bf16[128,1600]{1,0:T(8,128)(2,1)S(1)} %multiply_convert_fusion.3.refs_0_), custom_call_target="tpu_custom_call" | custom-call | tf_op jit(solution)/shard_map/pallas_call | solution.py:584
  396.7 5.4 fusion.326
  405.0 10.0 convolution_convert_fusion.5
  415.1 4.8 convolution_convert_fusion.2
  419.9 4.9 convolution_convert_fusion.1
  426.6 3.5 copy.171
  431.3 7.5 convolution_convert_fusion
  438.8 24.5 %shard_map.441 = (bf16[2,128,1600]{2,1,0:T(8,128)(2,1)S(1)}, bf16[200,1408]{1,0:T(8,128)(2,1)}, bf16[200,1408]{1,0:T(8,128)(2,1)}, bf16[344,512]{1,0:T(8,128)(2,1)}, bf16[344,512]{1,0:T(8,128)(2,1)}) custom-call(bf16[4,128,1600]{2,1,0:T(8,128)(2,1)S(1)} %bitcast.525, bf16[8,1,200,1408]{3,2,1,0:T(8,128)(2,1)} %bitcast.566, ...), custom_call_target="tpu_custom_call" | custom-call | tf_op jit(solution)/shard_map/pallas_call | solution.py:584
  467.0 25.9 %shard_map.442 = (bf16[4,128,1600]{2,1,0:T(8,128)(2,1)S(1)}, bf16[4,128,1600]{2,1,0:T(8,128)(2,1)S(1)}, bf16[200,1408]{1,0:T(8,128)(2,1)}, bf16[200,1408]{1,0:T(...) custom-call(bf16[128,1600]{1,0:T(8,128)(2,1)S(1)} %get-tuple-element.491.refs_0_, ...), custom_call_target="tpu_custom_call" | custom-call | tf_op jit(solution)/shard_map/pallas_call | solution.py:584
  501.9 24.9 %shard_map.443 = (bf16[4,400,128]{2,1,0:T(8,128)(2,1)S(1)}, bf16[200,1408]{1,0:T(8,128)(2,1)}, bf16[200,1408]{1,0:T(8,128)(2,1)}, bf16[344,512]{1,0:T(8,128)(2,1)}, bf16[344,512]{1,0:T(8,128)(2,1)}) custom-call(bf16[4,400,128]{2,1,0:T(8,128)(2,1)S(1)} %fusion.131.refs_0_, bf16[8,1,200,1408]{3,2,1,0:T(8,128)(2,1)} %bitcast.568, ...), custom_call_target="tpu_custom_call" | custom-call | tf_op jit(solution)/shard_map/pallas_call | solution.py:584
  526.9 25.1 %shard_map.444 = (bf16[1600,128]{1,0:T(8,128)(2,1)S(1)}, f32[320,768]{1,0:T(8,128)S(1)}, f32[320,768]{1,0:T(8,128)S(1)}, bf16[2,200,896]{2,1,0:T(8,128)(2,1)S(1)...) custom-call(bf16[1600,128]{1,0:T(8,128)(2,1)S(1)} %copy-done.20, ...), custom_call_target="tpu_custom_call" | custom-call | tf_op jit(solution)/shard_map/pallas_call | solution.py:718
  559.2 6.1 shard_map.445.refs_2_
  565.5 70.3 %shard_map.446 = (bf16[4,640,128]{2,1,0:T(8,128)(2,1)S(1)}, bf16[8,16,640]{2,1,0:T(8,128)(2,1)S(1)}, bf16[2,128,1600]{2,1,0:T(8,128)(2,1)S(1)}, bf16[200,1408]{1...) custom-call(bf16[4,640,128]{2,1,0:T(8,128)(2,1)S(1)} %pad_maximum_fu, ...), custom_call_target="tpu_custom_call" | custom-call | tf_op jit(solution)/shard_map/pallas_call | solution.py:584
  641.0 24.6 %shard_map.447 = (bf16[4,560,128]{2,1,0:T(8,128)(2,1)S(1)}, bf16[4,16,560]{2,1,0:T(8,128)(2,1)S(1)}, bf16[200,1408]{1,0:T(8,128)(2,1)}, bf16[200,1408]{1,0:T(8,1...) custom-call(bf16[4,560,128]{2,1,0:T(8,128)(2,1)S(1)} %bitcast.539, ...), custom_call_target="tpu_custom_call" | custom-call | tf_op jit(solution)/shard_map/pallas_call | solution.py:584
  673.9 3.5 bitcast_convert_fusion
  681.6 3.8 copy.179
  690.5 4.9 convolution_convert_fusion.3
  695.4 18.3 %shard_map.448 = (f32[4,16,896]{2,1,0:T(8,128)S(1)}, bf16[2,200,1408]{2,1,0:T(8,128)(2,1)S(1)}, bf16[200,896]{1,0:T(8,128)(2,1)}, bf16[200,560]{1,0:T(8,128)(2,1...) custom-call(f32[4,128,896]{2,1,0:T(8,128)S(1)} %get-tuple-element.430.refs_0_, f32[4,128,896]{2,1,0:T(8,128)S(1)} %copy-done.3, ...), custom_call_target="tpu_custom_call" | custom-call | tf_op jit(solution)/shard_map/pallas_call | solution.py:718
  719.1 37.5 %shard_map.449 = (bf16[4,4,16,896]{3,2,1,0:T(8,128)(2,1)S(1)}, bf16[2,200,1408]{2,1,0:T(8,128)(2,1)S(1)}, bf16[200,896]{1,0:T(8,128)(2,1)}, bf16[200,896]{1,0:T(...) custom-call(bf16[4,16,896]{2,1,0:T(8,128)(2,1)S(1)} %convert_element, ...), custom_call_target="tpu_custom_call" | custom-call | tf_op jit(solution)/shard_map/pallas_call | solution.py:584
  757.9 46.9 %shard_map.450 = (f32[4,128,896]{2,1,0:T(8,128)S(1)}, f32[4,128,896]{2,1,0:T(8,128)S(1)}, f32[4,128,16,128]{3,2,1,0:T(8,128)}, f32[4,128,16,128]{3,2,1,0:T(8,128...) custom-call(f32[4,128,896]{2,1,0:T(8,128)S(1)} %get-tuple-element.43, ...), custom_call_target="tpu_custom_call" | custom-call | tf_op jit(solution)/shard_map/pallas_call | solution.py:718
  810.8 3.5 reduce_sum.428
  814.5 4.3 fusion.307
  819.7 32.9 %shard_map.451 = (f32[4,132,512]{2,1,0:T(8,128)S(1)}, bf16[200,896]{1,0:T(8,128)(2,1)}, bf16[200,896]{1,0:T(8,128)(2,1)}, bf16[200,560]{1,0:T(8,128)(2,1)}, bf16...) custom-call(f32[132,512]{1,0:T(8,128)S(1)} %pad_maximum_fusion.13.re, ...), custom_call_target="tpu_custom_call" | custom-call | tf_op jit(solution)/shard_map/pallas_call | solution.py:584
  855.0 6.8 multiply_reduce_fusion.3
  872.0 7.4 collective-permute-start.2
  881.7 5.1 fusion.37
  903.3 28.1 %shard_map.452 = (bf16[2,128,1600]{2,1,0:T(8,128)(2,1)S(1)}, bf16[2,16,1600]{2,1,0:T(8,128)(2,1)S(1)}, bf16[200,512]{1,0:T(8,128)(2,1)}, bf16[200,512]{1,0:T(8,1...) custom-call(bf16[4,128,1600]{2,1,0:T(8,128)(2,1)S(1)} %copy.183.refs, ...), custom_call_target="tpu_custom_call" | custom-call | tf_op jit(solution)/shard_map/pallas_call | solution.py:584
  935.0 16.9 %shard_map.453 = (f32[4,20,1600]{2,1,0:T(8,128)S(1)}, bf16[200,512]{1,0:T(8,128)(2,1)}, bf16[200,512]{1,0:T(8,128)(2,1)}, bf16[200,384]{1,0:T(8,128)(2,1)}, bf16...) custom-call(f32[20,1600]{1,0:T(8,128)S(1)} %concatenate.138.refs_0_, ...), custom_call_target="tpu_custom_call" | custom-call | tf_op jit(solution)/shard_map/pallas_call | solution.py:584
  952.0 25.9 %shard_map.454 = (bf16[8,20,1600]{2,1,0:T(8,128)(2,1)S(1)}, bf16[8,22,896]{2,1,0:T(8,128)(2,1)S(1)}, bf16[200,512]{1,0:T(8,128)(2,1)}, bf16[200,512]{1,0:T(8,128...) custom-call(bf16[20,1600]{1,0:T(8,128)(2,1)S(1)} %reduce_sum.441.ref, ...), custom_call_target="tpu_custom_call" | custom-call | tf_op jit(solution)/shard_map/pallas_call | solution.py:584
  989.0 35.7 %shard_map.455 = (bf16[2,200,896]{2,1,0:T(8,128)(2,1)S(1)}, bf16[200,512]{1,0:T(8,128)(2,1)S(1)}, bf16[400,512]{1,0:T(8,128)(2,1)S(1)}, bf16[400,128]{1,0:T(8,128)(2,1)S(1)}, f32[4,22,896]{2,1,0:T(8,128)S(1)}) custom-call(bf16[2,200,896]{2,1,0:T(8,128)(2,1)S(1)} %pad_maximum_fusion.9.refs_0_, bf16[200,512]{1,0:T(8,128)(2,1)S(1)} %fusion.208.refs_1_, ...), custom_call_target="tpu_custom_call" | custom-call | tf_op jit(solution)/shard_map/pallas_call | solution.py:584
  1051.2 3.7 fusion.113
  (655 shorter events, 218.4 us)
Async XLA Ops:
  3.0 97.2 %copy-start.137 = (f32[1600]{0:T(1024)}, f32[1600]{0:T(1024)S(1)}, u32[]{:S(2)}) copy-start(f32[1600]{0:T(1024)S(1)} %get-tuple-element.390) | copy-start | bytes 19204
  3.1 377.6 %copy-start.157 = (f32[1600]{0:T(1024)}, f32[1600]{0:T(1024)S(1)}, u32[]{:S(2)}) copy-start(f32[1600]{0:T(1024)S(1)} %get-tuple-element.388) | copy-start | bytes 19204
  3.1 377.6 %copy-start.159 = (f32[1600]{0:T(1024)}, f32[1600]{0:T(1024)S(1)}, u32[]{:S(2)}) copy-start(f32[1600]{0:T(1024)S(1)} %get-tuple-element.389) | copy-start | bytes 19204
  76.0 24.3 %copy-start.7 = (bf16[4,2,25,8,560]{4,3,2,1,0:T(8,128)(2,1)}, bf16[4,2,25,8,560]{4,3,2,1,0:T(8,128)(2,1)S(1)}, u32[]{:S(2)}) copy-start(bf16[4,2,25,8,560]{4,3,2,1,0:T(8,128)(2,1)S(1)} %get-tuple-element.143) | copy-start | bytes 5376004
  81.3 165.9 %collective-permute-start = (f32[4,3,896]{2,1,0:T(4,128)}, f32[4,3,896]{2,1,0:T(4,128)}, u32[]{:S(2)}, u32[]{:S(2)}) collective-permute-start(f32[4,3,896]{2,1,0:T(4,128)} %slice.640), channel_id=1, source_target_pairs={{0,1},{1,2},{2,3},{3,4},{4,5},{5,6},{6,7},{8,9},{9,10},{10,11},{11... | collective-permute-start | bytes 129032 | tf_op jit(solution)/shard_map/ppermute | solution.py:1054
  85.7 160.8 %copy-start.120 = (f32[22,800]{1,0:T(8,128)}, f32[22,800]{1,0:T(8,128)S(1)}, u32[]{:S(2)}) copy-start(f32[22,800]{1,0:T(8,128)S(1)} %constant_dynamic-slice_fusion) | copy-start | bytes 211204
  100.2 14.7 %copy-start.210 = (f32[16]{0:T(128)}, f32[16]{0:T(128)S(1)}, u32[]{:S(2)}) copy-start(f32[16]{0:T(128)S(1)} %multiply_reduce_fusion.16) | copy-start | bytes 196
  143.5 22.1 %copy-start.25 = (f32[768,128]{1,0:T(8,128)}, f32[768,128]{1,0:T(8,128)S(1)}, u32[]{:S(2)}) copy-start(f32[768,128]{1,0:T(8,128)S(1)} %pad_select_fusion.refs_3_) | copy-start | bytes 1179652
  212.6 24.7 %copy-start.36 = (bf16[400,1600]{1,0:T(8,128)(2,1)S(1)}, bf16[400,1600]{1,0:T(8,128)(2,1)}, u32[]{:S(2)}) copy-start(bf16[400,1600]{1,0:T(8,128)(2,1)} %weight_ref.2) | copy-start | bytes 3840004
  247.1 100.6 %copy-start.162 = (f32[896]{0:T(1024)}, f32[896]{0:T(1024)S(1)}, u32[]{:S(2)}) copy-start(f32[896]{0:T(1024)S(1)} %get-tuple-element.393) | copy-start | bytes 10756
  279.1 41.1 %copy-start.5 = (f32[4,128,896]{2,1,0:T(8,128)}, f32[4,128,896]{2,1,0:T(8,128)S(1)}, u32[]{:S(2)}) copy-start(f32[4,128,896]{2,1,0:T(8,128)S(1)} %get-tuple-element.465.refs_1_) | copy-start | bytes 5505028
  280.3 40.0 %copy-start.2 = (f32[4,128,16,128]{3,2,1,0:T(8,128)}, f32[4,128,16,128]{3,2,1,0:T(8,128)S(1)}, u32[]{:S(2)}) copy-start(f32[4,128,16,128]{3,2,1,0:T(8,128)S(1)} %broadcast_in_dim.186.refs_2_.refs_3_) | copy-start | bytes 12582916
  289.0 29.1 %copy-start.66 = (bf16[400,58]{1,0:T(8,128)(2,1)}, bf16[400,58]{1,0:T(8,128)(2,1)S(1)}, u32[]{:S(2)}) copy-start(bf16[400,58]{1,0:T(8,128)(2,1)S(1)} %get-tuple-element.246) | copy-start | bytes 139204
  289.1 30.0 %copy-start.123 = (f32[512,16]{1,0:T(8,128)S(1)}, f32[512,16]{1,0:T(8,128)}, u32[]{:S(2)}) copy-start(f32[512,16]{1,0:T(8,128)} %copy.211) | copy-start | bytes 98308
  320.2 27.5 %copy-start = (f32[4,128,16,128]{3,2,1,0:T(8,128)}, f32[4,128,16,128]{3,2,1,0:T(8,128)S(1)}, u32[]{:S(2)}) copy-start(f32[4,128,16,128]{3,2,1,0:T(8,128)S(1)} %broadcast_in_dim.188.refs_3_.refs_2_.refs_4_) | copy-start | bytes 12582916
  320.2 27.5 %copy-start.70 = (f32[4,128,896]{2,1,0:T(8,128)S(1)}, f32[4,128,896]{2,1,0:T(8,128)}, u32[]{:S(2)}) copy-start(f32[4,128,896]{2,1,0:T(8,128)} %get-tuple-element.432) | copy-start | bytes 5505028
  320.2 27.5 %copy-start.82 = (f32[4,128,1792]{2,1,0:T(8,128)S(1)}, f32[4,128,1792]{2,1,0:T(8,128)}, u32[]{:S(2)}) copy-start(f32[4,128,1792]{2,1,0:T(8,128)} %copy-done.81) | copy-start | bytes 11010052
  347.7 77.0 %copy-start.28 = (bf16[4,128,1600]{2,1,0:T(8,128)(2,1)}, bf16[4,128,1600]{2,1,0:T(8,128)(2,1)S(1)}, u32[]{:S(2)}) copy-start(bf16[4,128,1600]{2,1,0:T(8,128)(2,1)S(1)} %get-tuple-element.165) | copy-start | bytes 4915204
  350.9 26.8 %slice-start = ((s8[4505600]{0:T(1024)(128)(4,1)}), s8[311296]{0:T(1024)(128)(4,1)S(1)}, s32[]{:S(2)}) async-start(s8[4505600]{0:T(1024)(128)(4,1)} %bitcast.526), calls=%async_computation | async-start | bytes 622592
  353.4 24.3 %slice-start.1 = ((s8[4505600]{0:T(1024)(128)(4,1)}), s8[4194304]{0:T(1024)(128)(4,1)S(1)}, s32[]{:S(2)}) async-start(s8[4505600]{0:T(1024)(128)(4,1)} %bitcast.526), calls=%async_computation.1 | async-start | bytes 8388608
  377.4 89.2 %copy-start.183 = (f32[128]{0:T(128)}, f32[128]{0:T(128)S(1)}, u32[]{:S(2)}) copy-start(f32[128]{0:T(128)S(1)} %fusion.274) | copy-start | bytes 1540
  377.7 88.9 %copy-start.185 = (f32[128]{0:T(128)}, f32[128]{0:T(128)S(1)}, u32[]{:S(2)}) copy-start(f32[128]{0:T(128)S(1)} %fusion.273) | copy-start | bytes 1540
  381.2 15.5 %copy-start.86 = (f32[128,1600]{1,0:T(8,128)}, f32[128,1600]{1,0:T(8,128)S(1)}, u32[]{:S(2)}) copy-start(f32[128,1600]{1,0:T(8,128)S(1)} %get-tuple-element.428) | copy-start | bytes 2457604
  381.2 83.0 %copy-start.187 = (f32[128]{0:T(128)}, f32[128]{0:T(128)S(1)}, u32[]{:S(2)}) copy-start(f32[128]{0:T(128)S(1)} %fusion.275) | copy-start | bytes 1540
  438.8 24.7 %copy-start.87 = (f32[128,1600]{1,0:T(8,128)S(1)}, f32[128,1600]{1,0:T(8,128)}, u32[]{:S(2)}) copy-start(f32[128,1600]{1,0:T(8,128)} %copy-done.86) | copy-start | bytes 2457604
  467.0 25.9 %copy-start.24 = (bf16[800,1600]{1,0:T(8,128)(2,1)S(1)}, bf16[800,1600]{1,0:T(8,128)(2,1)}, u32[]{:S(2)}) copy-start(bf16[800,1600]{1,0:T(8,128)(2,1)} %weight_ref.3) | copy-start | bytes 7680004
  501.9 25.0 %copy-start.20 = (bf16[1600,128]{1,0:T(8,128)(2,1)S(1)}, bf16[1600,128]{1,0:T(8,128)(2,1)}, u32[]{:S(2)}) copy-start(bf16[1600,128]{1,0:T(8,128)(2,1)} %copy-done.19) | copy-start | bytes 1228804
  501.9 25.0 %copy-start.26 = (f32[768,128]{1,0:T(8,128)S(1)}, f32[768,128]{1,0:T(8,128)}, u32[]{:S(2)}) copy-start(f32[768,128]{1,0:T(8,128)} %copy-done.25) | copy-start | bytes 1179652
  501.9 25.0 %copy-start.27 = (bf16[2,200,896]{2,1,0:T(8,128)(2,1)S(1)}, bf16[2,200,896]{2,1,0:T(8,128)(2,1)}, u32[]{:S(2)}) copy-start(bf16[2,200,896]{2,1,0:T(8,128)(2,1)} %pad_maximum_fusion.8.refs_6_) | copy-start | bytes 2150404
  640.9 24.7 %copy-start.8 = (bf16[4,2,25,8,560]{4,3,2,1,0:T(8,128)(2,1)S(1)}, bf16[4,2,25,8,560]{4,3,2,1,0:T(8,128)(2,1)}, u32[]{:S(2)}) copy-start(bf16[4,2,25,8,560]{4,3,2,1,0:T(8,128)(2,1)} %copy-done.7) | copy-start | bytes 5376004
  640.9 27.1 %copy-start.71 = (f32[4,128,896]{2,1,0:T(8,128)S(1)}, f32[4,128,896]{2,1,0:T(8,128)}, u32[]{:S(2)}) copy-start(f32[4,128,896]{2,1,0:T(8,128)} %get-tuple-element.432) | copy-start | bytes 5505028
  640.9 27.1 %copy-start.83 = (f32[4,128,1792]{2,1,0:T(8,128)S(1)}, f32[4,128,1792]{2,1,0:T(8,128)}, u32[]{:S(2)}) copy-start(f32[4,128,1792]{2,1,0:T(8,128)} %copy-done.81) | copy-start | bytes 11010052
  640.9 27.1 %copy-start.113 = (f32[512,800]{1,0:T(8,128)S(1)}, f32[512,800]{1,0:T(8,128)}, u32[]{:S(2)}) copy-start(f32[512,800]{1,0:T(8,128)} %fusion.328) | copy-start | bytes 4915204
  695.4 18.3 %copy-start.136 = (bf16[200,1408]{1,0:T(8,128)(2,1)S(1)}, bf16[200,1408]{1,0:T(8,128)(2,1)}, u32[]{:S(2)}) copy-start(bf16[200,1408]{1,0:T(8,128)(2,1)} %get-tuple-element.201) | copy-start | bytes 1689604
  719.1 38.6 %copy-start.168 = (f32[4,896]{1,0:T(4,128)S(1)}, f32[4,896]{1,0:T(4,128)}, u32[]{:S(2)}) copy-start(f32[4,896]{1,0:T(4,128)} %get-tuple-element.509) | copy-start | bytes 43012
  719.1 38.6 %copy-start.169 = (f32[4,896]{1,0:T(4,128)S(1)}, f32[4,896]{1,0:T(4,128)}, u32[]{:S(2)}) copy-start(f32[4,896]{1,0:T(4,128)} %get-tuple-element.510) | copy-start | bytes 43012
  719.1 38.6 %copy-start.170 = (f32[4,896]{1,0:T(4,128)S(1)}, f32[4,896]{1,0:T(4,128)}, u32[]{:S(2)}) copy-start(f32[4,896]{1,0:T(4,128)} %get-tuple-element.511) | copy-start | bytes 43012
  719.1 38.6 %copy-start.171 = (f32[4,896]{1,0:T(4,128)S(1)}, f32[4,896]{1,0:T(4,128)}, u32[]{:S(2)}) copy-start(f32[4,896]{1,0:T(4,128)} %get-tuple-element.512) | copy-start | bytes 43012
  719.1 38.8 %copy-start.6 = (f32[4,128,896]{2,1,0:T(8,128)S(1)}, f32[4,128,896]{2,1,0:T(8,128)}, u32[]{:S(2)}) copy-start(f32[4,128,896]{2,1,0:T(8,128)} %copy-done.5) | copy-start | bytes 5505028
  861.8 19.8 %slice-start.4 = ((s8[4505600]{0:T(1024)(128)(4,1)}), s8[4194304]{0:T(1024)(128)(4,1)S(1)}, s32[]{:S(2)}) async-start(s8[4505600]{0:T(1024)(128)(4,1)} %bitcast.624), calls=%async_computation.4 | async-start | bytes 8388608
  862.6 19.1 %slice-start.5 = ((s8[4505600]{0:T(1024)(128)(4,1)}), s8[311296]{0:T(1024)(128)(4,1)S(1)}, s32[]{:S(2)}) async-start(s8[4505600]{0:T(1024)(128)(4,1)} %bitcast.624), calls=%async_computation.5 | async-start | bytes 622592
  863.3 25.8 %collective-permute-start.1 = (bf16[4,3,896]{2,1,0:T(4,128)(2,1)S(1)}, bf16[4,3,896]{2,1,0:T(4,128)(2,1)S(1)}, u32[]{:S(2)}, u32[]{:S(2)}) collective-permute-start(bf16[4,3,896]{2,1,0:T(4,128)(2,1)S(1)} %slice.880), channel_id=1, source_target_pairs={{1,0},{2,1},{3,2},{4,3},{5,4},{6,5},{7,6},{9,8},{10,9},{11,10},{12... | collective-permute-start | bytes 64520 | tf_op jit(solution)/shard_map/ppermute | solution.py:1385
  872.0 173.0 %collective-permute-start.2 = (bf16[688,512]{1,0:T(8,128)(2,1)}, bf16[688,512]{1,0:T(8,128)(2,1)}, u32[]{:S(2)}, u32[]{:S(2)}) collective-permute-start(bf16[688,512]{1,0:T(8,128)(2,1)} %pad_maximum_fusion.10), channel_id=1, source_target_pairs={{0,0},{1,1},{2,8},{3,9},{4,16},{5,17},{6,24},{7,25},{8,2},{9,3},{1... | collective-permute-start | bytes 2113544 | tf_op jit(solution)/shard_map/ppermute | solution.py:1358
  903.3 28.2 %copy-start.201 = (f32[128]{0:T(128)S(1)}, f32[128]{0:T(128)}, u32[]{:S(2)}) copy-start(f32[128]{0:T(128)} %copy-done.200) | copy-start | bytes 1540
  952.0 28.2 %copy-start.105 = (f32[128,1600]{1,0:T(8,128)S(1)}, f32[128,1600]{1,0:T(8,128)}, u32[]{:S(2)}) copy-start(f32[128,1600]{1,0:T(8,128)} %convert_reduce_fusion.1) | copy-start | bytes 2457604
  989.0 37.4 %copy-start.67 = (bf16[400,58]{1,0:T(8,128)(2,1)S(1)}, bf16[400,58]{1,0:T(8,128)(2,1)}, u32[]{:S(2)}) copy-start(bf16[400,58]{1,0:T(8,128)(2,1)} %copy-done.66) | copy-start | bytes 139204
  989.0 37.4 %copy-start.129 = (f32[1,400,58]{2,1,0:T(8,128)S(1)}, f32[1,400,58]{2,1,0:T(8,128)}, u32[]{:S(2)}) copy-start(f32[1,400,58]{2,1,0:T(8,128)} %copy.219) | copy-start | bytes 278404
  989.0 37.4 %copy-start.130 = (f32[1,400,58]{2,1,0:T(8,128)S(1)}, f32[1,400,58]{2,1,0:T(8,128)}, u32[]{:S(2)}) copy-start(f32[1,400,58]{2,1,0:T(8,128)} %copy.218) | copy-start | bytes 278404
  (174 other events, 617.0 us)
